TPU v7x, 512 devices: a whole 4x4x16 slice. The times are simulated.
512 devices in a mesh: slab: 8 (over y, core), tile: 64 (over z, x).
Axes of the slice: x: 4, y: 4, z: 16, core: 2. Of those that a mesh axis runs over, the one named last changes fastest.
Arguments:
- depth_layers: float32 [8, 64, 512, 512], P('slab', 'tile'), may hold values from 1 to 3
- thickness_layers: float32 [8, 64, 512, 512], P('slab', 'tile'), may hold values from 0.05 to 0.5
- coverage: int32 [64, 512, 512], P('tile', 'slab'), may hold values 0 or 1
Outputs:
- smooth_depth: float32 [64, 512, 512], P('tile', 'slab')
- shade: float32 [64, 512, 512], P('tile', 'slab')
All inputs are finite; a program needn't handle non-finite values. No bound on the sum of `coverage` on one device may be relied on, other than what follows from the above.
Results may differ from a plain program's by a relative error of at most 0.00002.
Values sent between devices are 32-bit elements; how exact they have to be, the bound alone decides.
No kernel may reach another device: no remote copies, remote signals or barrier semaphores. Data moves between devices by JAX's collectives and lax.ppermute only.
A program may use at most 64 MiB of HBM per device.

v0:
```python
import math

import jax
import jax.numpy as jnp
from jax import lax
from jax.sharding import PartitionSpec as P

SWEEPS = 4


flow_step = 0.2


def shifted(block, axis, distance):
    devices = range(lax.axis_size(axis))
    route = [((i - distance) % len(devices), i) for i in devices]
    return lax.ppermute(block, axis, route)


def shifted_2(value, axis, steps):
    count = lax.axis_size(axis)
    first, last = (max(0, -steps), min(count, count - steps))
    return lax.ppermute(value, axis, [(source, source + steps) for source in range(first, last)])


def flow_sweep(extended):
    slope_x = (extended[1:-1, 2:] - extended[1:-1, :-2]) * 0.5
    slope_y = (extended[2:, 1:-1] - extended[:-2, 1:-1]) * 0.5
    norm_inv = lax.rsqrt(1.0 + slope_x * slope_x + slope_y * slope_y)
    normal_x = slope_x * norm_inv
    normal_y = slope_y * norm_inv
    divergence = (normal_x[1:-1, 2:] - normal_x[1:-1, :-2]) * 0.5 + (
        normal_y[2:, 1:-1] - normal_y[:-2, 1:-1]
    ) * 0.5
    return extended[2:-2, 2:-2] + flow_step * divergence


def shading(extended, thickness, coverage):
    slope_x = (extended[1:-1, 2:] - extended[1:-1, :-2]) * 0.5
    slope_y = (extended[2:, 1:-1] - extended[:-2, 1:-1]) * 0.5
    norm_inv = lax.rsqrt(1.0 + slope_x * slope_x + slope_y * slope_y)
    diffuse = jnp.maximum((0.8 - 0.36 * slope_x - 0.48 * slope_y) * norm_inv, 0.0)
    gloss = jnp.maximum((0.9487 - 0.1897 * slope_x - 0.253 * slope_y) * norm_inv, 0.0) ** 16
    fluid = coverage.astype(jnp.float32)
    lit = 0.15 + 0.7 * jnp.exp(-0.8 * thickness) * diffuse + 0.4 * gloss
    return fluid * lit + (1.0 - fluid) * 0.05


def refill_rows(extended, margin, top_edge, bottom_edge):
    total_rows = extended.shape[0]
    width = extended.shape[1]
    head_block = jnp.where(
        top_edge,
        jnp.broadcast_to(extended[margin : margin + 1], (margin, width)),
        extended[:margin],
    )
    tail_block = jnp.where(
        bottom_edge,
        jnp.broadcast_to(extended[total_rows - margin - 1 : total_rows - margin], (margin, width)),
        extended[total_rows - margin :],
    )
    return jnp.concatenate([head_block, extended[margin : total_rows - margin], tail_block], axis=0)


def refill_cols(extended, margin, left_edge, right_edge):
    total_cols = extended.shape[1]
    height = extended.shape[0]
    head_block = jnp.where(
        left_edge,
        jnp.broadcast_to(extended[:, margin : margin + 1], (height, margin)),
        extended[:, :margin],
    )
    tail_block = jnp.where(
        right_edge,
        jnp.broadcast_to(
            extended[:, total_cols - margin - 1 : total_cols - margin], (height, margin)
        ),
        extended[:, total_cols - margin :],
    )
    return jnp.concatenate(
        [head_block, extended[:, margin : total_cols - margin], tail_block], axis=1
    )


def extend(surface, margin, grid, first_band, last_band, edges):
    above_slab = shifted(surface[-margin:], "slab", 1)
    below_slab = shifted(surface[:margin], "slab", -1)
    above_tile = shifted_2(above_slab, "tile", grid)
    below_tile = shifted_2(below_slab, "tile", -grid)
    above = jnp.where(first_band, above_tile, above_slab)
    below = jnp.where(last_band, below_tile, below_slab)
    tall = jnp.concatenate([above, surface, below], axis=0)
    tall = refill_rows(tall, margin, edges[0], edges[1])
    left_cols = shifted_2(tall[:, -margin:], "tile", 1)
    right_cols = shifted_2(tall[:, :margin], "tile", -1)
    wide = jnp.concatenate([left_cols, tall, right_cols], axis=1)
    return refill_cols(wide, margin, edges[2], edges[3])


def local(depth_layers, thickness_layers, coverage):
    slab_count = lax.axis_size("slab")
    grid = math.isqrt(lax.axis_size("tile"))
    slab_index = lax.axis_index("slab")
    tile_index = lax.axis_index("tile")
    grid_row = tile_index // grid
    grid_col = tile_index % grid
    first_band = slab_index == 0
    last_band = slab_index == slab_count - 1
    edges = (
        first_band & (grid_row == 0),
        last_band & (grid_row == grid - 1),
        grid_col == 0,
        grid_col == grid - 1,
    )
    depth_tile = depth_layers[0, 0]
    thick_tile = thickness_layers[0, 0]
    depth_parts, thick_parts = (
        lax.all_to_all(depth_tile[None], "slab", split_axis=1, concat_axis=0, tiled=True),
        lax.all_to_all(thick_tile[None], "slab", split_axis=1, concat_axis=0, tiled=True),
    )
    depth_band = jnp.min(depth_parts, axis=0)
    thick_band = jnp.sum(thick_parts, axis=0)
    surface = depth_band
    for sweep_index in range(SWEEPS):
        surface = flow_sweep(extend(surface, 2, grid, first_band, last_band, edges))
    shade = shading(extend(surface, 1, grid, first_band, last_band, edges), thick_band, coverage[0])
    return (surface[None], shade[None])


def solution(mesh):
    return jax.shard_map(
        local,
        mesh=mesh,
        in_specs=(
            P("slab", "tile", None, None),
            P("slab", "tile", None, None),
            P("tile", "slab", None),
        ),
        out_specs=(P("tile", "slab", None), P("tile", "slab", None)),
        check_vma=False,
    )
```

profile of v0, /device:TPU:136, one launch (start us, length us, event | category | flops | bytes accessed | tf_op | source)
XLA Modules:
  0.0 176.5 jit_solution(14811572393977385673)
XLA Ops:
  0.6 1.9 %broadcast_in_dim_squeeze.6 = f32[1,512,512]{2,0,1:T(1,128)S(1)} reshape(f32[1,1,512,512]{3,2,1,0:T(8,128)} %param.3) | data formatting | bytes 2097152 | tf_op jit(solution)/shard_map/broadcast_in_dim;squeeze | solution.py:118
  2.6 19.4 %all_to_all.24 = f32[1,512,512]{2,0,1:T(1,128)S(1)} all-to-all(f32[1,512,512]{2,0,1:T(1,128)S(1)} %broadcast_in_dim_squeeze.6), channel_id=1, replica_groups=mesh['slab'=8,'tile'=64] {'slab'}, dimensions={1} | all-to-all | bytes 2097152 | tf_op jit(solution)/shard_map/all_to_all | solution.py:118
  22.2 1.7 collective-permute-start.2
  23.9 1.3 collective-permute-done
  25.1 5.2 %collective-permute-start.1 = (f32[2,512]{1,0:T(2,128)S(1)}, f32[2,512]{1,0:T(2,128)S(1)}, u32[]{:S(2)}, u32[]{:S(2)}) collective-permute-start(f32[2,512]{1,0:T(2,128)S(1)} %collective-permute-done), channel_id=1, source_target_pairs={{0,8},{1,9},{2,10},{3,11},{4,12},{5,13},{6,14},{7,15},{8,16},{9,17... | collective-permute-start | bytes 12296 | tf_op jit(solution)/shard_map/ppermute | solution.py:23
  30.4 2.8 %collective-permute-start.3 = (f32[2,512]{1,0:T(2,128)S(1)}, f32[2,512]{1,0:T(2,128)S(1)}, u32[]{:S(2)}, u32[]{:S(2)}) collective-permute-start(f32[2,512]{1,0:T(2,128)S(1)} %collective-permute-done.2), channel_id=1, source_target_pairs={{8,0},{9,1},{10,2},{11,3},{12,4},{13,5},{14,6},{15,7},{16,8},{17,9... | collective-permute-start | bytes 12296 | tf_op jit(solution)/shard_map/ppermute | solution.py:23
  33.2 5.2 %collective-permute-done.3 = f32[2,512]{1,0:T(2,128)S(1)} collective-permute-done((f32[2,512]{1,0:T(2,128)S(1)}, f32[2,512]{1,0:T(2,128)S(1)}, u32[]{:S(2)}, u32[]{:S(2)}) %collective-permute-start.3) | collective-permute-done | bytes 4128 | tf_op jit(solution)/shard_map/ppermute | solution.py:23
  38.4 3.4 %collective-permute-start.5 = (f32[68,2]{1,0:T(8,128)S(1)}, f32[68,2]{1,0:T(8,128)S(1)}, u32[]{:S(2)}, u32[]{:S(2)}) collective-permute-start(f32[68,2]{1,0:T(8,128)S(1)} %get-tuple-element.18), channel_id=1, source_target_pairs={{0,1},{1,2},{2,3},{3,4},{4,5},{5,6},{6,7},{7,8},{8,9},{9,10},{10,1... | collective-permute-start | bytes 1640 | tf_op jit(solution)/shard_map/ppermute | solution.py:23
  41.8 0.2 slice_reduce_fusion.6
  42.0 5.8 %collective-permute-start.4 = (f32[68,2]{1,0:T(8,128)S(1)}, f32[68,2]{1,0:T(8,128)S(1)}, u32[]{:S(2)}, u32[]{:S(2)}) collective-permute-start(f32[68,2]{1,0:T(8,128)S(1)} %get-tuple-element.19), channel_id=1, source_target_pairs={{1,0},{2,1},{3,2},{4,3},{5,4},{6,5},{7,6},{8,7},{9,8},{10,9},{11,1... | collective-permute-start | bytes 1640 | tf_op jit(solution)/shard_map/ppermute | solution.py:23
  47.9 1.5 collective-permute-done.4
  49.6 0.2 fusion.18
  49.8 0.2 fusion.19
  50.1 0.2 fusion.33
  50.3 1.7 collective-permute-start.8
  52.0 1.3 collective-permute-done.6
  53.3 4.8 %collective-permute-start.7 = (f32[2,512]{1,0:T(2,128)S(1)}, f32[2,512]{1,0:T(2,128)S(1)}, u32[]{:S(2)}, u32[]{:S(2)}) collective-permute-start(f32[2,512]{1,0:T(2,128)S(1)} %collective-permute-done.6), channel_id=1, source_target_pairs={{0,8},{1,9},{2,10},{3,11},{4,12},{5,13},{6,14},{7,15},{8,16},{9,17... | collective-permute-start | bytes 12296 | tf_op jit(solution)/shard_map/ppermute | solution.py:23
  58.2 3.1 %collective-permute-start.9 = (f32[2,512]{1,0:T(2,128)S(1)}, f32[2,512]{1,0:T(2,128)S(1)}, u32[]{:S(2)}, u32[]{:S(2)}) collective-permute-start(f32[2,512]{1,0:T(2,128)S(1)} %collective-permute-done.8), channel_id=1, source_target_pairs={{8,0},{9,1},{10,2},{11,3},{12,4},{13,5},{14,6},{15,7},{16,8},{17,9... | collective-permute-start | bytes 12296 | tf_op jit(solution)/shard_map/ppermute | solution.py:23
  61.3 3.2 %collective-permute-done.9 = f32[2,512]{1,0:T(2,128)S(1)} collective-permute-done((f32[2,512]{1,0:T(2,128)S(1)}, f32[2,512]{1,0:T(2,128)S(1)}, u32[]{:S(2)}, u32[]{:S(2)}) %collective-permute-start.9) | collective-permute-done | bytes 4128 | tf_op jit(solution)/shard_map/ppermute | solution.py:23
  64.7 3.1 %collective-permute-start.11 = (f32[68,2]{1,0:T(8,128)S(1)}, f32[68,2]{1,0:T(8,128)S(1)}, u32[]{:S(2)}, u32[]{:S(2)}) collective-permute-start(f32[68,2]{1,0:T(8,128)S(1)} %get-tuple-element.16), channel_id=1, source_target_pairs={{0,1},{1,2},{2,3},{3,4},{4,5},{5,6},{6,7},{7,8},{8,9},{9,10},{10,1... | collective-permute-start | bytes 1640 | tf_op jit(solution)/shard_map/ppermute | solution.py:23
  67.8 0.2 slice_reduce_fusion.4
  67.9 7.6 %collective-permute-start.10 = (f32[68,2]{1,0:T(8,128)S(1)}, f32[68,2]{1,0:T(8,128)S(1)}, u32[]{:S(2)}, u32[]{:S(2)}) collective-permute-start(f32[68,2]{1,0:T(8,128)S(1)} %get-tuple-element.17), channel_id=1, source_target_pairs={{1,0},{2,1},{3,2},{4,3},{5,4},{6,5},{7,6},{8,7},{9,8},{10,9},{11,1... | collective-permute-start | bytes 1640 | tf_op jit(solution)/shard_map/ppermute | solution.py:23
  75.6 1.5 collective-permute-done.10
  77.2 0.1 pad_maximum_fusion.25
  77.4 0.2 fusion.16
  77.6 0.2 fusion.17
  77.9 0.2 fusion.30
  78.1 1.7 collective-permute-start.14
  79.8 1.3 collective-permute-done.12
  81.1 2.1 %collective-permute-start.13 = (f32[2,512]{1,0:T(2,128)S(1)}, f32[2,512]{1,0:T(2,128)S(1)}, u32[]{:S(2)}, u32[]{:S(2)}) collective-permute-start(f32[2,512]{1,0:T(2,128)S(1)} %collective-permute-done.12), channel_id=1, source_target_pairs={{0,8},{1,9},{2,10},{3,11},{4,12},{5,13},{6,14},{7,15},{8,16},{9,17... | collective-permute-start | bytes 12296 | tf_op jit(solution)/shard_map/ppermute | solution.py:23
  83.3 5.8 %collective-permute-start.15 = (f32[2,512]{1,0:T(2,128)S(1)}, f32[2,512]{1,0:T(2,128)S(1)}, u32[]{:S(2)}, u32[]{:S(2)}) collective-permute-start(f32[2,512]{1,0:T(2,128)S(1)} %collective-permute-done.14), channel_id=1, source_target_pairs={{8,0},{9,1},{10,2},{11,3},{12,4},{13,5},{14,6},{15,7},{16,8},{17,9... | collective-permute-start | bytes 12296 | tf_op jit(solution)/shard_map/ppermute | solution.py:23
  89.1 1.3 collective-permute-done.15
  90.5 1.9 %collective-permute-start.17 = (f32[68,2]{1,0:T(8,128)S(1)}, f32[68,2]{1,0:T(8,128)S(1)}, u32[]{:S(2)}, u32[]{:S(2)}) collective-permute-start(f32[68,2]{1,0:T(8,128)S(1)} %get-tuple-element.14), channel_id=1, source_target_pairs={{0,1},{1,2},{2,3},{3,4},{4,5},{5,6},{6,7},{7,8},{8,9},{9,10},{10,1... | collective-permute-start | bytes 1640 | tf_op jit(solution)/shard_map/ppermute | solution.py:23
  92.4 0.2 slice_reduce_fusion.2
  92.6 8.0 %collective-permute-start.16 = (f32[68,2]{1,0:T(8,128)S(1)}, f32[68,2]{1,0:T(8,128)S(1)}, u32[]{:S(2)}, u32[]{:S(2)}) collective-permute-start(f32[68,2]{1,0:T(8,128)S(1)} %get-tuple-element.15), channel_id=1, source_target_pairs={{1,0},{2,1},{3,2},{4,3},{5,4},{6,5},{7,6},{8,7},{9,8},{10,9},{11,1... | collective-permute-start | bytes 1640 | tf_op jit(solution)/shard_map/ppermute | solution.py:23
  100.7 1.5 collective-permute-done.16
  102.5 0.2 fusion.14
  102.7 0.2 fusion.15
  103.0 0.2 fusion.27
  103.2 0.5 copy-done.1
  103.7 1.7 broadcast_in_dim_squeeze.7
  105.4 8.8 %all-to-all-start.1 = ((f32[1,512,512]{2,0,1:T(1,128)}), f32[1,512,512]{2,0,1:T(1,128)S(1)}, u32[]{:S(2)}, u32[]{:S(2)}) async-start(f32[1,512,512]{2,0,1:T(1,128)} %broadcast_in_dim_squeeze.7), calls=%async_computation.1 | async-start | bytes 2097152 | tf_op jit(solution)/shard_map/all_to_all | solution.py:119
  114.3 3.1 %collective-permute-start.19 = (f32[2,512]{1,0:T(2,128)S(1)}, f32[2,512]{1,0:T(2,128)S(1)}, u32[]{:S(2)}, u32[]{:S(2)}) collective-permute-start(f32[2,512]{1,0:T(2,128)S(1)} %collective-permute-done.18), channel_id=1, source_target_pairs={{0,8},{1,9},{2,10},{3,11},{4,12},{5,13},{6,14},{7,15},{8,16},{9,17... | collective-permute-start | bytes 12296 | tf_op jit(solution)/shard_map/ppermute | solution.py:23
  117.4 8.9 %collective-permute-done.20 = f32[2,512]{1,0:T(2,128)S(1)} collective-permute-done((f32[2,512]{1,0:T(2,128)S(1)}, f32[2,512]{1,0:T(2,128)S(1)}, u32[]{:S(2)}, u32[]{:S(2)}) %collective-permute-start.20) | collective-permute-done | bytes 4128 | tf_op jit(solution)/shard_map/ppermute | solution.py:17
  126.3 4.3 %collective-permute-start.21 = (f32[2,512]{1,0:T(2,128)S(1)}, f32[2,512]{1,0:T(2,128)S(1)}, u32[]{:S(2)}, u32[]{:S(2)}) collective-permute-start(f32[2,512]{1,0:T(2,128)S(1)} %collective-permute-done.20), channel_id=1, source_target_pairs={{8,0},{9,1},{10,2},{11,3},{12,4},{13,5},{14,6},{15,7},{16,8},{17,9... | collective-permute-start | bytes 12296 | tf_op jit(solution)/shard_map/ppermute | solution.py:23
  130.6 2.1 %collective-permute-done.21 = f32[2,512]{1,0:T(2,128)S(1)} collective-permute-done((f32[2,512]{1,0:T(2,128)S(1)}, f32[2,512]{1,0:T(2,128)S(1)}, u32[]{:S(2)}, u32[]{:S(2)}) %collective-permute-start.21) | collective-permute-done | bytes 4128 | tf_op jit(solution)/shard_map/ppermute | solution.py:23
  132.8 1.9 %collective-permute-start.23 = (f32[68,2]{1,0:T(8,128)S(1)}, f32[68,2]{1,0:T(8,128)S(1)}, u32[]{:S(2)}, u32[]{:S(2)}) collective-permute-start(f32[68,2]{1,0:T(8,128)S(1)} %get-tuple-element.12), channel_id=1, source_target_pairs={{0,1},{1,2},{2,3},{3,4},{4,5},{5,6},{6,7},{7,8},{8,9},{9,10},{10,1... | collective-permute-start | bytes 1640 | tf_op jit(solution)/shard_map/ppermute | solution.py:23
  134.7 0.2 slice_reduce_fusion
  134.9 8.8 %collective-permute-start.22 = (f32[68,2]{1,0:T(8,128)S(1)}, f32[68,2]{1,0:T(8,128)S(1)}, u32[]{:S(2)}, u32[]{:S(2)}) collective-permute-start(f32[68,2]{1,0:T(8,128)S(1)} %get-tuple-element.13), channel_id=1, source_target_pairs={{1,0},{2,1},{3,2},{4,3},{5,4},{6,5},{7,6},{8,7},{9,8},{10,9},{11,1... | collective-permute-start | bytes 1640 | tf_op jit(solution)/shard_map/ppermute | solution.py:23
  143.8 1.5 collective-permute-done.22
  145.5 0.2 fusion.12
  145.7 0.2 fusion.13
  146.0 0.2 fusion.24
  146.2 0.1 collective-permute-start.26
  146.3 0.4 collective-permute-start.24
  146.7 0.9 collective-permute-done.26
  147.7 2.6 %collective-permute-start.27 = (f32[1,512]{1,0:T(1,128)S(1)}, f32[1,512]{1,0:T(1,128)S(1)}, u32[]{:S(2)}, u32[]{:S(2)}) collective-permute-start(f32[1,512]{1,0:T(1,128)S(1)} %collective-permute-done.26), channel_id=1, source_target_pairs={{8,0},{9,1},{10,2},{11,3},{12,4},{13,5},{14,6},{15,7},{16,8},{17,9... | collective-permute-start | bytes 6152 | tf_op jit(solution)/shard_map/ppermute | solution.py:23
  150.3 4.1 %collective-permute-start.25 = (f32[1,512]{1,0:T(1,128)S(1)}, f32[1,512]{1,0:T(1,128)S(1)}, u32[]{:S(2)}, u32[]{:S(2)}) collective-permute-start(f32[1,512]{1,0:T(1,128)S(1)} %collective-permute-done.24), channel_id=1, source_target_pairs={{0,8},{1,9},{2,10},{3,11},{4,12},{5,13},{6,14},{7,15},{8,16},{9,17... | collective-permute-start | bytes 6152 | tf_op jit(solution)/shard_map/ppermute | solution.py:23
  154.4 3.5 %collective-permute-done.25 = f32[1,512]{1,0:T(1,128)S(1)} collective-permute-done((f32[1,512]{1,0:T(1,128)S(1)}, f32[1,512]{1,0:T(1,128)S(1)}, u32[]{:S(2)}, u32[]{:S(2)}) %collective-permute-start.25) | collective-permute-done | bytes 2080 | tf_op jit(solution)/shard_map/ppermute | solution.py:23
  157.9 6.4 %collective-permute-start.28 = (f32[66,1]{1,0:T(8,128)S(1)}, f32[66,1]{1,0:T(8,128)S(1)}, u32[]{:S(2)}, u32[]{:S(2)}) collective-permute-start(f32[66,1]{1,0:T(8,128)S(1)} %pad_maximum_fusion.40), channel_id=1, source_target_pairs={{1,0},{2,1},{3,2},{4,3},{5,4},{6,5},{7,6},{8,7},{9,8},{10,9},{11,1... | collective-permute-start | bytes 800 | tf_op jit(solution)/shard_map/ppermute | solution.py:23
  164.4 1.6 collective-permute-done.28
  166.1 1.9 %collective-permute-start.29 = (f32[66,1]{1,0:T(8,128)S(1)}, f32[66,1]{1,0:T(8,128)S(1)}, u32[]{:S(2)}, u32[]{:S(2)}) collective-permute-start(f32[66,1]{1,0:T(8,128)S(1)} %get-tuple-element.11), channel_id=1, source_target_pairs={{0,1},{1,2},{2,3},{3,4},{4,5},{5,6},{6,7},{7,8},{8,9},{9,10},{10,1... | collective-permute-start | bytes 800 | tf_op jit(solution)/shard_map/ppermute | solution.py:23
  168.2 7.4 %collective-permute-done.29 = f32[66,1]{1,0:T(8,128)S(1)} collective-permute-done((f32[66,1]{1,0:T(8,128)S(1)}, f32[66,1]{1,0:T(8,128)S(1)}, u32[]{:S(2)}, u32[]{:S(2)}) %collective-permute-start.29) | collective-permute-done | bytes 296 | tf_op jit(solution)/shard_map/ppermute | solution.py:23
  175.6 0.9 fusion.35
  (69 shorter events, 2.1 us)
Async XLA Ops:
  22.1 3.0 %collective-permute-start = (f32[2,512]{1,0:T(2,128)S(1)}, f32[2,512]{1,0:T(2,128)S(1)}, u32[]{:S(2)}, u32[]{:S(2)}) collective-permute-start(f32[2,512]{1,0:T(2,128)S(1)} %get-tuple-element.38), channel_id=1, source_target_pairs={{448,0},{0,64},{64,128},{128,192},{192,256},{256,320},{320,384},{3... | collective-permute-start | bytes 12296 | tf_op jit(solution)/shard_map/ppermute | solution.py:17
  22.2 8.2 %collective-permute-start.2 = (f32[2,512]{1,0:T(2,128)S(1)}, f32[2,512]{1,0:T(2,128)S(1)}, u32[]{:S(2)}, u32[]{:S(2)}) collective-permute-start(f32[2,512]{1,0:T(2,128)S(1)} %get-tuple-element.39), channel_id=1, source_target_pairs={{64,0},{128,64},{192,128},{256,192},{320,256},{384,320},{448,384},... | collective-permute-start | bytes 12296 | tf_op jit(solution)/shard_map/ppermute | solution.py:17
  25.1 8.0 %collective-permute-start.1 = (f32[2,512]{1,0:T(2,128)S(1)}, f32[2,512]{1,0:T(2,128)S(1)}, u32[]{:S(2)}, u32[]{:S(2)}) collective-permute-start(f32[2,512]{1,0:T(2,128)S(1)} %collective-permute-done), channel_id=1, source_target_pairs={{0,8},{1,9},{2,10},{3,11},{4,12},{5,13},{6,14},{7,15},{8,16},{9,17... | collective-permute-start | bytes 12296 | tf_op jit(solution)/shard_map/ppermute | solution.py:23
  30.4 8.0 %collective-permute-start.3 = (f32[2,512]{1,0:T(2,128)S(1)}, f32[2,512]{1,0:T(2,128)S(1)}, u32[]{:S(2)}, u32[]{:S(2)}) collective-permute-start(f32[2,512]{1,0:T(2,128)S(1)} %collective-permute-done.2), channel_id=1, source_target_pairs={{8,0},{9,1},{10,2},{11,3},{12,4},{13,5},{14,6},{15,7},{16,8},{17,9... | collective-permute-start | bytes 12296 | tf_op jit(solution)/shard_map/ppermute | solution.py:23
  38.4 9.4 %collective-permute-start.5 = (f32[68,2]{1,0:T(8,128)S(1)}, f32[68,2]{1,0:T(8,128)S(1)}, u32[]{:S(2)}, u32[]{:S(2)}) collective-permute-start(f32[68,2]{1,0:T(8,128)S(1)} %get-tuple-element.18), channel_id=1, source_target_pairs={{0,1},{1,2},{2,3},{3,4},{4,5},{5,6},{6,7},{7,8},{8,9},{9,10},{10,1... | collective-permute-start | bytes 1640 | tf_op jit(solution)/shard_map/ppermute | solution.py:23
  42.0 7.4 %collective-permute-start.4 = (f32[68,2]{1,0:T(8,128)S(1)}, f32[68,2]{1,0:T(8,128)S(1)}, u32[]{:S(2)}, u32[]{:S(2)}) collective-permute-start(f32[68,2]{1,0:T(8,128)S(1)} %get-tuple-element.19), channel_id=1, source_target_pairs={{1,0},{2,1},{3,2},{4,3},{5,4},{6,5},{7,6},{8,7},{9,8},{10,9},{11,1... | collective-permute-start | bytes 1640 | tf_op jit(solution)/shard_map/ppermute | solution.py:23
  50.3 3.0 %collective-permute-start.6 = (f32[2,512]{1,0:T(2,128)S(1)}, f32[2,512]{1,0:T(2,128)S(1)}, u32[]{:S(2)}, u32[]{:S(2)}) collective-permute-start(f32[2,512]{1,0:T(2,128)S(1)} %get-tuple-element.34), channel_id=1, source_target_pairs={{448,0},{0,64},{64,128},{128,192},{192,256},{256,320},{320,384},{3... | collective-permute-start | bytes 12296 | tf_op jit(solution)/shard_map/ppermute | solution.py:17
  50.3 7.9 %collective-permute-start.8 = (f32[2,512]{1,0:T(2,128)S(1)}, f32[2,512]{1,0:T(2,128)S(1)}, u32[]{:S(2)}, u32[]{:S(2)}) collective-permute-start(f32[2,512]{1,0:T(2,128)S(1)} %get-tuple-element.35), channel_id=1, source_target_pairs={{64,0},{128,64},{192,128},{256,192},{320,256},{384,320},{448,384},... | collective-permute-start | bytes 12296 | tf_op jit(solution)/shard_map/ppermute | solution.py:17
  53.3 8.0 %collective-permute-start.7 = (f32[2,512]{1,0:T(2,128)S(1)}, f32[2,512]{1,0:T(2,128)S(1)}, u32[]{:S(2)}, u32[]{:S(2)}) collective-permute-start(f32[2,512]{1,0:T(2,128)S(1)} %collective-permute-done.6), channel_id=1, source_target_pairs={{0,8},{1,9},{2,10},{3,11},{4,12},{5,13},{6,14},{7,15},{8,16},{9,17... | collective-permute-start | bytes 12296 | tf_op jit(solution)/shard_map/ppermute | solution.py:23
  58.2 6.4 %collective-permute-start.9 = (f32[2,512]{1,0:T(2,128)S(1)}, f32[2,512]{1,0:T(2,128)S(1)}, u32[]{:S(2)}, u32[]{:S(2)}) collective-permute-start(f32[2,512]{1,0:T(2,128)S(1)} %collective-permute-done.8), channel_id=1, source_target_pairs={{8,0},{9,1},{10,2},{11,3},{12,4},{13,5},{14,6},{15,7},{16,8},{17,9... | collective-permute-start | bytes 12296 | tf_op jit(solution)/shard_map/ppermute | solution.py:23
  64.7 10.9 %collective-permute-start.11 = (f32[68,2]{1,0:T(8,128)S(1)}, f32[68,2]{1,0:T(8,128)S(1)}, u32[]{:S(2)}, u32[]{:S(2)}) collective-permute-start(f32[68,2]{1,0:T(8,128)S(1)} %get-tuple-element.16), channel_id=1, source_target_pairs={{0,1},{1,2},{2,3},{3,4},{4,5},{5,6},{6,7},{7,8},{8,9},{9,10},{10,1... | collective-permute-start | bytes 1640 | tf_op jit(solution)/shard_map/ppermute | solution.py:23
  67.9 9.2 %collective-permute-start.10 = (f32[68,2]{1,0:T(8,128)S(1)}, f32[68,2]{1,0:T(8,128)S(1)}, u32[]{:S(2)}, u32[]{:S(2)}) collective-permute-start(f32[68,2]{1,0:T(8,128)S(1)} %get-tuple-element.17), channel_id=1, source_target_pairs={{1,0},{2,1},{3,2},{4,3},{5,4},{6,5},{7,6},{8,7},{9,8},{10,9},{11,1... | collective-permute-start | bytes 1640 | tf_op jit(solution)/shard_map/ppermute | solution.py:23
  78.1 3.0 %collective-permute-start.12 = (f32[2,512]{1,0:T(2,128)S(1)}, f32[2,512]{1,0:T(2,128)S(1)}, u32[]{:S(2)}, u32[]{:S(2)}) collective-permute-start(f32[2,512]{1,0:T(2,128)S(1)} %get-tuple-element.30), channel_id=1, source_target_pairs={{448,0},{0,64},{64,128},{128,192},{192,256},{256,320},{320,384},{3... | collective-permute-start | bytes 12296 | tf_op jit(solution)/shard_map/ppermute | solution.py:17
  78.1 5.2 %collective-permute-start.14 = (f32[2,512]{1,0:T(2,128)S(1)}, f32[2,512]{1,0:T(2,128)S(1)}, u32[]{:S(2)}, u32[]{:S(2)}) collective-permute-start(f32[2,512]{1,0:T(2,128)S(1)} %get-tuple-element.31), channel_id=1, source_target_pairs={{64,0},{128,64},{192,128},{256,192},{320,256},{384,320},{448,384},... | collective-permute-start | bytes 12296 | tf_op jit(solution)/shard_map/ppermute | solution.py:17
  81.1 8.0 %collective-permute-start.13 = (f32[2,512]{1,0:T(2,128)S(1)}, f32[2,512]{1,0:T(2,128)S(1)}, u32[]{:S(2)}, u32[]{:S(2)}) collective-permute-start(f32[2,512]{1,0:T(2,128)S(1)} %collective-permute-done.12), channel_id=1, source_target_pairs={{0,8},{1,9},{2,10},{3,11},{4,12},{5,13},{6,14},{7,15},{8,16},{9,17... | collective-permute-start | bytes 12296 | tf_op jit(solution)/shard_map/ppermute | solution.py:23
  83.3 7.1 %collective-permute-start.15 = (f32[2,512]{1,0:T(2,128)S(1)}, f32[2,512]{1,0:T(2,128)S(1)}, u32[]{:S(2)}, u32[]{:S(2)}) collective-permute-start(f32[2,512]{1,0:T(2,128)S(1)} %collective-permute-done.14), channel_id=1, source_target_pairs={{8,0},{9,1},{10,2},{11,3},{12,4},{13,5},{14,6},{15,7},{16,8},{17,9... | collective-permute-start | bytes 12296 | tf_op jit(solution)/shard_map/ppermute | solution.py:23
  90.5 10.2 %collective-permute-start.17 = (f32[68,2]{1,0:T(8,128)S(1)}, f32[68,2]{1,0:T(8,128)S(1)}, u32[]{:S(2)}, u32[]{:S(2)}) collective-permute-start(f32[68,2]{1,0:T(8,128)S(1)} %get-tuple-element.14), channel_id=1, source_target_pairs={{0,1},{1,2},{2,3},{3,4},{4,5},{5,6},{6,7},{7,8},{8,9},{9,10},{10,1... | collective-permute-start | bytes 1640 | tf_op jit(solution)/shard_map/ppermute | solution.py:23
  92.6 9.7 %collective-permute-start.16 = (f32[68,2]{1,0:T(8,128)S(1)}, f32[68,2]{1,0:T(8,128)S(1)}, u32[]{:S(2)}, u32[]{:S(2)}) collective-permute-start(f32[68,2]{1,0:T(8,128)S(1)} %get-tuple-element.15), channel_id=1, source_target_pairs={{1,0},{2,1},{3,2},{4,3},{5,4},{6,5},{7,6},{8,7},{9,8},{10,9},{11,1... | collective-permute-start | bytes 1640 | tf_op jit(solution)/shard_map/ppermute | solution.py:23
  102.5 1.2 copy-start.1
  103.2 11.2 %collective-permute-start.18 = (f32[2,512]{1,0:T(2,128)S(1)}, f32[2,512]{1,0:T(2,128)S(1)}, u32[]{:S(2)}, u32[]{:S(2)}) collective-permute-start(f32[2,512]{1,0:T(2,128)S(1)} %get-tuple-element.26), channel_id=1, source_target_pairs={{448,0},{0,64},{64,128},{128,192},{192,256},{256,320},{320,384},{3... | collective-permute-start | bytes 12296 | tf_op jit(solution)/shard_map/ppermute | solution.py:17
  105.4 62.6 %all-to-all-start.1 = ((f32[1,512,512]{2,0,1:T(1,128)}), f32[1,512,512]{2,0,1:T(1,128)S(1)}, u32[]{:S(2)}, u32[]{:S(2)}) async-start(f32[1,512,512]{2,0,1:T(1,128)} %broadcast_in_dim_squeeze.7), calls=%async_computation.1 | async-start | bytes 2097152 | tf_op jit(solution)/shard_map/all_to_all | solution.py:119
  114.2 12.1 %collective-permute-start.20 = (f32[2,512]{1,0:T(2,128)S(1)}, f32[2,512]{1,0:T(2,128)S(1)}, u32[]{:S(2)}, u32[]{:S(2)}) collective-permute-start(f32[2,512]{1,0:T(2,128)S(1)} %get-tuple-element.27), channel_id=1, source_target_pairs={{64,0},{128,64},{192,128},{256,192},{320,256},{384,320},{448,384},... | collective-permute-start | bytes 12296 | tf_op jit(solution)/shard_map/ppermute | solution.py:17
  114.3 16.3 %collective-permute-start.19 = (f32[2,512]{1,0:T(2,128)S(1)}, f32[2,512]{1,0:T(2,128)S(1)}, u32[]{:S(2)}, u32[]{:S(2)}) collective-permute-start(f32[2,512]{1,0:T(2,128)S(1)} %collective-permute-done.18), channel_id=1, source_target_pairs={{0,8},{1,9},{2,10},{3,11},{4,12},{5,13},{6,14},{7,15},{8,16},{9,17... | collective-permute-start | bytes 12296 | tf_op jit(solution)/shard_map/ppermute | solution.py:23
  126.3 6.4 %collective-permute-start.21 = (f32[2,512]{1,0:T(2,128)S(1)}, f32[2,512]{1,0:T(2,128)S(1)}, u32[]{:S(2)}, u32[]{:S(2)}) collective-permute-start(f32[2,512]{1,0:T(2,128)S(1)} %collective-permute-done.20), channel_id=1, source_target_pairs={{8,0},{9,1},{10,2},{11,3},{12,4},{13,5},{14,6},{15,7},{16,8},{17,9... | collective-permute-start | bytes 12296 | tf_op jit(solution)/shard_map/ppermute | solution.py:23
  132.8 10.9 %collective-permute-start.23 = (f32[68,2]{1,0:T(8,128)S(1)}, f32[68,2]{1,0:T(8,128)S(1)}, u32[]{:S(2)}, u32[]{:S(2)}) collective-permute-start(f32[68,2]{1,0:T(8,128)S(1)} %get-tuple-element.12), channel_id=1, source_target_pairs={{0,1},{1,2},{2,3},{3,4},{4,5},{5,6},{6,7},{7,8},{8,9},{9,10},{10,1... | collective-permute-start | bytes 1640 | tf_op jit(solution)/shard_map/ppermute | solution.py:23
  134.9 10.4 %collective-permute-start.22 = (f32[68,2]{1,0:T(8,128)S(1)}, f32[68,2]{1,0:T(8,128)S(1)}, u32[]{:S(2)}, u32[]{:S(2)}) collective-permute-start(f32[68,2]{1,0:T(8,128)S(1)} %get-tuple-element.13), channel_id=1, source_target_pairs={{1,0},{2,1},{3,2},{4,3},{5,4},{6,5},{7,6},{8,7},{9,8},{10,9},{11,1... | collective-permute-start | bytes 1640 | tf_op jit(solution)/shard_map/ppermute | solution.py:23
  146.2 29.4 %copy-start = (f32[64,512]{1,0:T(8,128)}, f32[64,512]{1,0:T(8,128)S(1)}, u32[]{:S(2)}) copy-start(f32[64,512]{1,0:T(8,128)S(1)} %fusion.24) | copy-start | bytes 393220
  146.2 1.5 collective-permute-start.26
  146.3 3.9 %collective-permute-start.24 = (f32[1,512]{1,0:T(1,128)S(1)}, f32[1,512]{1,0:T(1,128)S(1)}, u32[]{:S(2)}, u32[]{:S(2)}) collective-permute-start(f32[1,512]{1,0:T(1,128)S(1)} %get-tuple-element.23), channel_id=1, source_target_pairs={{448,0},{0,64},{64,128},{128,192},{192,256},{256,320},{320,384},{3... | collective-permute-start | bytes 6152 | tf_op jit(solution)/shard_map/ppermute | solution.py:17
  147.7 6.8 %collective-permute-start.27 = (f32[1,512]{1,0:T(1,128)S(1)}, f32[1,512]{1,0:T(1,128)S(1)}, u32[]{:S(2)}, u32[]{:S(2)}) collective-permute-start(f32[1,512]{1,0:T(1,128)S(1)} %collective-permute-done.26), channel_id=1, source_target_pairs={{8,0},{9,1},{10,2},{11,3},{12,4},{13,5},{14,6},{15,7},{16,8},{17,9... | collective-permute-start | bytes 6152 | tf_op jit(solution)/shard_map/ppermute | solution.py:23
  150.3 7.6 %collective-permute-start.25 = (f32[1,512]{1,0:T(1,128)S(1)}, f32[1,512]{1,0:T(1,128)S(1)}, u32[]{:S(2)}, u32[]{:S(2)}) collective-permute-start(f32[1,512]{1,0:T(1,128)S(1)} %collective-permute-done.24), channel_id=1, source_target_pairs={{0,8},{1,9},{2,10},{3,11},{4,12},{5,13},{6,14},{7,15},{8,16},{9,17... | collective-permute-start | bytes 6152 | tf_op jit(solution)/shard_map/ppermute | solution.py:23
  157.9 8.1 %collective-permute-start.28 = (f32[66,1]{1,0:T(8,128)S(1)}, f32[66,1]{1,0:T(8,128)S(1)}, u32[]{:S(2)}, u32[]{:S(2)}) collective-permute-start(f32[66,1]{1,0:T(8,128)S(1)} %pad_maximum_fusion.40), channel_id=1, source_target_pairs={{1,0},{2,1},{3,2},{4,3},{5,4},{6,5},{7,6},{8,7},{9,8},{10,9},{11,1... | collective-permute-start | bytes 800 | tf_op jit(solution)/shard_map/ppermute | solution.py:23
  166.1 9.5 %collective-permute-start.29 = (f32[66,1]{1,0:T(8,128)S(1)}, f32[66,1]{1,0:T(8,128)S(1)}, u32[]{:S(2)}, u32[]{:S(2)}) collective-permute-start(f32[66,1]{1,0:T(8,128)S(1)} %get-tuple-element.11), channel_id=1, source_target_pairs={{0,1},{1,2},{2,3},{3,4},{4,5},{5,6},{6,7},{7,8},{8,9},{9,10},{10,1... | collective-permute-start | bytes 800 | tf_op jit(solution)/shard_map/ppermute | solution.py:23
  168.1 7.5 %copy-start.2 = (s32[1,64,512]{2,1,0:T(8,128)S(1)}, s32[1,64,512]{2,1,0:T(8,128)}, u32[]{:S(2)}) copy-start(s32[1,64,512]{2,1,0:T(8,128)} %param.5) | copy-start | bytes 393220
where the time goes:
time: 177 us; the launch traced here: 176 us
  starting transfers between devices  101 us (57%)
  waiting for transfers between devices  44 us (25%)
  blocking collectives  19.4 us (11%)
  local copies, waits for them, and re-layouts  5.38 us (3%)
  other arithmetic  5.01 us (3%)
    ppermute x20, starting transfers between devices, shifted_2(): lax.ppermute(value, axis, [(source, source + steps) for source in range(f...  86.7 us
    ppermute x20, waiting for transfers between devices, shifted_2(): lax.ppermute(value, axis, [(source, source + steps) for source in range(f...  30.3 us
    all_to_all x1, blocking collectives, local(): lax.all_to_all(depth_tile[None], 'slab', split_axis=1, concat_axis=0, til...  19.4 us
    ppermute x10, waiting for transfers between devices, shifted(): return lax.ppermute(block, axis, route)  13.7 us
    all_to_all x1, starting transfers between devices, local(): lax.all_to_all(thick_tile[None], 'slab', split_axis=1, concat_axis=0, til...  8.8 us
    ppermute x10, starting transfers between devices, shifted(): return lax.ppermute(block, axis, route)  5.87 us
  transfers between devices with their start and end apart: 31, of which 16 were waited for; matrix products, arithmetic and copies ran while one was open for 2% of the time, Pallas kernels for 0%

commit v1 on v0

v1 whole, which is shorter than its diff:
```python
import functools
import math

import jax
import jax.numpy as jnp
from jax import lax
from jax.experimental import pallas as pl
from jax.experimental.pallas import tpu as pltpu
from jax.sharding import PartitionSpec as P

SWEEPS = 4
FLOW_STEP = 0.2

PAD = 16
LANES = 128


def ring(value, step):
    count = lax.axis_size("slab")
    return lax.ppermute(value, "slab", [(i, (i + step) % count) for i in range(count)])


def reduce_bands(bands, combine, index):
    count = bands.shape[0]

    def share(offset):
        return lax.dynamic_index_in_dim(bands, (index + offset + count) % count, 0, keepdims=False)

    ahead = count // 2
    behind = count - 1 - ahead
    forward = share(ahead)
    backward = share(-behind)
    for distance in range(ahead, 0, -1):
        forward = ring(forward, 1)
        if distance > 1:
            forward = combine(forward, share(distance - 1))
        if distance <= behind:
            backward = ring(backward, -1)
            if distance > 1:
                backward = combine(backward, share(1 - distance))
    return share(0), forward, backward


def tile_edges(value, grid, slabs):
    tiles = grid * grid
    route = []
    for t in range(tiles - grid):
        upper = (slabs - 1) * tiles + t
        lower = t + grid
        route += [(upper, lower), (lower, upper)]
    return lax.ppermute(value, ("slab", "tile"), route)


def to_column(value, grid, step):
    route = []
    for t in range(grid * grid):
        if 0 <= t % grid + step < grid:
            route.append((t, t + step))
    return lax.ppermute(value, "tile", route)


def flow_kernel(
    rows,
    width,
    edge_ref,
    above_ref,
    band_ref,
    below_ref,
    left_ref,
    right_ref,
    thick_a_ref,
    thick_b_ref,
    thick_c_ref,
    cover_ref,
    smooth_ref,
    shade_ref,
    surface,
    partial,
    normal_y,
):
    blocks = width // LANES
    total = rows + 2 * PAD
    top = PAD
    bottom = PAD + rows
    lane = lax.broadcasted_iota(jnp.int32, (8, LANES), 1)

    for j in range(blocks):
        cols = pl.ds(j * LANES, LANES)
        surface[j, 0:PAD, :] = above_ref[:, cols]
        surface[j, top:bottom, :] = band_ref[:, cols]
        surface[j, bottom:total, :] = below_ref[:, cols]
    for r in range(0, total, 8):
        surface[blocks, r : r + 8, :] = jnp.where(
            lane < LANES // 2, right_ref[r : r + 8, :], left_ref[r : r + 8, :]
        )

    def refill():
        @pl.when(edge_ref[0] == 1)
        def _():
            for j in range(blocks + 1):
                surface[j, top - 2 : top, :] = jnp.broadcast_to(surface[j, top : top + 1, :], (2, LANES))

        @pl.when(edge_ref[1] == 1)
        def _():
            for j in range(blocks + 1):
                surface[j, bottom : bottom + 2, :] = jnp.broadcast_to(
                    surface[j, bottom - 1 : bottom, :], (2, LANES)
                )

        @pl.when(edge_ref[2] == 1)
        def _():
            for r in range(8, total - 8, 8):
                first = jnp.broadcast_to(surface[0, r : r + 8, 0:1], (8, LANES))
                surface[blocks, r : r + 8, :] = jnp.where(
                    lane >= LANES // 2, first, surface[blocks, r : r + 8, :]
                )

        @pl.when(edge_ref[3] == 1)
        def _():
            for r in range(8, total - 8, 8):
                last = jnp.broadcast_to(
                    surface[blocks - 1, r : r + 8, LANES - 1 : LANES], (8, LANES)
                )
                surface[blocks, r : r + 8, :] = jnp.where(
                    lane < LANES // 2, last, surface[blocks, r : r + 8, :]
                )

    def across(pieces):
        after = [pltpu.roll(p, LANES - 1, 1) for p in pieces]
        before = [pltpu.roll(p, 1, 1) for p in pieces]
        n = len(pieces)
        return [
            jnp.where(lane == LANES - 1, after[(j + 1) % n], after[j])
            - jnp.where(lane == 0, before[(j - 1) % n], before[j])
            for j in range(n)
        ]

    for _ in range(SWEEPS):
        refill()
        for r in range(8, total - 8, 8):
            here = [surface[j, r : r + 8, :] for j in range(blocks + 1)]
            wide_x = across(here)
            wide_y = [
                surface[j, r + 1 : r + 9, :] - surface[j, r - 1 : r + 7, :] for j in range(blocks + 1)
            ]
            inverse = [
                lax.rsqrt(1.0 + 0.25 * (x * x + y * y)) for x, y in zip(wide_x, wide_y)
            ]
            spread = across([x * w for x, w in zip(wide_x, inverse)])
            for j in range(blocks + 1):
                normal_y[j, r : r + 8, :] = wide_y[j] * inverse[j]
                partial[j, r : r + 8, :] = here[j] + (0.25 * FLOW_STEP) * spread[j]
        for r in range(8, total - 8, 8):
            for j in range(blocks + 1):
                surface[j, r : r + 8, :] = partial[j, r : r + 8, :] + (0.25 * FLOW_STEP) * (
                    normal_y[j, r + 1 : r + 9, :] - normal_y[j, r - 1 : r + 7, :]
                )

    refill()
    for r in range(0, rows, 8):
        here = [surface[j, top + r : top + r + 8, :] for j in range(blocks + 1)]
        wide_x = across(here)
        for j in range(blocks):
            cols = pl.ds(j * LANES, LANES)
            x = 0.5 * wide_x[j]
            y = 0.5 * (
                surface[j, top + r + 1 : top + r + 9, :] - surface[j, top + r - 1 : top + r + 7, :]
            )
            inverse = lax.rsqrt(1.0 + (x * x + y * y))
            diffuse = jnp.maximum((0.8 - 0.36 * x - 0.48 * y) * inverse, 0.0)
            gloss = jnp.maximum((0.9487 - 0.1897 * x - 0.253 * y) * inverse, 0.0)
            for _ in range(4):
                gloss = gloss * gloss
            thick = (
                thick_a_ref[r : r + 8, cols] + thick_b_ref[r : r + 8, cols] + thick_c_ref[r : r + 8, cols]
            )
            fluid = cover_ref[r : r + 8, cols].astype(jnp.float32)
            lit = 0.15 + 0.7 * jnp.exp(-0.8 * thick) * diffuse + 0.4 * gloss
            smooth_ref[r : r + 8, cols] = here[j]
            shade_ref[r : r + 8, cols] = fluid * lit + (1.0 - fluid) * 0.05


def local(depth_layers, thickness_layers, coverage):
    slabs = lax.axis_size("slab")
    grid = math.isqrt(lax.axis_size("tile"))
    slab = lax.axis_index("slab")
    tile = lax.axis_index("tile")
    _, _, height, width = depth_layers.shape
    rows = height // slabs
    first, last = slab == 0, slab == slabs - 1
    edges = jnp.stack(
        [
            first & (tile // grid == 0),
            last & (tile // grid == grid - 1),
            tile % grid == 0,
            tile % grid == grid - 1,
        ]
    ).astype(jnp.int32)

    parts = reduce_bands(depth_layers.reshape(slabs, rows, width), jnp.minimum, slab)
    band = jnp.minimum(jnp.minimum(parts[0], parts[1]), parts[2])

    head, tail = band[:PAD], band[-PAD:]
    above = ring(tail, 1)
    below = ring(head, -1)
    beyond = tile_edges(jnp.where(first, head, tail), grid, slabs)
    above = jnp.where(first, beyond, above)
    below = jnp.where(last, beyond, below)

    def column(start):
        cut = slice(start, start + LANES)
        return jnp.concatenate([above[:, cut], band[:, cut], below[:, cut]], axis=0)

    left = to_column(column(width - LANES), grid, 1)
    right = to_column(column(0), grid, -1)

    thickness_layers, band = lax.optimization_barrier((thickness_layers, band))
    thick = reduce_bands(thickness_layers.reshape(slabs, rows, width), jnp.add, slab)

    vmem = pl.BlockSpec(memory_space=pltpu.VMEM)
    total = rows + 2 * PAD
    blocks = width // LANES + 1
    out = jax.ShapeDtypeStruct((rows, width), jnp.float32)
    smooth, shade = pl.pallas_call(
        functools.partial(flow_kernel, rows, width),
        out_shape=(out, out),
        in_specs=[pl.BlockSpec(memory_space=pltpu.SMEM)] + [vmem] * 9,
        out_specs=(vmem, vmem),
        scratch_shapes=[pltpu.VMEM((blocks, total, LANES), jnp.float32)] * 3,
    )(edges, above, band, below, left, right, *thick, coverage[0])
    return (smooth[None], shade[None])


def solution(mesh):
    return jax.shard_map(
        local,
        mesh=mesh,
        in_specs=(
            P("slab", "tile", None, None),
            P("slab", "tile", None, None),
            P("tile", "slab", None),
        ),
        out_specs=(P("tile", "slab", None), P("tile", "slab", None)),
        check_vma=False,
    )
```

time: 177 us -> 67.1 us (0.38)
  the two profiles are of different devices: /device:TPU:136 before, /device:TPU:96 now
where the time goes in v1:
time: 67.1 us; the launch traced here: 66.9 us
  starting transfers between devices  32.8 us (49%)
  waiting for transfers between devices  24.6 us (37%)
  Pallas kernels  4.36 us (6%)
  local copies, waits for them, and re-layouts  2.48 us (4%)
  other arithmetic  1.75 us (3%)
  between operations  0.97 us (1%)
    ppermute x16, starting transfers between devices, ring(): lax.ppermute(value, 'slab', [(i, (i + step) % count) for i in range(count)])  24.7 us
    ppermute x16, waiting for transfers between devices, ring(): lax.ppermute(value, 'slab', [(i, (i + step) % count) for i in range(count)])  19 us
    ppermute x2, starting transfers between devices, to_column(): return lax.ppermute(value, 'tile', route)  6.12 us
    ppermute x2, waiting for transfers between devices, to_column(): return lax.ppermute(value, 'tile', route)  5.56 us
    pallas_call x1, Pallas kernels, local(): pl.pallas_call(functools.partial(flow_kernel, rows, width), out_shape=(ou...  4.36 us
    ppermute x1, starting transfers between devices, tile_edges(): return lax.ppermute(value, ('slab', 'tile'), route)  1.91 us
    squeeze x2, local copies, waits for them, and re-layouts, share(): lax.dynamic_index_in_dim(bands, (index + offset + count) % count, 0, keep...  1.76 us
  transfers between devices with their start and end apart: 19, of which 7 were waited for; matrix products, arithmetic and copies ran while one was open for 2% of the time, Pallas kernels for 0%

profile of v1, /device:TPU:96, one launch (start us, length us, event | category | flops | bytes accessed | tf_op | source)
XLA Modules:
  0.0 66.9 jit_solution(11944015071251660647)
XLA Ops:
  0.6 0.0 copy-start.1
  0.7 1.1 %dynamic-slice_bitcast_fusion.4 = (f32[64,512]{1,0:T(8,128)S(1)}, f32[64,512]{1,0:T(8,128)S(1)}) fusion(f32[8,64,512]{2,1,0:T(8,128)} %bitcast.43, s32[]{:T(128)S(6)} %select_n.119, s32[]{:T(128)S(6)} %select_n.127), kind=kLoop, calls=%fused_computation.16 | loop fusion | bytes 524296 | tf_op jit(solution)/shard_map/jit(dynamic_index_in_dim)/squeeze | solution.py:27
  1.7 0.0 collective-permute-start
  1.8 2.9 %collective-permute-start.4 = (f32[64,512]{1,0:T(8,128)S(1)}, f32[64,512]{1,0:T(8,128)S(1)}, u32[]{:S(2)}, u32[]{:S(2)}) collective-permute-start(f32[64,512]{1,0:T(8,128)S(1)} %get-tuple-element.22), channel_id=1, source_target_pairs={{0,448},{64,0},{128,64},{192,128},{256,192},{320,256},{384,320},{4... | collective-permute-start | bytes 393224 | tf_op jit(solution)/shard_map/ppermute | solution.py:20
  4.7 2.6 %collective-permute-done = f32[64,512]{1,0:T(8,128)S(1)} collective-permute-done((f32[64,512]{1,0:T(8,128)S(1)}, f32[64,512]{1,0:T(8,128)S(1)}, u32[]{:S(2)}, u32[]{:S(2)}) %collective-permute-start) | collective-permute-done | bytes 131104 | tf_op jit(solution)/shard_map/ppermute | solution.py:20
  7.4 0.9 %bitcast_minimum_fusion.4 = f32[64,512]{1,0:T(8,128)S(1)} fusion(f32[64,512]{1,0:T(8,128)S(1)} %collective-permute-done, f32[8,64,512]{2,1,0:T(8,128)} %bitcast.44, s32[]{:T(128)S(6)} %select_n.121), kind=kLoop, calls=%fused_computation.9 | loop fusion | flops 32768 | bytes 393220 | tf_op jit(solution)/shard_map/min | solution.py:36
  8.3 0.0 collective-permute-start.1
  8.3 0.0 copy-start.2
  8.4 0.0 collective-permute-done.4
  8.4 5.5 %collective-permute-done.1 = f32[64,512]{1,0:T(8,128)S(1)} collective-permute-done((f32[64,512]{1,0:T(8,128)S(1)}, f32[64,512]{1,0:T(8,128)S(1)}, u32[]{:S(2)}, u32[]{:S(2)}) %collective-permute-start.1) | collective-permute-done | bytes 131104 | tf_op jit(solution)/shard_map/ppermute | solution.py:20
  13.9 0.0 copy-done.1
  13.9 0.0 collective-permute-start.2
  14.0 2.9 %collective-permute-start.5 = (f32[64,512]{1,0:T(8,128)S(1)}, f32[64,512]{1,0:T(8,128)S(1)}, u32[]{:S(2)}, u32[]{:S(2)}) collective-permute-start(f32[64,512]{1,0:T(8,128)S(1)} %get-tuple-element.20), channel_id=1, source_target_pairs={{0,448},{64,0},{128,64},{192,128},{256,192},{320,256},{384,320},{4... | collective-permute-start | bytes 393224 | tf_op jit(solution)/shard_map/ppermute | solution.py:20
  16.9 2.6 %collective-permute-done.2 = f32[64,512]{1,0:T(8,128)S(1)} collective-permute-done((f32[64,512]{1,0:T(8,128)S(1)}, f32[64,512]{1,0:T(8,128)S(1)}, u32[]{:S(2)}, u32[]{:S(2)}) %collective-permute-start.2) | collective-permute-done | bytes 131104 | tf_op jit(solution)/shard_map/ppermute | solution.py:20
  19.6 0.0 collective-permute-done.5
  19.6 0.0 collective-permute-start.3
  19.6 3.0 %collective-permute-start.6 = (f32[64,512]{1,0:T(8,128)S(1)}, f32[64,512]{1,0:T(8,128)S(1)}, u32[]{:S(2)}, u32[]{:S(2)}) collective-permute-start(f32[64,512]{1,0:T(8,128)S(1)} %get-tuple-element.18), channel_id=1, source_target_pairs={{0,448},{64,0},{128,64},{192,128},{256,192},{320,256},{384,320},{4... | collective-permute-start | bytes 393224 | tf_op jit(solution)/shard_map/ppermute | solution.py:20
  22.6 2.6 %collective-permute-done.3 = f32[64,512]{1,0:T(8,128)S(1)} collective-permute-done((f32[64,512]{1,0:T(8,128)S(1)}, f32[64,512]{1,0:T(8,128)S(1)}, u32[]{:S(2)}, u32[]{:S(2)}) %collective-permute-start.3) | collective-permute-done | bytes 131104 | tf_op jit(solution)/shard_map/ppermute | solution.py:20
  25.2 0.0 collective-permute-done.6
  25.3 0.0 copy-start
  25.3 0.0 copy-done.2
  25.3 0.7 %dynamic-slice_bitcast_fusion = (f32[64,512]{1,0:T(8,128)S(1)}, f32[64,512]{1,0:T(8,128)S(1)}, f32[64,512]{1,0:T(8,128)}) fusion(f32[8,64,512]{2,1,0:T(8,128)S(1)} %bitcast.48, s32[]{:T(128)S(6)} %select_n.127, s32[]{:T(128)S(6)} %select_n.119, s32[]{:T(128)S(6)} %select_n.117), kind=kLoop, calls=%fused_computation.12 | loop fusion | bytes 786444 | tf_op jit(solution)/shard_map/jit(dynamic_index_in_dim)/squeeze | solution.py:27
  26.0 0.0 collective-permute-start.12
  26.0 3.0 %collective-permute-start.16 = (f32[64,512]{1,0:T(8,128)S(1)}, f32[64,512]{1,0:T(8,128)S(1)}, u32[]{:S(2)}, u32[]{:S(2)}) collective-permute-start(f32[64,512]{1,0:T(8,128)S(1)} %get-tuple-element.14), channel_id=1, source_target_pairs={{0,448},{64,0},{128,64},{192,128},{256,192},{320,256},{384,320},{4... | collective-permute-start | bytes 393224 | tf_op jit(solution)/shard_map/ppermute | solution.py:20
  29.0 1.9 %collective-permute-start.7 = (f32[16,512]{1,0:T(8,128)S(1)}, f32[16,512]{1,0:T(8,128)S(1)}, u32[]{:S(2)}, u32[]{:S(2)}) collective-permute-start(f32[16,512]{1,0:T(8,128)S(1)} %get-tuple-element.26), channel_id=1, source_target_pairs={{448,8},{8,448},{449,9},{9,449},{450,10},{10,450},{451,11},{11,451... | collective-permute-start | bytes 98312 | tf_op jit(solution)/shard_map/ppermute | solution.py:51
  30.9 0.0 collective-permute-start.8
  30.9 6.9 %collective-permute-start.9 = (f32[16,512]{1,0:T(8,128)S(1)}, f32[16,512]{1,0:T(8,128)S(1)}, u32[]{:S(2)}, u32[]{:S(2)}) collective-permute-start(f32[16,512]{1,0:T(8,128)S(1)} %get-tuple-element.25), channel_id=1, source_target_pairs={{0,448},{64,0},{128,64},{192,128},{256,192},{320,256},{384,320},{4... | collective-permute-start | bytes 98312 | tf_op jit(solution)/shard_map/ppermute | solution.py:20
  37.8 0.0 copy-done
  37.8 0.0 collective-permute-done.12
  37.8 0.0 collective-permute-start.13
  37.9 0.0 collective-permute-done.7
  37.9 1.5 %collective-permute-done.8 = f32[16,512]{1,0:T(8,128)S(1)} collective-permute-done((f32[16,512]{1,0:T(8,128)S(1)}, f32[16,512]{1,0:T(8,128)S(1)}, u32[]{:S(2)}, u32[]{:S(2)}) %collective-permute-start.8) | collective-permute-done | bytes 32800 | tf_op jit(solution)/shard_map/ppermute | solution.py:20
  39.4 0.0 collective-permute-done.9
  39.4 0.0 copy-start.3
  39.4 0.0 copy-start.4
  39.4 0.0 collective-permute-done.16
  39.4 4.0 %collective-permute-done.13 = f32[64,512]{1,0:T(8,128)S(1)} collective-permute-done((f32[64,512]{1,0:T(8,128)S(1)}, f32[64,512]{1,0:T(8,128)S(1)}, u32[]{:S(2)}, u32[]{:S(2)}) %collective-permute-start.13) | collective-permute-done | bytes 131104 | tf_op jit(solution)/shard_map/ppermute | solution.py:20
  43.5 0.0 collective-permute-start.14
  43.5 2.9 %collective-permute-start.17 = (f32[64,512]{1,0:T(8,128)S(1)}, f32[64,512]{1,0:T(8,128)S(1)}, u32[]{:S(2)}, u32[]{:S(2)}) collective-permute-start(f32[64,512]{1,0:T(8,128)S(1)} %get-tuple-element.12), channel_id=1, source_target_pairs={{0,448},{64,0},{128,64},{192,128},{256,192},{320,256},{384,320},{4... | collective-permute-start | bytes 393224 | tf_op jit(solution)/shard_map/ppermute | solution.py:20
  46.5 0.0 copy-done.3
  46.5 0.0 copy-done.4
  46.5 4.2 %collective-permute-start.11 = (f32[96,128]{1,0:T(8,128)S(1)}, f32[96,128]{1,0:T(8,128)S(1)}, u32[]{:S(2)}, u32[]{:S(2)}) collective-permute-start(f32[96,128]{1,0:T(8,128)S(1)} %pad_maximum_fusion.1), channel_id=1, source_target_pairs={{1,0},{2,1},{3,2},{4,3},{5,4},{6,5},{7,6},{9,8},{10,9},{11,10},{12... | collective-permute-start | bytes 147464 | tf_op jit(solution)/shard_map/ppermute | solution.py:59
  50.7 0.0 collective-permute-done.14
  50.7 0.0 collective-permute-done.17
  50.8 0.0 collective-permute-start.15
  50.8 2.9 %collective-permute-start.18 = (f32[64,512]{1,0:T(8,128)S(1)}, f32[64,512]{1,0:T(8,128)S(1)}, u32[]{:S(2)}, u32[]{:S(2)}) collective-permute-start(f32[64,512]{1,0:T(8,128)S(1)} %get-tuple-element.10), channel_id=1, source_target_pairs={{0,448},{64,0},{128,64},{192,128},{256,192},{320,256},{384,320},{4... | collective-permute-start | bytes 393224 | tf_op jit(solution)/shard_map/ppermute | solution.py:20
  53.7 1.9 %collective-permute-start.10 = (f32[96,128]{1,0:T(8,128)S(1)}, f32[96,128]{1,0:T(8,128)S(1)}, u32[]{:S(2)}, u32[]{:S(2)}) collective-permute-start(f32[96,128]{1,0:T(8,128)S(1)} %pad_maximum_fusion), channel_id=1, source_target_pairs={{0,1},{1,2},{2,3},{3,4},{4,5},{5,6},{6,7},{8,9},{9,10},{10,11},{11... | collective-permute-start | bytes 147464 | tf_op jit(solution)/shard_map/ppermute | solution.py:59
  55.7 0.6 add_convert_fusion.edge_ref
  56.3 0.0 collective-permute-done.11.right_ref
  56.3 0.0 copy-start.7
  56.3 5.6 %collective-permute-done.10.left_ref = f32[96,128]{1,0:T(8,128)S(1)} collective-permute-done((f32[96,128]{1,0:T(8,128)S(1)}, f32[96,128]{1,0:T(8,128)S(1)}, u32[]{:S(2)}, u32[]{:S(2)}) %collective-permute-start.10) | collective-permute-done | bytes 49184 | tf_op jit(solution)/shard_map/ppermute | solution.py:59
  61.8 0.0 copy-start.8
  61.8 0.0 collective-permute-done.15.thick_b_ref
  61.8 0.0 copy-start.5
  61.8 0.0 collective-permute-done.18.thick_c_ref
  61.8 0.0 copy-start.6
  61.9 0.0 copy-done.7
  61.9 0.6 copy-done.8
  62.4 0.1 copy-done.5
  62.5 0.0 copy-done.6
  62.5 4.4 %shard_map.50 = (f32[64,512]{1,0:T(8,128)}, f32[64,512]{1,0:T(8,128)}) custom-call(s32[4]{0:T(128)} %add_convert_fusion.edge_ref, f32[16,512]{1,0:T(8,128)} %copy-done.4, f32[64,512]{1,0:T(8,128)} %copy-done, f32[16,512]{1,0:T(8,128)} %copy-done.3, f32[96,128]{1,0:T(8,128)} %copy-done.8, f32[96,128]{1,0:T(8,128)} %copy-done.7, ...), custom_call_target="tpu_custom_call" | custom-call | tf_op jit(solution)/shard_map/pallas_call | solution.py:224
  (12 shorter events, 0.2 us)
Async XLA Ops:
  0.6 13.3 %copy-start.1 = (f32[1,1,512,512]{3,2,1,0:T(8,128)S(1)}, f32[1,1,512,512]{3,2,1,0:T(8,128)}, u32[]{:S(2)}) copy-start(f32[1,1,512,512]{3,2,1,0:T(8,128)} %param.3) | copy-start | bytes 3145732
  1.7 5.6 %collective-permute-start = (f32[64,512]{1,0:T(8,128)S(1)}, f32[64,512]{1,0:T(8,128)S(1)}, u32[]{:S(2)}, u32[]{:S(2)}) collective-permute-start(f32[64,512]{1,0:T(8,128)S(1)} %get-tuple-element.21), channel_id=1, source_target_pairs={{0,64},{64,128},{128,192},{192,256},{256,320},{320,384},{384,448},... | collective-permute-start | bytes 393224 | tf_op jit(solution)/shard_map/ppermute | solution.py:20
  1.8 6.6 %collective-permute-start.4 = (f32[64,512]{1,0:T(8,128)S(1)}, f32[64,512]{1,0:T(8,128)S(1)}, u32[]{:S(2)}, u32[]{:S(2)}) collective-permute-start(f32[64,512]{1,0:T(8,128)S(1)} %get-tuple-element.22), channel_id=1, source_target_pairs={{0,448},{64,0},{128,64},{192,128},{256,192},{320,256},{384,320},{4... | collective-permute-start | bytes 393224 | tf_op jit(solution)/shard_map/ppermute | solution.py:20
  8.3 5.6 %collective-permute-start.1 = (f32[64,512]{1,0:T(8,128)S(1)}, f32[64,512]{1,0:T(8,128)S(1)}, u32[]{:S(2)}, u32[]{:S(2)}) collective-permute-start(f32[64,512]{1,0:T(8,128)S(1)} %bitcast_minimum_fusion.4), channel_id=1, source_target_pairs={{0,64},{64,128},{128,192},{192,256},{256,320},{320,384},{384,448},... | collective-permute-start | bytes 393224 | tf_op jit(solution)/shard_map/ppermute | solution.py:20
  8.3 16.9 %copy-start.2 = (f32[1,1,512,512]{3,2,1,0:T(8,128)S(1)}, f32[1,1,512,512]{3,2,1,0:T(8,128)}, u32[]{:S(2)}) copy-start(f32[1,1,512,512]{3,2,1,0:T(8,128)} %param.4) | copy-start | bytes 3145732
  13.9 5.6 %collective-permute-start.2 = (f32[64,512]{1,0:T(8,128)S(1)}, f32[64,512]{1,0:T(8,128)S(1)}, u32[]{:S(2)}, u32[]{:S(2)}) collective-permute-start(f32[64,512]{1,0:T(8,128)S(1)} %get-tuple-element.19), channel_id=1, source_target_pairs={{0,64},{64,128},{128,192},{192,256},{256,320},{320,384},{384,448},... | collective-permute-start | bytes 393224 | tf_op jit(solution)/shard_map/ppermute | solution.py:20
  14.0 5.6 %collective-permute-start.5 = (f32[64,512]{1,0:T(8,128)S(1)}, f32[64,512]{1,0:T(8,128)S(1)}, u32[]{:S(2)}, u32[]{:S(2)}) collective-permute-start(f32[64,512]{1,0:T(8,128)S(1)} %get-tuple-element.20), channel_id=1, source_target_pairs={{0,448},{64,0},{128,64},{192,128},{256,192},{320,256},{384,320},{4... | collective-permute-start | bytes 393224 | tf_op jit(solution)/shard_map/ppermute | solution.py:20
  19.6 5.6 %collective-permute-start.3 = (f32[64,512]{1,0:T(8,128)S(1)}, f32[64,512]{1,0:T(8,128)S(1)}, u32[]{:S(2)}, u32[]{:S(2)}) collective-permute-start(f32[64,512]{1,0:T(8,128)S(1)} %get-tuple-element.17), channel_id=1, source_target_pairs={{0,64},{64,128},{128,192},{192,256},{256,320},{320,384},{384,448},... | collective-permute-start | bytes 393224 | tf_op jit(solution)/shard_map/ppermute | solution.py:20
  19.6 5.6 %collective-permute-start.6 = (f32[64,512]{1,0:T(8,128)S(1)}, f32[64,512]{1,0:T(8,128)S(1)}, u32[]{:S(2)}, u32[]{:S(2)}) collective-permute-start(f32[64,512]{1,0:T(8,128)S(1)} %get-tuple-element.18), channel_id=1, source_target_pairs={{0,448},{64,0},{128,64},{192,128},{256,192},{320,256},{384,320},{4... | collective-permute-start | bytes 393224 | tf_op jit(solution)/shard_map/ppermute | solution.py:20
  25.3 12.5 %copy-start = (f32[64,512]{1,0:T(8,128)}, f32[64,512]{1,0:T(8,128)S(1)}, u32[]{:S(2)}) copy-start(f32[64,512]{1,0:T(8,128)S(1)} %fusion.band_ref) | copy-start | bytes 393220
  26.0 11.8 %collective-permute-start.12 = (f32[64,512]{1,0:T(8,128)S(1)}, f32[64,512]{1,0:T(8,128)S(1)}, u32[]{:S(2)}, u32[]{:S(2)}) collective-permute-start(f32[64,512]{1,0:T(8,128)S(1)} %get-tuple-element.15), channel_id=1, source_target_pairs={{0,64},{64,128},{128,192},{192,256},{256,320},{320,384},{384,448},... | collective-permute-start | bytes 393224 | tf_op jit(solution)/shard_map/ppermute | solution.py:20
  26.0 13.4 %collective-permute-start.16 = (f32[64,512]{1,0:T(8,128)S(1)}, f32[64,512]{1,0:T(8,128)S(1)}, u32[]{:S(2)}, u32[]{:S(2)}) collective-permute-start(f32[64,512]{1,0:T(8,128)S(1)} %get-tuple-element.14), channel_id=1, source_target_pairs={{0,448},{64,0},{128,64},{192,128},{256,192},{320,256},{384,320},{4... | collective-permute-start | bytes 393224 | tf_op jit(solution)/shard_map/ppermute | solution.py:20
  29.0 8.9 %collective-permute-start.7 = (f32[16,512]{1,0:T(8,128)S(1)}, f32[16,512]{1,0:T(8,128)S(1)}, u32[]{:S(2)}, u32[]{:S(2)}) collective-permute-start(f32[16,512]{1,0:T(8,128)S(1)} %get-tuple-element.26), channel_id=1, source_target_pairs={{448,8},{8,448},{449,9},{9,449},{450,10},{10,450},{451,11},{11,451... | collective-permute-start | bytes 98312 | tf_op jit(solution)/shard_map/ppermute | solution.py:51
  30.9 8.5 %collective-permute-start.8 = (f32[16,512]{1,0:T(8,128)S(1)}, f32[16,512]{1,0:T(8,128)S(1)}, u32[]{:S(2)}, u32[]{:S(2)}) collective-permute-start(f32[16,512]{1,0:T(8,128)S(1)} %get-tuple-element.27), channel_id=1, source_target_pairs={{0,64},{64,128},{128,192},{192,256},{256,320},{320,384},{384,448},... | collective-permute-start | bytes 98312 | tf_op jit(solution)/shard_map/ppermute | solution.py:20
  30.9 8.5 %collective-permute-start.9 = (f32[16,512]{1,0:T(8,128)S(1)}, f32[16,512]{1,0:T(8,128)S(1)}, u32[]{:S(2)}, u32[]{:S(2)}) collective-permute-start(f32[16,512]{1,0:T(8,128)S(1)} %get-tuple-element.25), channel_id=1, source_target_pairs={{0,448},{64,0},{128,64},{192,128},{256,192},{320,256},{384,320},{4... | collective-permute-start | bytes 98312 | tf_op jit(solution)/shard_map/ppermute | solution.py:20
  37.8 5.6 %collective-permute-start.13 = (f32[64,512]{1,0:T(8,128)S(1)}, f32[64,512]{1,0:T(8,128)S(1)}, u32[]{:S(2)}, u32[]{:S(2)}) collective-permute-start(f32[64,512]{1,0:T(8,128)S(1)} %bitcast_add_fusion.4), channel_id=1, source_target_pairs={{0,64},{64,128},{128,192},{192,256},{256,320},{320,384},{384,448},... | collective-permute-start | bytes 393224 | tf_op jit(solution)/shard_map/ppermute | solution.py:20
  39.4 7.1 %copy-start.3 = (f32[16,512]{1,0:T(8,128)}, f32[16,512]{1,0:T(8,128)S(1)}, u32[]{:S(2)}) copy-start(f32[16,512]{1,0:T(8,128)S(1)} %get-tuple-element.32.below_ref) | copy-start | bytes 98308
  39.4 7.1 %copy-start.4 = (f32[16,512]{1,0:T(8,128)}, f32[16,512]{1,0:T(8,128)S(1)}, u32[]{:S(2)}) copy-start(f32[16,512]{1,0:T(8,128)S(1)} %get-tuple-element.33.above_ref) | copy-start | bytes 98308
  43.5 7.2 %collective-permute-start.14 = (f32[64,512]{1,0:T(8,128)S(1)}, f32[64,512]{1,0:T(8,128)S(1)}, u32[]{:S(2)}, u32[]{:S(2)}) collective-permute-start(f32[64,512]{1,0:T(8,128)S(1)} %get-tuple-element.13), channel_id=1, source_target_pairs={{0,64},{64,128},{128,192},{192,256},{256,320},{320,384},{384,448},... | collective-permute-start | bytes 393224 | tf_op jit(solution)/shard_map/ppermute | solution.py:20
  43.5 7.2 %collective-permute-start.17 = (f32[64,512]{1,0:T(8,128)S(1)}, f32[64,512]{1,0:T(8,128)S(1)}, u32[]{:S(2)}, u32[]{:S(2)}) collective-permute-start(f32[64,512]{1,0:T(8,128)S(1)} %get-tuple-element.12), channel_id=1, source_target_pairs={{0,448},{64,0},{128,64},{192,128},{256,192},{320,256},{384,320},{4... | collective-permute-start | bytes 393224 | tf_op jit(solution)/shard_map/ppermute | solution.py:20
  46.5 9.8 %collective-permute-start.11 = (f32[96,128]{1,0:T(8,128)S(1)}, f32[96,128]{1,0:T(8,128)S(1)}, u32[]{:S(2)}, u32[]{:S(2)}) collective-permute-start(f32[96,128]{1,0:T(8,128)S(1)} %pad_maximum_fusion.1), channel_id=1, source_target_pairs={{1,0},{2,1},{3,2},{4,3},{5,4},{6,5},{7,6},{9,8},{10,9},{11,10},{12... | collective-permute-start | bytes 147464 | tf_op jit(solution)/shard_map/ppermute | solution.py:59
  50.8 11.1 %collective-permute-start.15 = (f32[64,512]{1,0:T(8,128)S(1)}, f32[64,512]{1,0:T(8,128)S(1)}, u32[]{:S(2)}, u32[]{:S(2)}) collective-permute-start(f32[64,512]{1,0:T(8,128)S(1)} %get-tuple-element.11), channel_id=1, source_target_pairs={{0,64},{64,128},{128,192},{192,256},{256,320},{320,384},{384,448},... | collective-permute-start | bytes 393224 | tf_op jit(solution)/shard_map/ppermute | solution.py:20
  50.8 11.0 %collective-permute-start.18 = (f32[64,512]{1,0:T(8,128)S(1)}, f32[64,512]{1,0:T(8,128)S(1)}, u32[]{:S(2)}, u32[]{:S(2)}) collective-permute-start(f32[64,512]{1,0:T(8,128)S(1)} %get-tuple-element.10), channel_id=1, source_target_pairs={{0,448},{64,0},{128,64},{192,128},{256,192},{320,256},{384,320},{4... | collective-permute-start | bytes 393224 | tf_op jit(solution)/shard_map/ppermute | solution.py:20
  53.7 8.1 %collective-permute-start.10 = (f32[96,128]{1,0:T(8,128)S(1)}, f32[96,128]{1,0:T(8,128)S(1)}, u32[]{:S(2)}, u32[]{:S(2)}) collective-permute-start(f32[96,128]{1,0:T(8,128)S(1)} %pad_maximum_fusion), channel_id=1, source_target_pairs={{0,1},{1,2},{2,3},{3,4},{4,5},{5,6},{6,7},{8,9},{9,10},{10,11},{11... | collective-permute-start | bytes 147464 | tf_op jit(solution)/shard_map/ppermute | solution.py:59
  56.3 5.6 %copy-start.7 = (f32[96,128]{1,0:T(8,128)}, f32[96,128]{1,0:T(8,128)S(1)}, u32[]{:S(2)}) copy-start(f32[96,128]{1,0:T(8,128)S(1)} %collective-permute-done.11.right_ref) | copy-start | bytes 147460
  61.8 0.6 copy-start.8
  61.8 0.7 copy-start.5
  61.8 0.7 %copy-start.6 = (f32[64,512]{1,0:T(8,128)}, f32[64,512]{1,0:T(8,128)S(1)}, u32[]{:S(2)}) copy-start(f32[64,512]{1,0:T(8,128)S(1)} %collective-permute-done.18.thick_c_ref) | copy-start | bytes 393220

commit v2 on v1

--- a/solution.py
+++ b/solution.py
@@ -13,64 +13,105 @@
 
 PAD = 16
 LANES = 128
-
-
-def ring(value, step):
-    count = lax.axis_size("slab")
-    return lax.ppermute(value, "slab", [(i, (i + step) % count) for i in range(count)])
-
-
-def reduce_bands(bands, combine, index):
-    count = bands.shape[0]
-
-    def share(offset):
-        return lax.dynamic_index_in_dim(bands, (index + offset + count) % count, 0, keepdims=False)
-
-    ahead = count // 2
-    behind = count - 1 - ahead
-    forward = share(ahead)
-    backward = share(-behind)
-    for distance in range(ahead, 0, -1):
-        forward = ring(forward, 1)
-        if distance > 1:
-            forward = combine(forward, share(distance - 1))
-        if distance <= behind:
-            backward = ring(backward, -1)
-            if distance > 1:
-                backward = combine(backward, share(1 - distance))
-    return share(0), forward, backward
-
-
-def tile_edges(value, grid, slabs):
+PARAMS = pltpu.CompilerParams(vmem_limit_bytes=16 * 1024 * 1024)
+
+
+def pick_kernel(flip, depth_ref, thick_ref, out_ref, sems):
+    parity = (lax.axis_index("slab") + flip) % 2
+    copies = [
+        pltpu.make_async_copy(ref.at[:, parity], out_ref.at[k], sems.at[k])
+        for k, ref in enumerate((depth_ref, thick_ref))
+    ]
+    for copy in copies:
+        copy.start()
+    for copy in copies:
+        copy.wait()
+
+
+def pair_cores(depth, thick):
+    bands, rows, width = depth.shape
+    shape = (bands // 2, 2, rows, width)
+
+    layers = [
+        pltpu.with_memory_space_constraint(a.reshape(shape), pltpu.HBM) for a in (depth, thick)
+    ]
+
+    def pick(flip):
+        return pl.pallas_call(
+            functools.partial(pick_kernel, flip),
+            compiler_params=PARAMS,
+            out_shape=pltpu.VMEM((2, bands // 2, rows, width), jnp.float32),
+            in_specs=[pl.BlockSpec(memory_space=pltpu.HBM)] * 2,
+            out_specs=pl.BlockSpec(memory_space=pltpu.VMEM),
+            scratch_shapes=[pltpu.SemaphoreType.DMA((2,))],
+        )(*layers)
+
+    own = pick(0)
+    got = lax.ppermute(pick(1), "slab", [(i, i ^ 1) for i in range(bands)])
+    return jnp.minimum(own[0], got[0]), own[1] + got[1]
+
+
+def to_owners(value):
+    slabs = lax.axis_size("slab")
+    groups = [list(range(parity, slabs, 2)) for parity in range(2)]
+    return lax.all_to_all(
+        value, "slab", split_axis=0, concat_axis=0, axis_index_groups=groups, tiled=True
+    )
+
+
+def to_owners_by_swaps(value, slab):
+    slabs = lax.axis_size("slab")
+    chips = slabs // 2
+    chip = slab // 2
+
+    def share(index):
+        return lax.dynamic_index_in_dim(value, index, 0, keepdims=False)
+
+    total = share(chip)
+    for step in range(1, chips):
+        route = [(i, (i // 2 ^ step) * 2 + i % 2) for i in range(slabs)]
+        total = total + lax.ppermute(share(chip ^ step), "slab", route)
+    return total
+
+
+def neighbour_rows(band, grid, slabs, core):
     tiles = grid * grid
-    route = []
-    for t in range(tiles - grid):
-        upper = (slabs - 1) * tiles + t
-        lower = t + grid
-        route += [(upper, lower), (lower, upper)]
-    return lax.ppermute(value, ("slab", "tile"), route)
-
-
-def to_column(value, grid, step):
-    route = []
+    across = []
+    for t in range(tiles):
+        for s in range(1, slabs, 2):
+            upper = s * tiles + t
+            lower = (s + 1) * tiles + t if s + 1 < slabs else t + grid
+            if s + 1 < slabs or t + grid < tiles:
+                across += [(upper, lower), (lower, upper)]
+    odd = core == 1
+    head, tail = band[:PAD], band[-PAD:]
+    far = lax.ppermute(jnp.where(odd, tail, head), ("slab", "tile"), across)
+    near = lax.ppermute(jnp.where(odd, head, tail), "slab", [(i, i ^ 1) for i in range(slabs)])
+    return far, near
+
+
+def neighbour_columns(first, last, grid, column):
+    odd = column % 2 == 1
+    near, far = [], []
     for t in range(grid * grid):
-        if 0 <= t % grid + step < grid:
-            route.append((t, t + step))
-    return lax.ppermute(value, "tile", route)
+        if t % grid + 1 < grid:
+            (near if t % 2 == 0 else far).extend([(t, t + 1), (t + 1, t)])
+    far = lax.ppermute(jnp.where(odd, last, first), "tile", far)
+    near = lax.ppermute(jnp.where(odd, first, last), "tile", near)
+    return jnp.where(odd, near, far), jnp.where(odd, far, near)
 
 
 def flow_kernel(
     rows,
     width,
-    edge_ref,
+    grid,
+    slabs,
     above_ref,
     band_ref,
     below_ref,
     left_ref,
     right_ref,
-    thick_a_ref,
-    thick_b_ref,
-    thick_c_ref,
+    parts_ref,
     cover_ref,
     smooth_ref,
     shade_ref,
@@ -82,6 +123,11 @@
     total = rows + 2 * PAD
     top = PAD
     bottom = PAD + rows
+    slab, tile = lax.axis_index("slab"), lax.axis_index("tile")
+    top_edge = (slab == 0) & (tile < grid)
+    bottom_edge = (slab == slabs - 1) & (tile >= grid * (grid - 1))
+    left_edge = lax.rem(tile, grid) == 0
+    right_edge = lax.rem(tile, grid) == grid - 1
     lane = lax.broadcasted_iota(jnp.int32, (8, LANES), 1)
 
     for j in range(blocks):
@@ -95,19 +141,19 @@
         )
 
     def refill():
-        @pl.when(edge_ref[0] == 1)
+        @pl.when(top_edge)
         def _():
             for j in range(blocks + 1):
                 surface[j, top - 2 : top, :] = jnp.broadcast_to(surface[j, top : top + 1, :], (2, LANES))
 
-        @pl.when(edge_ref[1] == 1)
+        @pl.when(bottom_edge)
         def _():
             for j in range(blocks + 1):
                 surface[j, bottom : bottom + 2, :] = jnp.broadcast_to(
                     surface[j, bottom - 1 : bottom, :], (2, LANES)
                 )
 
-        @pl.when(edge_ref[2] == 1)
+        @pl.when(left_edge)
         def _():
             for r in range(8, total - 8, 8):
                 first = jnp.broadcast_to(surface[0, r : r + 8, 0:1], (8, LANES))
@@ -115,7 +161,7 @@
                     lane >= LANES // 2, first, surface[blocks, r : r + 8, :]
                 )
 
-        @pl.when(edge_ref[3] == 1)
+        @pl.when(right_edge)
         def _():
             for r in range(8, total - 8, 8):
                 last = jnp.broadcast_to(
@@ -171,9 +217,8 @@
             gloss = jnp.maximum((0.9487 - 0.1897 * x - 0.253 * y) * inverse, 0.0)
             for _ in range(4):
                 gloss = gloss * gloss
-            thick = (
-                thick_a_ref[r : r + 8, cols] + thick_b_ref[r : r + 8, cols] + thick_c_ref[r : r + 8, cols]
-            )
+            layers = [parts_ref[k, r : r + 8, cols] for k in range(parts_ref.shape[0])]
+            thick = functools.reduce(jnp.add, layers)
             fluid = cover_ref[r : r + 8, cols].astype(jnp.float32)
             lit = 0.15 + 0.7 * jnp.exp(-0.8 * thick) * diffuse + 0.4 * gloss
             smooth_ref[r : r + 8, cols] = here[j]
@@ -187,47 +232,38 @@
     tile = lax.axis_index("tile")
     _, _, height, width = depth_layers.shape
     rows = height // slabs
-    first, last = slab == 0, slab == slabs - 1
-    edges = jnp.stack(
-        [
-            first & (tile // grid == 0),
-            last & (tile // grid == grid - 1),
-            tile % grid == 0,
-            tile % grid == grid - 1,
-        ]
-    ).astype(jnp.int32)
-
-    parts = reduce_bands(depth_layers.reshape(slabs, rows, width), jnp.minimum, slab)
-    band = jnp.minimum(jnp.minimum(parts[0], parts[1]), parts[2])
-
-    head, tail = band[:PAD], band[-PAD:]
-    above = ring(tail, 1)
-    below = ring(head, -1)
-    beyond = tile_edges(jnp.where(first, head, tail), grid, slabs)
-    above = jnp.where(first, beyond, above)
-    below = jnp.where(last, beyond, below)
-
-    def column(start):
-        cut = slice(start, start + LANES)
-        return jnp.concatenate([above[:, cut], band[:, cut], below[:, cut]], axis=0)
-
-    left = to_column(column(width - LANES), grid, 1)
-    right = to_column(column(0), grid, -1)
-
-    thickness_layers, band = lax.optimization_barrier((thickness_layers, band))
-    thick = reduce_bands(thickness_layers.reshape(slabs, rows, width), jnp.add, slab)
+    core = slab % 2
+
+    depth, thick = pair_cores(
+        depth_layers.reshape(slabs, rows, width), thickness_layers.reshape(slabs, rows, width)
+    )
+    parts = to_owners(depth)
+    thick = to_owners_by_swaps(thick, slab)[None]
+    band = jnp.min(parts, axis=0)
+    far, near = neighbour_rows(band, grid, slabs, core)
+    odd = core == 1
+    above, below = jnp.where(odd, near, far), jnp.where(odd, far, near)
+    tall = [
+        jnp.concatenate([a[:, cut] for a in (above, band, below)], axis=0)
+        for cut in (slice(0, LANES), slice(width - LANES, width))
+    ]
+    left, right = neighbour_columns(*tall, grid, tile % grid)
 
     vmem = pl.BlockSpec(memory_space=pltpu.VMEM)
     total = rows + 2 * PAD
     blocks = width // LANES + 1
     out = jax.ShapeDtypeStruct((rows, width), jnp.float32)
+    operands = [
+        pltpu.with_memory_space_constraint(a, pltpu.VMEM) for a in (above, band, below, left, right, thick)
+    ]
     smooth, shade = pl.pallas_call(
-        functools.partial(flow_kernel, rows, width),
+        functools.partial(flow_kernel, rows, width, grid, slabs),
+        compiler_params=PARAMS,
         out_shape=(out, out),
-        in_specs=[pl.BlockSpec(memory_space=pltpu.SMEM)] + [vmem] * 9,
+        in_specs=[vmem] * 7,
         out_specs=(vmem, vmem),
         scratch_shapes=[pltpu.VMEM((blocks, total, LANES), jnp.float32)] * 3,
-    )(edges, above, band, below, left, right, *thick, coverage[0])
+    )(*operands, coverage[0])
     return (smooth[None], shade[None])
 
 

time: 67.1 us -> 48 us (0.72)
  the two profiles are of different devices: /device:TPU:96 before, /device:TPU:416 now
where the time goes in v2:
time: 48 us; the launch traced here: 47.6 us
  starting transfers between devices  28.7 us (60%)
  waiting for transfers between devices  11.4 us (24%)
  Pallas kernels  5.53 us (12%)
  other arithmetic  1.16 us (2%)
  between operations  0.81 us (2%)
    ppermute x3, starting transfers between devices, to_owners_by_swaps(): total = total + lax.ppermute(share(chip ^ step), 'slab', route)  9.83 us
    ppermute x1, starting transfers between devices, neighbour_columns(): far = lax.ppermute(jnp.where(odd, last, first), 'tile', far)  5.11 us
    all_to_all x1, starting transfers between devices, to_owners(): lax.all_to_all(value, 'slab', split_axis=0, concat_axis=0, axis_index_gro...  4.46 us
    ppermute x1, waiting for transfers between devices, neighbour_rows(): far = lax.ppermute(jnp.where(odd, tail, head), ('slab', 'tile'), across)  3.99 us
    ppermute x1, starting transfers between devices, neighbour_rows(): far = lax.ppermute(jnp.where(odd, tail, head), ('slab', 'tile'), across)  3.51 us
    pallas_call x1, Pallas kernels, local(): pl.pallas_call(functools.partial(flow_kernel, rows, width, grid, slabs),...  3.07 us
    ppermute x1, waiting for transfers between devices, neighbour_columns(): near = lax.ppermute(jnp.where(odd, first, last), 'tile', near)  3.01 us
    pallas_call x2, Pallas kernels, pick(): pl.pallas_call(functools.partial(pick_kernel, flip), compiler_params=PARA...  2.46 us
  transfers between devices with their start and end apart: 9, of which 5 were waited for; matrix products, arithmetic and copies ran while one was open for 0% of the time, Pallas kernels for 3%

profile of v2, /device:TPU:416, one launch (start us, length us, event | category | flops | bytes accessed | tf_op | source)
XLA Modules:
  0.0 47.6 jit_solution(9862317568030321432)
XLA Ops:
  0.6 1.2 %shard_map.51 = f32[2,4,64,512]{3,2,1,0:T(8,128)S(1)} custom-call(f32[4,2,64,512]{3,2,1,0:T(8,128)} %bitcast.24, f32[4,2,64,512]{3,2,1,0:T(8,128)} %bitcast.26), custom_call_target="tpu_custom_call" | custom-call | tf_op jit(solution)/shard_map/pallas_call | solution.py:40
  1.9 1.9 %collective-permute-start = (f32[2,4,64,512]{3,2,1,0:T(8,128)S(1)}, f32[2,4,64,512]{3,2,1,0:T(8,128)S(1)}, u32[]{:S(2)}, u32[]{:S(2)}) collective-permute-start(f32[2,4,64,512]{3,2,1,0:T(8,128)S(1)} %shard_map.51), channel_id=1, source_target_pairs={{0,64},{64,0},{128,192},{192,128},{256,320},{320,256},{384,448},{4... | collective-permute-start | bytes 3145736 | tf_op jit(solution)/shard_map/ppermute | solution.py:50
  3.8 1.2 %shard_map.50 = f32[2,4,64,512]{3,2,1,0:T(8,128)S(1)} custom-call(f32[4,2,64,512]{3,2,1,0:T(8,128)} %bitcast.25, f32[4,2,64,512]{3,2,1,0:T(8,128)} %bitcast.27), custom_call_target="tpu_custom_call" | custom-call | tf_op jit(solution)/shard_map/pallas_call | solution.py:40
  5.0 1.4 %collective-permute-done = f32[2,4,64,512]{3,2,1,0:T(8,128)S(1)} collective-permute-done((f32[2,4,64,512]{3,2,1,0:T(8,128)S(1)}, f32[2,4,64,512]{3,2,1,0:T(8,128)S(1)}, u32[]{:S(2)}, u32[]{:S(2)}) %collective-permute-start) | collective-permute-done | bytes 1048608 | tf_op jit(solution)/shard_map/ppermute | solution.py:50
  6.4 1.0 %slice_add_fusion = (f32[1,4,64,512]{3,2,1,0:T(8,128)S(1)}, f32[4,64,512]{2,1,0:T(8,128)}) fusion(f32[2,4,64,512]{3,2,1,0:T(8,128)S(1)} %collective-permute-done, f32[2,4,64,512]{3,2,1,0:T(8,128)S(1)} %shard_map.50), kind=kLoop, calls=%fused_computation | loop fusion | flops 262144 | bytes 3145728 | tf_op jit(solution)/shard_map/add | solution.py:51
  7.5 4.5 %all-to-all-start = ((f32[4,64,512]{2,1,0:T(8,128)}), f32[4,64,512]{2,1,0:T(8,128)S(1)}, u32[]{:S(2)}, u32[]{:S(2)}) async-start(f32[4,64,512]{2,1,0:T(8,128)} %get-tuple-element.7), calls=%async_computation | async-start | bytes 1048576 | tf_op jit(solution)/shard_map/all_to_all | solution.py:57
  12.0 5.1 %collective-permute-start.7 = (f32[64,512]{1,0:T(8,128)S(1)}, f32[64,512]{1,0:T(8,128)S(1)}, u32[]{:S(2)}, u32[]{:S(2)}) collective-permute-start(f32[64,512]{1,0:T(8,128)S(1)} %get-tuple-element.9), channel_id=1, source_target_pairs={{0,384},{64,448},{128,256},{192,320},{256,128},{320,192},{384,0},{... | collective-permute-start | bytes 393224 | tf_op jit(solution)/shard_map/ppermute | solution.py:73
  17.1 2.8 %collective-permute-start.6 = (f32[64,512]{1,0:T(8,128)S(1)}, f32[64,512]{1,0:T(8,128)S(1)}, u32[]{:S(2)}, u32[]{:S(2)}) collective-permute-start(f32[64,512]{1,0:T(8,128)S(1)} %get-tuple-element.10), channel_id=1, source_target_pairs={{0,256},{64,320},{128,384},{192,448},{256,0},{320,64},{384,128},{4... | collective-permute-start | bytes 393224 | tf_op jit(solution)/shard_map/ppermute | solution.py:73
  19.9 1.9 %collective-permute-start.5 = (f32[64,512]{1,0:T(8,128)S(1)}, f32[64,512]{1,0:T(8,128)S(1)}, u32[]{:S(2)}, u32[]{:S(2)}) collective-permute-start(f32[64,512]{1,0:T(8,128)S(1)} %get-tuple-element.8), channel_id=1, source_target_pairs={{0,128},{64,192},{128,0},{192,64},{256,384},{320,448},{384,256},{4... | collective-permute-start | bytes 393224 | tf_op jit(solution)/shard_map/ppermute | solution.py:73
  21.8 2.1 %all-to-all-done = f32[4,64,512]{2,1,0:T(8,128)S(1)} async-done(((f32[4,64,512]{2,1,0:T(8,128)}), f32[4,64,512]{2,1,0:T(8,128)S(1)}, u32[]{:S(2)}, u32[]{:S(2)}) %all-to-all-start) | async-done | bytes 524320 | tf_op jit(solution)/shard_map/all_to_all | solution.py:57
  23.9 3.5 %collective-permute-start.2 = (f32[16,512]{1,0:T(8,128)S(1)}, f32[16,512]{1,0:T(8,128)S(1)}, u32[]{:S(2)}, u32[]{:S(2)}) collective-permute-start(f32[16,512]{1,0:T(8,128)S(1)} %get-tuple-element.13), channel_id=1, source_target_pairs={{64,128},{128,64},{192,256},{256,192},{320,384},{384,320},{448,8},... | collective-permute-start | bytes 98312 | tf_op jit(solution)/shard_map/ppermute | solution.py:88
  27.5 1.9 %collective-permute-start.1 = (f32[16,512]{1,0:T(8,128)S(1)}, f32[16,512]{1,0:T(8,128)S(1)}, u32[]{:S(2)}, u32[]{:S(2)}) collective-permute-start(f32[16,512]{1,0:T(8,128)S(1)} %get-tuple-element.14), channel_id=1, source_target_pairs={{0,64},{64,0},{128,192},{192,128},{256,320},{320,256},{384,448},{4... | collective-permute-start | bytes 98312 | tf_op jit(solution)/shard_map/ppermute | solution.py:89
  29.4 4.0 %collective-permute-done.2 = f32[16,512]{1,0:T(8,128)S(1)} collective-permute-done((f32[16,512]{1,0:T(8,128)S(1)}, f32[16,512]{1,0:T(8,128)S(1)}, u32[]{:S(2)}, u32[]{:S(2)}) %collective-permute-start.2) | collective-permute-done | bytes 32800 | tf_op jit(solution)/shard_map/ppermute | solution.py:88
  33.4 0.0 collective-permute-done.1
  33.5 5.1 %collective-permute-start.4 = (f32[96,128]{1,0:T(8,128)S(1)}, f32[96,128]{1,0:T(8,128)S(1)}, u32[]{:S(2)}, u32[]{:S(2)}) collective-permute-start(f32[96,128]{1,0:T(8,128)S(1)} %get-tuple-element.17), channel_id=1, source_target_pairs={{1,2},{2,1},{3,4},{4,3},{5,6},{6,5},{9,10},{10,9},{11,12},{12,11},... | collective-permute-start | bytes 147464 | tf_op jit(solution)/shard_map/ppermute | solution.py:99
  38.6 1.9 %collective-permute-start.3 = (f32[96,128]{1,0:T(8,128)S(1)}, f32[96,128]{1,0:T(8,128)S(1)}, u32[]{:S(2)}, u32[]{:S(2)}) collective-permute-start(f32[96,128]{1,0:T(8,128)S(1)} %get-tuple-element.18), channel_id=1, source_target_pairs={{0,1},{1,0},{2,3},{3,2},{4,5},{5,4},{6,7},{7,6},{8,9},{9,8},{10,11... | collective-permute-start | bytes 147464 | tf_op jit(solution)/shard_map/ppermute | solution.py:100
  40.5 0.0 collective-permute-done.7
  40.5 0.0 collective-permute-done.6
  40.5 0.0 collective-permute-done.5
  40.6 0.0 copy-start
  40.6 1.0 %collective-permute-done.4 = f32[96,128]{1,0:T(8,128)S(1)} collective-permute-done((f32[96,128]{1,0:T(8,128)S(1)}, f32[96,128]{1,0:T(8,128)S(1)}, u32[]{:S(2)}, u32[]{:S(2)}) %collective-permute-start.4) | collective-permute-done | bytes 49184 | tf_op jit(solution)/shard_map/ppermute | solution.py:99
  41.5 3.0 %collective-permute-done.3 = f32[96,128]{1,0:T(8,128)S(1)} collective-permute-done((f32[96,128]{1,0:T(8,128)S(1)}, f32[96,128]{1,0:T(8,128)S(1)}, u32[]{:S(2)}, u32[]{:S(2)}) %collective-permute-start.3) | collective-permute-done | bytes 49184 | tf_op jit(solution)/shard_map/ppermute | solution.py:100
  44.6 0.0 copy-done
  44.6 3.1 %shard_map.52 = (f32[64,512]{1,0:T(8,128)}, f32[64,512]{1,0:T(8,128)}) custom-call(f32[16,512]{1,0:T(8,128)S(1)} %get-tuple-element.20.above_ref, f32[64,512]{1,0:T(8,128)S(1)} %reduce_min.9.band_ref, f32[16,512]{1,0:T(8,128)S(1)} %get-tuple-element.19.below_ref, f32[96,128]{1,0:T(8,128)S(1)} %get-tuple-element.16.left_ref, ...), custom_call_target="tpu_custom_call" | custom-call | tf_op jit(solution)/shard_map/pallas_call | solution.py:259
  (9 shorter events, 0.2 us)
Async XLA Ops:
  1.9 4.6 %collective-permute-start = (f32[2,4,64,512]{3,2,1,0:T(8,128)S(1)}, f32[2,4,64,512]{3,2,1,0:T(8,128)S(1)}, u32[]{:S(2)}, u32[]{:S(2)}) collective-permute-start(f32[2,4,64,512]{3,2,1,0:T(8,128)S(1)} %shard_map.51), channel_id=1, source_target_pairs={{0,64},{64,0},{128,192},{192,128},{256,320},{320,256},{384,448},{4... | collective-permute-start | bytes 3145736 | tf_op jit(solution)/shard_map/ppermute | solution.py:50
  7.5 16.4 %all-to-all-start = ((f32[4,64,512]{2,1,0:T(8,128)}), f32[4,64,512]{2,1,0:T(8,128)S(1)}, u32[]{:S(2)}, u32[]{:S(2)}) async-start(f32[4,64,512]{2,1,0:T(8,128)} %get-tuple-element.7), calls=%async_computation | async-start | bytes 1048576 | tf_op jit(solution)/shard_map/all_to_all | solution.py:57
  12.0 28.5 %collective-permute-start.7 = (f32[64,512]{1,0:T(8,128)S(1)}, f32[64,512]{1,0:T(8,128)S(1)}, u32[]{:S(2)}, u32[]{:S(2)}) collective-permute-start(f32[64,512]{1,0:T(8,128)S(1)} %get-tuple-element.9), channel_id=1, source_target_pairs={{0,384},{64,448},{128,256},{192,320},{256,128},{320,192},{384,0},{... | collective-permute-start | bytes 393224 | tf_op jit(solution)/shard_map/ppermute | solution.py:73
  17.1 23.4 %collective-permute-start.6 = (f32[64,512]{1,0:T(8,128)S(1)}, f32[64,512]{1,0:T(8,128)S(1)}, u32[]{:S(2)}, u32[]{:S(2)}) collective-permute-start(f32[64,512]{1,0:T(8,128)S(1)} %get-tuple-element.10), channel_id=1, source_target_pairs={{0,256},{64,320},{128,384},{192,448},{256,0},{320,64},{384,128},{4... | collective-permute-start | bytes 393224 | tf_op jit(solution)/shard_map/ppermute | solution.py:73
  19.9 20.6 %collective-permute-start.5 = (f32[64,512]{1,0:T(8,128)S(1)}, f32[64,512]{1,0:T(8,128)S(1)}, u32[]{:S(2)}, u32[]{:S(2)}) collective-permute-start(f32[64,512]{1,0:T(8,128)S(1)} %get-tuple-element.8), channel_id=1, source_target_pairs={{0,128},{64,192},{128,0},{192,64},{256,384},{320,448},{384,256},{4... | collective-permute-start | bytes 393224 | tf_op jit(solution)/shard_map/ppermute | solution.py:73
  23.9 9.5 %collective-permute-start.2 = (f32[16,512]{1,0:T(8,128)S(1)}, f32[16,512]{1,0:T(8,128)S(1)}, u32[]{:S(2)}, u32[]{:S(2)}) collective-permute-start(f32[16,512]{1,0:T(8,128)S(1)} %get-tuple-element.13), channel_id=1, source_target_pairs={{64,128},{128,64},{192,256},{256,192},{320,384},{384,320},{448,8},... | collective-permute-start | bytes 98312 | tf_op jit(solution)/shard_map/ppermute | solution.py:88
  27.5 5.9 %collective-permute-start.1 = (f32[16,512]{1,0:T(8,128)S(1)}, f32[16,512]{1,0:T(8,128)S(1)}, u32[]{:S(2)}, u32[]{:S(2)}) collective-permute-start(f32[16,512]{1,0:T(8,128)S(1)} %get-tuple-element.14), channel_id=1, source_target_pairs={{0,64},{64,0},{128,192},{192,128},{256,320},{320,256},{384,448},{4... | collective-permute-start | bytes 98312 | tf_op jit(solution)/shard_map/ppermute | solution.py:89
  33.5 8.1 %collective-permute-start.4 = (f32[96,128]{1,0:T(8,128)S(1)}, f32[96,128]{1,0:T(8,128)S(1)}, u32[]{:S(2)}, u32[]{:S(2)}) collective-permute-start(f32[96,128]{1,0:T(8,128)S(1)} %get-tuple-element.17), channel_id=1, source_target_pairs={{1,2},{2,1},{3,4},{4,3},{5,6},{6,5},{9,10},{10,9},{11,12},{12,11},... | collective-permute-start | bytes 147464 | tf_op jit(solution)/shard_map/ppermute | solution.py:99
  38.6 6.0 %collective-permute-start.3 = (f32[96,128]{1,0:T(8,128)S(1)}, f32[96,128]{1,0:T(8,128)S(1)}, u32[]{:S(2)}, u32[]{:S(2)}) collective-permute-start(f32[96,128]{1,0:T(8,128)S(1)} %get-tuple-element.18), channel_id=1, source_target_pairs={{0,1},{1,0},{2,3},{3,2},{4,5},{5,4},{6,7},{7,6},{8,9},{9,8},{10,11... | collective-permute-start | bytes 147464 | tf_op jit(solution)/shard_map/ppermute | solution.py:100
  40.6 4.0 %copy-start = (s32[1,64,512]{2,1,0:T(8,128)S(1)}, s32[1,64,512]{2,1,0:T(8,128)}, u32[]{:S(2)}) copy-start(s32[1,64,512]{2,1,0:T(8,128)} %param.5) | copy-start | bytes 393220

commit v3 on v2

v3 whole, which is shorter than its diff:
```python
import functools
import math

import jax
import jax.numpy as jnp
from jax import lax
from jax.experimental import pallas as pl
from jax.experimental.pallas import tpu as pltpu
from jax.sharding import PartitionSpec as P

SWEEPS = 4
FLOW_STEP = 0.2

PAD = 16
LANES = 128
PARAMS = pltpu.CompilerParams(vmem_limit_bytes=16 * 1024 * 1024)


def pick_kernel(flip, value_ref, out_ref, sem):
    copy = pltpu.make_async_copy(
        value_ref.at[:, (lax.axis_index("slab") + flip) % 2], out_ref, sem
    )
    copy.start()
    copy.wait()


def pair_sum(value):
    bands, rows, width = value.shape
    value = value.reshape(bands // 2, 2, rows, width)
    value = pltpu.with_memory_space_constraint(value, pltpu.HBM)

    def pick(flip):
        return pl.pallas_call(
            functools.partial(pick_kernel, flip),
            compiler_params=PARAMS,
            out_shape=pltpu.VMEM((bands // 2, rows, width), jnp.float32),
            in_specs=[pl.BlockSpec(memory_space=pltpu.HBM)],
            out_specs=pl.BlockSpec(memory_space=pltpu.VMEM),
            scratch_shapes=[pltpu.SemaphoreType.DMA],
        )(value)

    own = pick(0)
    return own + lax.ppermute(pick(1), "slab", [(i, i ^ 1) for i in range(bands)])


def sum_by_swaps(value, slab):
    slabs = lax.axis_size("slab")
    chips = slabs // 2
    chip = slab // 2

    def share(index):
        return lax.dynamic_index_in_dim(value, index, 0, keepdims=False)

    total = share(chip)
    for step in range(1, chips):
        route = [(i, (i // 2 ^ step) * 2 + i % 2) for i in range(slabs)]
        total = total + lax.ppermute(share(chip ^ step), "slab", route)
    return total


def neighbour_rows(band, grid, slabs, core):
    tiles = grid * grid
    across = []
    for t in range(tiles):
        for s in range(1, slabs, 2):
            upper = s * tiles + t
            lower = (s + 1) * tiles + t if s + 1 < slabs else t + grid
            if s + 1 < slabs or t + grid < tiles:
                across += [(upper, lower), (lower, upper)]
    odd = core == 1
    head, tail = band[:PAD], band[-PAD:]
    long = jnp.where(odd, band[-PAD - 8 :], band[: PAD + 8])
    far = lax.ppermute(long, ("slab", "tile"), across)
    far = jnp.where(odd, far[:PAD], far[8:])
    near = lax.ppermute(jnp.where(odd, head, tail), "slab", [(i, i ^ 1) for i in range(slabs)])
    return far, near


def neighbour_columns(first, last, grid, column):
    odd = column % 2 == 1
    near, far = [], []
    for t in range(grid * grid):
        if t % grid + 1 < grid:
            (near if t % 2 == 0 else far).extend([(t, t + 1), (t + 1, t)])
    long = jnp.where(odd, last, first)
    long = jnp.concatenate([long, long[:8]], axis=0)
    far = lax.ppermute(long, "tile", far)[:-8]
    near = lax.ppermute(jnp.where(odd, first, last), "tile", near)
    return jnp.where(odd, near, far), jnp.where(odd, far, near)


def flow(rows, grid, pieces, last, first, groups, surface, partial, normal_y, finish):
    total = rows + 2 * PAD
    top, bottom = PAD, PAD + rows
    slabs = lax.axis_size("slab")
    slab, tile = lax.axis_index("slab"), lax.axis_index("tile")
    top_edge = (slab == 0) & (tile < grid)
    bottom_edge = (slab == slabs - 1) & (tile >= grid * (grid - 1))
    left_edge = lax.rem(tile, grid) == 0
    right_edge = lax.rem(tile, grid) == grid - 1
    lane = lax.broadcasted_iota(jnp.int32, (8, LANES), 1)
    first_row = lax.broadcasted_iota(jnp.int32, (8, LANES), 0) == 0
    last_row = lax.broadcasted_iota(jnp.int32, (8, LANES), 0) == 7
    first_lane, last_lane = lane == 0, lane == LANES - 1

    def across(values, left, right):
        after = [pltpu.roll(p, LANES - 1, 1) for p in values]
        before = [pltpu.roll(p, 1, 1) for p in values]
        out = []
        for j in range(pieces):
            beyond, behind = after[(j + 1) % pieces], before[(j - 1) % pieces]
            if j == first:
                behind = jnp.where(left_edge, left, behind)
            if j == last:
                beyond = jnp.where(right_edge, right, beyond)
            out.append(jnp.where(last_lane, beyond, after[j]) - jnp.where(first_lane, behind, before[j]))
        return out

    def slopes(r):
        here = [surface[j, pl.ds(r, 8), :] for j in range(pieces)]
        wide_x = across(here, here[first], here[last])
        at_top = first_row & (top_edge & (r == top))
        at_bottom = last_row & (bottom_edge & (r == bottom - 8))
        wide_y = []
        for j in range(pieces):
            over = jnp.where(at_top, here[j], surface[j, pl.ds(r - 1, 8), :])
            under = jnp.where(at_bottom, here[j], surface[j, pl.ds(r + 1, 8), :])
            wide_y.append(under - over)
        return here, wide_x, wide_y

    zero = jnp.zeros((8, LANES), jnp.float32)

    def bend(r):
        here, wide_x, wide_y = slopes(r)
        inverse = [lax.rsqrt(1.0 + 0.25 * (x * x + y * y)) for x, y in zip(wide_x, wide_y)]
        spread = across([x * w for x, w in zip(wide_x, inverse)], zero, zero)
        level = (top_edge & (r < top)) | (bottom_edge & (r >= bottom))
        for j in range(pieces):
            normal_y[j, pl.ds(r, 8), :] = jnp.where(level, 0.0, wide_y[j] * inverse[j])
            partial[j, pl.ds(r, 8), :] = here[j] + (0.25 * FLOW_STEP) * spread[j]

    def move(r):
        for j in range(pieces):
            surface[j, pl.ds(r, 8), :] = partial[j, pl.ds(r, 8), :] + (0.25 * FLOW_STEP) * (
                normal_y[j, pl.ds(r + 1, 8), :] - normal_y[j, pl.ds(r - 1, 8), :]
            )

    def each(start, count, group, act):
        def step(i, carry):
            for k in range(group):
                act(start + pl.multiple_of((i * group + k) * 8, 8))
            return carry

        lax.fori_loop(0, count // group, step, 0)

    def sweep(i, carry):
        each(8, total // 8 - 2, groups[0], bend)
        each(8, total // 8 - 2, groups[1], move)
        return carry

    lax.fori_loop(0, SWEEPS, sweep, 0)
    each(0, rows // 8, groups[2], lambda r: finish(r, *slopes(top + r)))


def shaded(wide_x, wide_y, layers, cover):
    x, y = 0.5 * wide_x, 0.5 * wide_y
    inverse = lax.rsqrt(1.0 + (x * x + y * y))
    diffuse = jnp.maximum((0.8 - 0.36 * x - 0.48 * y) * inverse, 0.0)
    gloss = jnp.maximum((0.9487 - 0.1897 * x - 0.253 * y) * inverse, 0.0)
    for _ in range(4):
        gloss = gloss * gloss
    fluid = cover.astype(jnp.float32)
    lit = 0.15 + 0.7 * jnp.exp(-0.8 * functools.reduce(jnp.add, layers)) * diffuse + 0.4 * gloss
    return fluid * lit + (1.0 - fluid) * 0.05


def inner_kernel(rows, grid, above_ref, band_ref, below_ref, thick_ref, cover_ref, smooth_ref, shade_ref, *scratch):
    surface = scratch[0]
    blocks = surface.shape[0]
    for j in range(blocks):
        cols = pl.ds(j * LANES, LANES)
        surface[j, 0:PAD, :] = above_ref[:, cols]
        surface[j, PAD : PAD + rows, :] = band_ref[:, cols]
        surface[j, PAD + rows :, :] = below_ref[:, cols]

    def finish(r, here, wide_x, wide_y):
        span = pl.ds(r, 8)
        for j in range(blocks):
            cols = pl.ds(j * LANES, LANES)
            smooth_ref[span, cols] = here[j]
            shade_ref[span, cols] = shaded(wide_x[j], wide_y[j], [thick_ref[span, cols]], cover_ref[span, cols])

    flow(rows, grid, blocks, blocks - 1, 0, (5, 10, 4), *scratch, finish)


def outer_kernel(
    rows,
    grid,
    above_ref,
    band_ref,
    below_ref,
    left_ref,
    right_ref,
    thick_ref,
    cover_ref,
    inner_smooth_ref,
    inner_shade_ref,
    smooth_ref,
    shade_ref,
    *scratch,
):
    surface = scratch[0]
    total = rows + 2 * PAD
    blocks = band_ref.shape[1] // LANES
    low = lax.broadcasted_iota(jnp.int32, (8, LANES), 1) < LANES // 2
    outer = ((0, blocks - 1), (2, 0))
    for j, block in outer:
        cols = pl.ds(block * LANES, LANES)
        surface[j, 0:PAD, :] = above_ref[:, cols]
        surface[j, PAD : PAD + rows, :] = band_ref[:, cols]
        surface[j, PAD + rows :, :] = below_ref[:, cols]
    for r in range(0, total, 8):
        surface[1, r : r + 8, :] = jnp.where(low, right_ref[r : r + 8, :], left_ref[r : r + 8, :])
    middle = pl.ds(LANES, (blocks - 2) * LANES)
    smooth_ref[:, middle] = inner_smooth_ref[:, middle]
    shade_ref[:, middle] = inner_shade_ref[:, middle]

    def finish(r, here, wide_x, wide_y):
        span = pl.ds(r, 8)
        for j, block in outer:
            cols = pl.ds(block * LANES, LANES)
            keep = low if j == 0 else jnp.logical_not(low)
            shade = shaded(wide_x[j], wide_y[j], [thick_ref[span, cols]], cover_ref[span, cols])
            smooth_ref[span, cols] = jnp.where(keep, inner_smooth_ref[span, cols], here[j])
            shade_ref[span, cols] = jnp.where(keep, inner_shade_ref[span, cols], shade)

    flow(rows, grid, 3, 0, 2, (10, 10, 8), *scratch, finish)


def local(depth_layers, thickness_layers, coverage):
    slabs = lax.axis_size("slab")
    grid = math.isqrt(lax.axis_size("tile"))
    slab = lax.axis_index("slab")
    tile = lax.axis_index("tile")
    _, _, height, width = depth_layers.shape
    rows = height // slabs
    core = slab % 2

    parts = lax.all_to_all(
        depth_layers.reshape(slabs, rows, width), "slab", split_axis=0, concat_axis=0, tiled=True
    )
    thick = sum_by_swaps(pair_sum(thickness_layers.reshape(slabs, rows, width)), slab)
    band = jnp.min(parts, axis=0)
    far, near = neighbour_rows(band, grid, slabs, core)
    odd = core == 1
    above, below = jnp.where(odd, near, far), jnp.where(odd, far, near)
    tall = [
        jnp.concatenate([a[:, cut] for a in (above, band, below)], axis=0)
        for cut in (slice(0, LANES), slice(width - LANES, width))
    ]
    left, right = neighbour_columns(*tall, grid, tile % grid)

    vmem = pl.BlockSpec(memory_space=pltpu.VMEM)
    total = rows + 2 * PAD
    blocks = width // LANES
    above, band, below, left, right, thick, cover = (
        pltpu.with_memory_space_constraint(a, pltpu.VMEM)
        for a in (above, band, below, left, right, thick, coverage[0])
    )
    held = pltpu.VMEM((rows, width), jnp.float32)
    inner = pl.pallas_call(
        functools.partial(inner_kernel, rows, grid),
        compiler_params=PARAMS,
        out_shape=(held, held),
        in_specs=[vmem] * 5,
        out_specs=(vmem, vmem),
        scratch_shapes=[pltpu.VMEM((blocks, total, LANES), jnp.float32)] * 3,
    )(above, band, below, thick, cover)
    out = jax.ShapeDtypeStruct((rows, width), jnp.float32)
    smooth, shade = pl.pallas_call(
        functools.partial(outer_kernel, rows, grid),
        compiler_params=PARAMS,
        out_shape=(out, out),
        in_specs=[vmem] * 9,
        out_specs=(vmem, vmem),
        scratch_shapes=[pltpu.VMEM((3, total, LANES), jnp.float32)] * 3,
    )(
        above,
        band,
        below,
        left,
        right,
        thick,
        cover,
        *(pltpu.with_memory_space_constraint(a, pltpu.VMEM) for a in inner),
    )
    return (smooth[None], shade[None])


def solution(mesh):
    return jax.shard_map(
        local,
        mesh=mesh,
        in_specs=(
            P("slab", "tile", None, None),
            P("slab", "tile", None, None),
            P("tile", "slab", None),
        ),
        out_specs=(P("tile", "slab", None), P("tile", "slab", None)),
        check_vma=False,
    )
```

time: 48 us -> 45 us (0.938)
  the two profiles are of different devices: /device:TPU:416 before, /device:TPU:288 now
where the time goes in v3:
time: 45 us; the launch traced here: 44.5 us
  starting transfers between devices  29.5 us (66%)
  waiting for transfers between devices  7.55 us (17%)
  Pallas kernels  6.2 us (14%)
  between operations  0.94 us (2%)
    ppermute x3, starting transfers between devices, sum_by_swaps(): total = total + lax.ppermute(share(chip ^ step), 'slab', route)  10.4 us
    ppermute x1, starting transfers between devices, neighbour_columns(): far = lax.ppermute(long, 'tile', far)[:-8]  5.18 us
    all_to_all x1, starting transfers between devices, local(): lax.all_to_all(depth_layers.reshape(slabs, rows, width), 'slab', split_ax...  4.48 us
    ppermute x1, waiting for transfers between devices, neighbour_rows(): far = lax.ppermute(long, ('slab', 'tile'), across)  3.47 us
    ppermute x1, starting transfers between devices, neighbour_rows(): far = lax.ppermute(long, ('slab', 'tile'), across)  3.06 us
    ppermute x1, starting transfers between devices, pair_sum(): lax.ppermute(pick(1), 'slab', [(i, i ^ 1) for i in range(bands)])  2.41 us
    pallas_call x1, Pallas kernels, local(): pl.pallas_call(functools.partial(inner_kernel, rows, grid), compiler_para...  2.25 us
    pallas_call x2, Pallas kernels, pick(): pl.pallas_call(functools.partial(pick_kernel, flip), compiler_params=PARA...  2.11 us
  transfers between devices with their start and end apart: 9, of which 5 were waited for; matrix products, arithmetic and copies ran while one was open for 1% of the time, Pallas kernels for 10%

profile of v3, /device:TPU:288, one launch (start us, length us, event | category | flops | bytes accessed | tf_op | source)
XLA Modules:
  0.0 44.5 jit_solution(11385772858740547807)
XLA Ops:
  0.6 4.5 %all-to-all-start = ((f32[8,64,512]{2,1,0:T(8,128)}), f32[8,64,512]{2,1,0:T(8,128)S(1)}, u32[]{:S(2)}, u32[]{:S(2)}) async-start(f32[8,64,512]{2,1,0:T(8,128)} %bitcast.21), calls=%async_computation | async-start | bytes 2097152 | tf_op jit(solution)/shard_map/all_to_all | solution.py:249
  5.1 1.0 %shard_map.51 = f32[4,64,512]{2,1,0:T(8,128)S(1)} custom-call(f32[4,2,64,512]{3,2,1,0:T(8,128)} %bitcast.19), custom_call_target="tpu_custom_call" | custom-call | tf_op jit(solution)/shard_map/pallas_call | solution.py:33
  6.2 2.4 %collective-permute-start.4 = (f32[4,64,512]{2,1,0:T(8,128)S(1)}, f32[4,64,512]{2,1,0:T(8,128)S(1)}, u32[]{:S(2)}, u32[]{:S(2)}) collective-permute-start(f32[4,64,512]{2,1,0:T(8,128)S(1)} %shard_map.51), channel_id=1, source_target_pairs={{0,64},{64,0},{128,192},{192,128},{256,320},{320,256},{384,448},{4... | collective-permute-start | bytes 1572872 | tf_op jit(solution)/shard_map/ppermute | solution.py:43
  8.6 1.1 %shard_map.50 = f32[4,64,512]{2,1,0:T(8,128)S(1)} custom-call(f32[4,2,64,512]{3,2,1,0:T(8,128)} %bitcast.20), custom_call_target="tpu_custom_call" | custom-call | tf_op jit(solution)/shard_map/pallas_call | solution.py:33
  9.8 0.3 collective-permute-done.4
  10.1 0.1 add.39
  10.2 3.8 %collective-permute-start.5 = (f32[64,512]{1,0:T(8,128)S(1)}, f32[64,512]{1,0:T(8,128)S(1)}, u32[]{:S(2)}, u32[]{:S(2)}) collective-permute-start(f32[64,512]{1,0:T(8,128)S(1)} %get-tuple-element.10), channel_id=1, source_target_pairs={{0,128},{64,192},{128,0},{192,64},{256,384},{320,448},{384,256},{4... | collective-permute-start | bytes 393224 | tf_op jit(solution)/shard_map/ppermute | solution.py:57
  14.0 4.6 %collective-permute-start.6 = (f32[64,512]{1,0:T(8,128)S(1)}, f32[64,512]{1,0:T(8,128)S(1)}, u32[]{:S(2)}, u32[]{:S(2)}) collective-permute-start(f32[64,512]{1,0:T(8,128)S(1)} %get-tuple-element.12), channel_id=1, source_target_pairs={{0,256},{64,320},{128,384},{192,448},{256,0},{320,64},{384,128},{4... | collective-permute-start | bytes 393224 | tf_op jit(solution)/shard_map/ppermute | solution.py:57
  18.6 2.1 %collective-permute-start.7 = (f32[64,512]{1,0:T(8,128)S(1)}, f32[64,512]{1,0:T(8,128)S(1)}, u32[]{:S(2)}, u32[]{:S(2)}) collective-permute-start(f32[64,512]{1,0:T(8,128)S(1)} %get-tuple-element.11), channel_id=1, source_target_pairs={{0,384},{64,448},{128,256},{192,320},{256,128},{320,192},{384,0},{... | collective-permute-start | bytes 393224 | tf_op jit(solution)/shard_map/ppermute | solution.py:57
  20.7 0.9 %all-to-all-done = f32[8,64,512]{2,1,0:T(8,128)S(1)} async-done(((f32[8,64,512]{2,1,0:T(8,128)}), f32[8,64,512]{2,1,0:T(8,128)S(1)}, u32[]{:S(2)}, u32[]{:S(2)}) %all-to-all-start) | async-done | bytes 1048608 | tf_op jit(solution)/shard_map/all_to_all | solution.py:249
  21.6 0.1 reduce_min.9.band_ref
  21.7 3.1 %collective-permute-start.1 = (f32[24,512]{1,0:T(8,128)S(1)}, f32[24,512]{1,0:T(8,128)S(1)}, u32[]{:S(2)}, u32[]{:S(2)}) collective-permute-start(f32[24,512]{1,0:T(8,128)S(1)} %slice_select_fusion), channel_id=1, source_target_pairs={{64,128},{128,64},{192,256},{256,192},{320,384},{384,320},{448,8},... | collective-permute-start | bytes 147464 | tf_op jit(solution)/shard_map/ppermute | solution.py:73
  24.7 1.9 %collective-permute-start = (f32[16,512]{1,0:T(8,128)S(1)}, f32[16,512]{1,0:T(8,128)S(1)}, u32[]{:S(2)}, u32[]{:S(2)}) collective-permute-start(f32[16,512]{1,0:T(8,128)S(1)} %slice_select_fusion.4), channel_id=1, source_target_pairs={{0,64},{64,0},{128,192},{192,128},{256,320},{320,256},{384,448},{4... | collective-permute-start | bytes 98312 | tf_op jit(solution)/shard_map/ppermute | solution.py:75
  26.7 1.2 %collective-permute-done = f32[16,512]{1,0:T(8,128)S(1)} collective-permute-done((f32[16,512]{1,0:T(8,128)S(1)}, f32[16,512]{1,0:T(8,128)S(1)}, u32[]{:S(2)}, u32[]{:S(2)}) %collective-permute-start) | collective-permute-done | bytes 32800 | tf_op jit(solution)/shard_map/ppermute | solution.py:75
  27.8 3.5 %collective-permute-done.1 = f32[24,512]{1,0:T(8,128)S(1)} collective-permute-done((f32[24,512]{1,0:T(8,128)S(1)}, f32[24,512]{1,0:T(8,128)S(1)}, u32[]{:S(2)}, u32[]{:S(2)}) %collective-permute-start.1) | collective-permute-done | bytes 49184 | tf_op jit(solution)/shard_map/ppermute | solution.py:73
  31.4 5.2 %collective-permute-start.3 = (f32[104,128]{1,0:T(8,128)S(1)}, f32[104,128]{1,0:T(8,128)S(1)}, u32[]{:S(2)}, u32[]{:S(2)}) collective-permute-start(f32[104,128]{1,0:T(8,128)S(1)} %pad_maximum_fusion), channel_id=1, source_target_pairs={{1,2},{2,1},{3,4},{4,3},{5,6},{6,5},{9,10},{10,9},{11,12},{12,11},... | collective-permute-start | bytes 159752 | tf_op jit(solution)/shard_map/ppermute | solution.py:87
  36.6 0.0 copy-start
  36.6 2.1 %collective-permute-start.2 = (f32[96,128]{1,0:T(8,128)S(1)}, f32[96,128]{1,0:T(8,128)S(1)}, u32[]{:S(2)}, u32[]{:S(2)}) collective-permute-start(f32[96,128]{1,0:T(8,128)S(1)} %get-tuple-element.18), channel_id=1, source_target_pairs={{0,1},{1,0},{2,3},{3,2},{4,5},{5,4},{6,7},{7,6},{8,9},{9,8},{10,11... | collective-permute-start | bytes 147464 | tf_op jit(solution)/shard_map/ppermute | solution.py:88
  38.6 0.0 collective-permute-done.5
  38.6 0.0 collective-permute-done.6
  38.7 0.0 collective-permute-done.7
  38.7 0.0 copy-done
  38.7 2.2 %shard_map.52 = (f32[64,512]{1,0:T(8,128)S(1)}, f32[64,512]{1,0:T(8,128)S(1)}) custom-call(f32[16,512]{1,0:T(8,128)S(1)} %get-tuple-element.20.above_ref, f32[64,512]{1,0:T(8,128)S(1)} %reduce_min.9.band_ref, f32[16,512]{1,0:T(8,128)S(1)} %get-tuple-element.19.below_ref, f32[64,512]{1,0:T(8,128)S(1)} %fusion.1.thick_ref, s32[64,512]{1,0:T(8,128)S(1)} %bitcast.17), custom_call_target="tpu_custom_call" | custom-call | tf_op jit(solution)/shard_map/pallas_call | solution.py:271
  41.0 1.7 %collective-permute-done.2 = f32[96,128]{1,0:T(8,128)S(1)} collective-permute-done((f32[96,128]{1,0:T(8,128)S(1)}, f32[96,128]{1,0:T(8,128)S(1)}, u32[]{:S(2)}, u32[]{:S(2)}) %collective-permute-start.2) | collective-permute-done | bytes 49184 | tf_op jit(solution)/shard_map/ppermute | solution.py:88
  42.7 0.0 collective-permute-done.3
  42.7 1.8 %shard_map.53 = (f32[64,512]{1,0:T(8,128)}, f32[64,512]{1,0:T(8,128)}) custom-call(f32[16,512]{1,0:T(8,128)S(1)} %get-tuple-element.20.above_ref, f32[64,512]{1,0:T(8,128)S(1)} %reduce_min.9.band_ref, f32[16,512]{1,0:T(8,128)S(1)} %get-tuple-element.19.below_ref, f32[96,128]{1,0:T(8,128)S(1)} %get-tuple-element.16.left_ref, ...), custom_call_target="tpu_custom_call" | custom-call | tf_op jit(solution)/shard_map/pallas_call | solution.py:280
  (11 shorter events, 0.1 us)
Async XLA Ops:
  0.6 20.9 %all-to-all-start = ((f32[8,64,512]{2,1,0:T(8,128)}), f32[8,64,512]{2,1,0:T(8,128)S(1)}, u32[]{:S(2)}, u32[]{:S(2)}) async-start(f32[8,64,512]{2,1,0:T(8,128)} %bitcast.21), calls=%async_computation | async-start | bytes 2097152 | tf_op jit(solution)/shard_map/all_to_all | solution.py:249
  6.2 3.9 %collective-permute-start.4 = (f32[4,64,512]{2,1,0:T(8,128)S(1)}, f32[4,64,512]{2,1,0:T(8,128)S(1)}, u32[]{:S(2)}, u32[]{:S(2)}) collective-permute-start(f32[4,64,512]{2,1,0:T(8,128)S(1)} %shard_map.51), channel_id=1, source_target_pairs={{0,64},{64,0},{128,192},{192,128},{256,320},{320,256},{384,448},{4... | collective-permute-start | bytes 1572872 | tf_op jit(solution)/shard_map/ppermute | solution.py:43
  10.2 28.4 %collective-permute-start.5 = (f32[64,512]{1,0:T(8,128)S(1)}, f32[64,512]{1,0:T(8,128)S(1)}, u32[]{:S(2)}, u32[]{:S(2)}) collective-permute-start(f32[64,512]{1,0:T(8,128)S(1)} %get-tuple-element.10), channel_id=1, source_target_pairs={{0,128},{64,192},{128,0},{192,64},{256,384},{320,448},{384,256},{4... | collective-permute-start | bytes 393224 | tf_op jit(solution)/shard_map/ppermute | solution.py:57
  14.0 24.6 %collective-permute-start.6 = (f32[64,512]{1,0:T(8,128)S(1)}, f32[64,512]{1,0:T(8,128)S(1)}, u32[]{:S(2)}, u32[]{:S(2)}) collective-permute-start(f32[64,512]{1,0:T(8,128)S(1)} %get-tuple-element.12), channel_id=1, source_target_pairs={{0,256},{64,320},{128,384},{192,448},{256,0},{320,64},{384,128},{4... | collective-permute-start | bytes 393224 | tf_op jit(solution)/shard_map/ppermute | solution.py:57
  18.6 20.0 %collective-permute-start.7 = (f32[64,512]{1,0:T(8,128)S(1)}, f32[64,512]{1,0:T(8,128)S(1)}, u32[]{:S(2)}, u32[]{:S(2)}) collective-permute-start(f32[64,512]{1,0:T(8,128)S(1)} %get-tuple-element.11), channel_id=1, source_target_pairs={{0,384},{64,448},{128,256},{192,320},{256,128},{320,192},{384,0},{... | collective-permute-start | bytes 393224 | tf_op jit(solution)/shard_map/ppermute | solution.py:57
  21.7 9.6 %collective-permute-start.1 = (f32[24,512]{1,0:T(8,128)S(1)}, f32[24,512]{1,0:T(8,128)S(1)}, u32[]{:S(2)}, u32[]{:S(2)}) collective-permute-start(f32[24,512]{1,0:T(8,128)S(1)} %slice_select_fusion), channel_id=1, source_target_pairs={{64,128},{128,64},{192,256},{256,192},{320,384},{384,320},{448,8},... | collective-permute-start | bytes 147464 | tf_op jit(solution)/shard_map/ppermute | solution.py:73
  24.7 3.1 %collective-permute-start = (f32[16,512]{1,0:T(8,128)S(1)}, f32[16,512]{1,0:T(8,128)S(1)}, u32[]{:S(2)}, u32[]{:S(2)}) collective-permute-start(f32[16,512]{1,0:T(8,128)S(1)} %slice_select_fusion.4), channel_id=1, source_target_pairs={{0,64},{64,0},{128,192},{192,128},{256,320},{320,256},{384,448},{4... | collective-permute-start | bytes 98312 | tf_op jit(solution)/shard_map/ppermute | solution.py:75
  31.4 11.3 %collective-permute-start.3 = (f32[104,128]{1,0:T(8,128)S(1)}, f32[104,128]{1,0:T(8,128)S(1)}, u32[]{:S(2)}, u32[]{:S(2)}) collective-permute-start(f32[104,128]{1,0:T(8,128)S(1)} %pad_maximum_fusion), channel_id=1, source_target_pairs={{1,2},{2,1},{3,4},{4,3},{5,6},{6,5},{9,10},{10,9},{11,12},{12,11},... | collective-permute-start | bytes 159752 | tf_op jit(solution)/shard_map/ppermute | solution.py:87
  36.6 2.2 %copy-start = (s32[1,64,512]{2,1,0:T(8,128)S(1)}, s32[1,64,512]{2,1,0:T(8,128)}, u32[]{:S(2)}) copy-start(s32[1,64,512]{2,1,0:T(8,128)} %param.5) | copy-start | bytes 393220
  36.6 6.1 %collective-permute-start.2 = (f32[96,128]{1,0:T(8,128)S(1)}, f32[96,128]{1,0:T(8,128)S(1)}, u32[]{:S(2)}, u32[]{:S(2)}) collective-permute-start(f32[96,128]{1,0:T(8,128)S(1)} %get-tuple-element.18), channel_id=1, source_target_pairs={{0,1},{1,0},{2,3},{3,2},{4,5},{5,4},{6,7},{7,6},{8,9},{9,8},{10,11... | collective-permute-start | bytes 147464 | tf_op jit(solution)/shard_map/ppermute | solution.py:88

commit v4 on v3

--- a/solution.py
+++ b/solution.py
@@ -76,12 +76,20 @@
     return far, near
 
 
+def pack(block, start):
+    size = block.shape[0] // 4
+    return jnp.concatenate(
+        [block[k * size : (k + 1) * size, start : start + LANES // 4] for k in range(4)], axis=1
+    )
+
+
 def neighbour_columns(first, last, grid, column):
     odd = column % 2 == 1
     near, far = [], []
     for t in range(grid * grid):
         if t % grid + 1 < grid:
             (near if t % 2 == 0 else far).extend([(t, t + 1), (t + 1, t)])
+    first, last = pack(first, 0), pack(last, LANES - LANES // 4)
     long = jnp.where(odd, last, first)
     long = jnp.concatenate([long, long[:8]], axis=0)
     far = lax.ppermute(long, "tile", far)[:-8]
@@ -102,23 +110,27 @@
     first_row = lax.broadcasted_iota(jnp.int32, (8, LANES), 0) == 0
     last_row = lax.broadcasted_iota(jnp.int32, (8, LANES), 0) == 7
     first_lane, last_lane = lane == 0, lane == LANES - 1
+    at_left, at_right = left_edge & (lane == first[1]), right_edge & (lane == last[1])
 
     def across(values, left, right):
         after = [pltpu.roll(p, LANES - 1, 1) for p in values]
         before = [pltpu.roll(p, 1, 1) for p in values]
         out = []
         for j in range(pieces):
-            beyond, behind = after[(j + 1) % pieces], before[(j - 1) % pieces]
-            if j == first:
-                behind = jnp.where(left_edge, left, behind)
-            if j == last:
-                beyond = jnp.where(right_edge, right, beyond)
-            out.append(jnp.where(last_lane, beyond, after[j]) - jnp.where(first_lane, behind, before[j]))
+            beyond, behind = after[j], before[j]
+            if pieces > 1:
+                beyond = jnp.where(last_lane, after[(j + 1) % pieces], beyond)
+                behind = jnp.where(first_lane, before[(j - 1) % pieces], behind)
+            if j == last[0]:
+                beyond = jnp.where(at_right, right, beyond)
+            if j == first[0]:
+                behind = jnp.where(at_left, left, behind)
+            out.append(beyond - behind)
         return out
 
     def slopes(r):
         here = [surface[j, pl.ds(r, 8), :] for j in range(pieces)]
-        wide_x = across(here, here[first], here[last])
+        wide_x = across(here, here[first[0]], here[last[0]])
         at_top = first_row & (top_edge & (r == top))
         at_bottom = last_row & (bottom_edge & (r == bottom - 8))
         wide_y = []
@@ -190,7 +202,7 @@
             smooth_ref[span, cols] = here[j]
             shade_ref[span, cols] = shaded(wide_x[j], wide_y[j], [thick_ref[span, cols]], cover_ref[span, cols])
 
-    flow(rows, grid, blocks, blocks - 1, 0, (5, 10, 4), *scratch, finish)
+    flow(rows, grid, blocks, (blocks - 1, LANES - 1), (0, 0), (5, 10, 4), *scratch, finish)
 
 
 def outer_kernel(
@@ -212,29 +224,44 @@
     surface = scratch[0]
     total = rows + 2 * PAD
     blocks = band_ref.shape[1] // LANES
-    low = lax.broadcasted_iota(jnp.int32, (8, LANES), 1) < LANES // 2
-    outer = ((0, blocks - 1), (2, 0))
-    for j, block in outer:
+    quarter = LANES // 4
+    lane = lax.broadcasted_iota(jnp.int32, (8, LANES), 1)
+    low = lane < LANES // 2
+
+    def own(r, block):
         cols = pl.ds(block * LANES, LANES)
-        surface[j, 0:PAD, :] = above_ref[:, cols]
-        surface[j, PAD : PAD + rows, :] = band_ref[:, cols]
-        surface[j, PAD + rows :, :] = below_ref[:, cols]
+        if r < PAD:
+            return above_ref[r : r + 8, cols]
+        if r < PAD + rows:
+            return band_ref[r - PAD : r - PAD + 8, cols]
+        return below_ref[r - PAD - rows : r - PAD - rows + 8, cols]
+
+    size = total // 4
     for r in range(0, total, 8):
-        surface[1, r : r + 8, :] = jnp.where(low, right_ref[r : r + 8, :], left_ref[r : r + 8, :])
+        group, row = r // size, r % size
+        right = pltpu.roll(right_ref[row : row + 8, :], (5 - group) % 4 * quarter, 1)
+        left = pltpu.roll(left_ref[row : row + 8, :], (6 - group) % 4 * quarter, 1)
+        at_right = jnp.where(lane < quarter, pltpu.roll(own(r, blocks - 1), quarter, 1), right)
+        at_left = jnp.where(lane < 3 * quarter, left, pltpu.roll(own(r, 0), 3 * quarter, 1))
+        surface[0, r : r + 8, :] = jnp.where(low, at_right, at_left)
     middle = pl.ds(LANES, (blocks - 2) * LANES)
     smooth_ref[:, middle] = inner_smooth_ref[:, middle]
     shade_ref[:, middle] = inner_shade_ref[:, middle]
+    outer = (
+        (0, quarter, lane < quarter // 2),
+        (blocks - 1, 3 * quarter, lane >= LANES - quarter // 2),
+    )
 
     def finish(r, here, wide_x, wide_y):
         span = pl.ds(r, 8)
-        for j, block in outer:
+        for block, shift, new in outer:
             cols = pl.ds(block * LANES, LANES)
-            keep = low if j == 0 else jnp.logical_not(low)
-            shade = shaded(wide_x[j], wide_y[j], [thick_ref[span, cols]], cover_ref[span, cols])
-            smooth_ref[span, cols] = jnp.where(keep, inner_smooth_ref[span, cols], here[j])
-            shade_ref[span, cols] = jnp.where(keep, inner_shade_ref[span, cols], shade)
-
-    flow(rows, grid, 3, 0, 2, (10, 10, 8), *scratch, finish)
+            smooth, x, y = (pltpu.roll(a[0], shift, 1) for a in (here, wide_x, wide_y))
+            shade = shaded(x, y, [thick_ref[span, cols]], cover_ref[span, cols])
+            smooth_ref[span, cols] = jnp.where(new, smooth, inner_smooth_ref[span, cols])
+            shade_ref[span, cols] = jnp.where(new, shade, inner_shade_ref[span, cols])
+
+    flow(rows, grid, 1, (0, quarter - 1), (0, 3 * quarter), (10, 10, 8), *scratch, finish)
 
 
 def local(depth_layers, thickness_layers, coverage):
@@ -283,7 +310,7 @@
         out_shape=(out, out),
         in_specs=[vmem] * 9,
         out_specs=(vmem, vmem),
-        scratch_shapes=[pltpu.VMEM((3, total, LANES), jnp.float32)] * 3,
+        scratch_shapes=[pltpu.VMEM((1, total, LANES), jnp.float32)] * 3,
     )(
         above,
         band,

time: 45 us -> 44.6 us (level)
  no operation moved by 1% of the time
where the time goes in v4:
time: 44.6 us; the launch traced here: 44.1 us
  starting transfers between devices  29.5 us (66%)
  waiting for transfers between devices  7.11 us (16%)
  Pallas kernels  6.08 us (14%)
  between operations  0.94 us (2%)
    ppermute x3, starting transfers between devices, sum_by_swaps(): total = total + lax.ppermute(share(chip ^ step), 'slab', route)  10.4 us
    ppermute x1, starting transfers between devices, neighbour_columns(): far = lax.ppermute(long, 'tile', far)[:-8]  5.18 us
    all_to_all x1, starting transfers between devices, local(): lax.all_to_all(depth_layers.reshape(slabs, rows, width), 'slab', split_ax...  4.48 us
    ppermute x1, waiting for transfers between devices, neighbour_rows(): far = lax.ppermute(long, ('slab', 'tile'), across)  3.47 us
    ppermute x1, starting transfers between devices, neighbour_rows(): far = lax.ppermute(long, ('slab', 'tile'), across)  3.06 us
    ppermute x1, starting transfers between devices, pair_sum(): lax.ppermute(pick(1), 'slab', [(i, i ^ 1) for i in range(bands)])  2.41 us
    pallas_call x1, Pallas kernels, local(): pl.pallas_call(functools.partial(inner_kernel, rows, grid), compiler_para...  2.24 us
    pallas_call x2, Pallas kernels, pick(): pl.pallas_call(functools.partial(pick_kernel, flip), compiler_params=PARA...  2.11 us
  transfers between devices with their start and end apart: 9, of which 5 were waited for; matrix products, arithmetic and copies ran while one was open for 1% of the time, Pallas kernels for 10%

profile of v4, /device:TPU:288, one launch (start us, length us, event | category | flops | bytes accessed | tf_op | source)
XLA Modules:
  0.0 44.1 jit_solution(13323324377168691423)
XLA Ops:
  0.6 4.5 %all-to-all-start = ((f32[8,64,512]{2,1,0:T(8,128)}), f32[8,64,512]{2,1,0:T(8,128)S(1)}, u32[]{:S(2)}, u32[]{:S(2)}) async-start(f32[8,64,512]{2,1,0:T(8,128)} %bitcast.21), calls=%async_computation | async-start | bytes 2097152 | tf_op jit(solution)/shard_map/all_to_all | solution.py:276
  5.1 1.0 %shard_map.51 = f32[4,64,512]{2,1,0:T(8,128)S(1)} custom-call(f32[4,2,64,512]{3,2,1,0:T(8,128)} %bitcast.19), custom_call_target="tpu_custom_call" | custom-call | tf_op jit(solution)/shard_map/pallas_call | solution.py:33
  6.2 2.4 %collective-permute-start.4 = (f32[4,64,512]{2,1,0:T(8,128)S(1)}, f32[4,64,512]{2,1,0:T(8,128)S(1)}, u32[]{:S(2)}, u32[]{:S(2)}) collective-permute-start(f32[4,64,512]{2,1,0:T(8,128)S(1)} %shard_map.51), channel_id=1, source_target_pairs={{0,64},{64,0},{128,192},{192,128},{256,320},{320,256},{384,448},{4... | collective-permute-start | bytes 1572872 | tf_op jit(solution)/shard_map/ppermute | solution.py:43
  8.6 1.1 %shard_map.50 = f32[4,64,512]{2,1,0:T(8,128)S(1)} custom-call(f32[4,2,64,512]{3,2,1,0:T(8,128)} %bitcast.20), custom_call_target="tpu_custom_call" | custom-call | tf_op jit(solution)/shard_map/pallas_call | solution.py:33
  9.8 0.3 collective-permute-done.4
  10.1 0.1 add.39
  10.2 3.8 %collective-permute-start.5 = (f32[64,512]{1,0:T(8,128)S(1)}, f32[64,512]{1,0:T(8,128)S(1)}, u32[]{:S(2)}, u32[]{:S(2)}) collective-permute-start(f32[64,512]{1,0:T(8,128)S(1)} %get-tuple-element.13), channel_id=1, source_target_pairs={{0,128},{64,192},{128,0},{192,64},{256,384},{320,448},{384,256},{4... | collective-permute-start | bytes 393224 | tf_op jit(solution)/shard_map/ppermute | solution.py:57
  14.0 4.6 %collective-permute-start.6 = (f32[64,512]{1,0:T(8,128)S(1)}, f32[64,512]{1,0:T(8,128)S(1)}, u32[]{:S(2)}, u32[]{:S(2)}) collective-permute-start(f32[64,512]{1,0:T(8,128)S(1)} %get-tuple-element.15), channel_id=1, source_target_pairs={{0,256},{64,320},{128,384},{192,448},{256,0},{320,64},{384,128},{4... | collective-permute-start | bytes 393224 | tf_op jit(solution)/shard_map/ppermute | solution.py:57
  18.6 2.1 %collective-permute-start.7 = (f32[64,512]{1,0:T(8,128)S(1)}, f32[64,512]{1,0:T(8,128)S(1)}, u32[]{:S(2)}, u32[]{:S(2)}) collective-permute-start(f32[64,512]{1,0:T(8,128)S(1)} %get-tuple-element.14), channel_id=1, source_target_pairs={{0,384},{64,448},{128,256},{192,320},{256,128},{320,192},{384,0},{... | collective-permute-start | bytes 393224 | tf_op jit(solution)/shard_map/ppermute | solution.py:57
  20.7 0.9 %all-to-all-done = f32[8,64,512]{2,1,0:T(8,128)S(1)} async-done(((f32[8,64,512]{2,1,0:T(8,128)}), f32[8,64,512]{2,1,0:T(8,128)S(1)}, u32[]{:S(2)}, u32[]{:S(2)}) %all-to-all-start) | async-done | bytes 1048608 | tf_op jit(solution)/shard_map/all_to_all | solution.py:276
  21.6 0.1 reduce_min.9.band_ref
  21.7 3.1 %collective-permute-start.1 = (f32[24,512]{1,0:T(8,128)S(1)}, f32[24,512]{1,0:T(8,128)S(1)}, u32[]{:S(2)}, u32[]{:S(2)}) collective-permute-start(f32[24,512]{1,0:T(8,128)S(1)} %slice_select_fusion), channel_id=1, source_target_pairs={{64,128},{128,64},{192,256},{256,192},{320,384},{384,320},{448,8},... | collective-permute-start | bytes 147464 | tf_op jit(solution)/shard_map/ppermute | solution.py:73
  24.7 1.9 %collective-permute-start = (f32[16,512]{1,0:T(8,128)S(1)}, f32[16,512]{1,0:T(8,128)S(1)}, u32[]{:S(2)}, u32[]{:S(2)}) collective-permute-start(f32[16,512]{1,0:T(8,128)S(1)} %slice_select_fusion.2), channel_id=1, source_target_pairs={{0,64},{64,0},{128,192},{192,128},{256,320},{320,256},{384,448},{4... | collective-permute-start | bytes 98312 | tf_op jit(solution)/shard_map/ppermute | solution.py:75
  26.7 0.1 fusion.10
  26.7 1.1 %collective-permute-done = f32[16,512]{1,0:T(8,128)S(1)} collective-permute-done((f32[16,512]{1,0:T(8,128)S(1)}, f32[16,512]{1,0:T(8,128)S(1)}, u32[]{:S(2)}, u32[]{:S(2)}) %collective-permute-start) | collective-permute-done | bytes 32800 | tf_op jit(solution)/shard_map/ppermute | solution.py:75
  27.8 3.5 %collective-permute-done.1 = f32[24,512]{1,0:T(8,128)S(1)} collective-permute-done((f32[24,512]{1,0:T(8,128)S(1)}, f32[24,512]{1,0:T(8,128)S(1)}, u32[]{:S(2)}, u32[]{:S(2)}) %collective-permute-start.1) | collective-permute-done | bytes 49184 | tf_op jit(solution)/shard_map/ppermute | solution.py:73
  31.3 0.1 broadcast_select_fusion.2
  31.5 5.2 %collective-permute-start.3 = (f32[32,128]{1,0:T(8,128)S(1)}, f32[32,128]{1,0:T(8,128)S(1)}, u32[]{:S(2)}, u32[]{:S(2)}) collective-permute-start(f32[32,128]{1,0:T(8,128)S(1)} %pad_maximum_fusion), channel_id=1, source_target_pairs={{1,2},{2,1},{3,4},{4,3},{5,6},{6,5},{9,10},{10,9},{11,12},{12,11},... | collective-permute-start | bytes 49160 | tf_op jit(solution)/shard_map/ppermute | solution.py:95
  36.7 0.0 copy-start
  36.7 2.1 %collective-permute-start.2 = (f32[24,128]{1,0:T(8,128)S(1)}, f32[24,128]{1,0:T(8,128)S(1)}, u32[]{:S(2)}, u32[]{:S(2)}) collective-permute-start(f32[24,128]{1,0:T(8,128)S(1)} %broadcast_select_fusion.3), channel_id=1, source_target_pairs={{0,1},{1,0},{2,3},{3,2},{4,5},{5,4},{6,7},{7,6},{8,9},{9,8},{10,11... | collective-permute-start | bytes 36872 | tf_op jit(solution)/shard_map/ppermute | solution.py:96
  38.7 0.0 collective-permute-done.5
  38.7 0.0 collective-permute-done.6
  38.8 0.0 collective-permute-done.7
  38.8 0.0 copy-done
  38.8 2.2 %shard_map.52 = (f32[64,512]{1,0:T(8,128)S(1)}, f32[64,512]{1,0:T(8,128)S(1)}) custom-call(f32[16,512]{1,0:T(8,128)S(1)} %get-tuple-element.23.above_ref, f32[64,512]{1,0:T(8,128)S(1)} %reduce_min.9.band_ref, f32[16,512]{1,0:T(8,128)S(1)} %get-tuple-element.22.below_ref, f32[64,512]{1,0:T(8,128)S(1)} %fusion.1.thick_ref, s32[64,512]{1,0:T(8,128)S(1)} %bitcast.17), custom_call_target="tpu_custom_call" | custom-call | tf_op jit(solution)/shard_map/pallas_call | solution.py:298
  41.1 1.3 %collective-permute-done.2 = f32[24,128]{1,0:T(8,128)S(1)} collective-permute-done((f32[24,128]{1,0:T(8,128)S(1)}, f32[24,128]{1,0:T(8,128)S(1)}, u32[]{:S(2)}, u32[]{:S(2)}) %collective-permute-start.2) | collective-permute-done | bytes 12320 | tf_op jit(solution)/shard_map/ppermute | solution.py:96
  42.4 0.0 collective-permute-done.3
  42.4 1.7 %shard_map.53 = (f32[64,512]{1,0:T(8,128)}, f32[64,512]{1,0:T(8,128)}) custom-call(f32[16,512]{1,0:T(8,128)S(1)} %get-tuple-element.23.above_ref, f32[64,512]{1,0:T(8,128)S(1)} %reduce_min.9.band_ref, f32[16,512]{1,0:T(8,128)S(1)} %get-tuple-element.22.below_ref, f32[24,128]{1,0:T(8,128)S(1)} %get-tuple-element.29.left_ref, ...), custom_call_target="tpu_custom_call" | custom-call | tf_op jit(solution)/shard_map/pallas_call | solution.py:307
  (11 shorter events, 0.1 us)
Async XLA Ops:
  0.6 20.9 %all-to-all-start = ((f32[8,64,512]{2,1,0:T(8,128)}), f32[8,64,512]{2,1,0:T(8,128)S(1)}, u32[]{:S(2)}, u32[]{:S(2)}) async-start(f32[8,64,512]{2,1,0:T(8,128)} %bitcast.21), calls=%async_computation | async-start | bytes 2097152 | tf_op jit(solution)/shard_map/all_to_all | solution.py:276
  6.2 3.9 %collective-permute-start.4 = (f32[4,64,512]{2,1,0:T(8,128)S(1)}, f32[4,64,512]{2,1,0:T(8,128)S(1)}, u32[]{:S(2)}, u32[]{:S(2)}) collective-permute-start(f32[4,64,512]{2,1,0:T(8,128)S(1)} %shard_map.51), channel_id=1, source_target_pairs={{0,64},{64,0},{128,192},{192,128},{256,320},{320,256},{384,448},{4... | collective-permute-start | bytes 1572872 | tf_op jit(solution)/shard_map/ppermute | solution.py:43
  10.2 28.5 %collective-permute-start.5 = (f32[64,512]{1,0:T(8,128)S(1)}, f32[64,512]{1,0:T(8,128)S(1)}, u32[]{:S(2)}, u32[]{:S(2)}) collective-permute-start(f32[64,512]{1,0:T(8,128)S(1)} %get-tuple-element.13), channel_id=1, source_target_pairs={{0,128},{64,192},{128,0},{192,64},{256,384},{320,448},{384,256},{4... | collective-permute-start | bytes 393224 | tf_op jit(solution)/shard_map/ppermute | solution.py:57
  14.0 24.7 %collective-permute-start.6 = (f32[64,512]{1,0:T(8,128)S(1)}, f32[64,512]{1,0:T(8,128)S(1)}, u32[]{:S(2)}, u32[]{:S(2)}) collective-permute-start(f32[64,512]{1,0:T(8,128)S(1)} %get-tuple-element.15), channel_id=1, source_target_pairs={{0,256},{64,320},{128,384},{192,448},{256,0},{320,64},{384,128},{4... | collective-permute-start | bytes 393224 | tf_op jit(solution)/shard_map/ppermute | solution.py:57
  18.6 20.1 %collective-permute-start.7 = (f32[64,512]{1,0:T(8,128)S(1)}, f32[64,512]{1,0:T(8,128)S(1)}, u32[]{:S(2)}, u32[]{:S(2)}) collective-permute-start(f32[64,512]{1,0:T(8,128)S(1)} %get-tuple-element.14), channel_id=1, source_target_pairs={{0,384},{64,448},{128,256},{192,320},{256,128},{320,192},{384,0},{... | collective-permute-start | bytes 393224 | tf_op jit(solution)/shard_map/ppermute | solution.py:57
  21.7 9.6 %collective-permute-start.1 = (f32[24,512]{1,0:T(8,128)S(1)}, f32[24,512]{1,0:T(8,128)S(1)}, u32[]{:S(2)}, u32[]{:S(2)}) collective-permute-start(f32[24,512]{1,0:T(8,128)S(1)} %slice_select_fusion), channel_id=1, source_target_pairs={{64,128},{128,64},{192,256},{256,192},{320,384},{384,320},{448,8},... | collective-permute-start | bytes 147464 | tf_op jit(solution)/shard_map/ppermute | solution.py:73
  24.7 3.1 %collective-permute-start = (f32[16,512]{1,0:T(8,128)S(1)}, f32[16,512]{1,0:T(8,128)S(1)}, u32[]{:S(2)}, u32[]{:S(2)}) collective-permute-start(f32[16,512]{1,0:T(8,128)S(1)} %slice_select_fusion.2), channel_id=1, source_target_pairs={{0,64},{64,0},{128,192},{192,128},{256,320},{320,256},{384,448},{4... | collective-permute-start | bytes 98312 | tf_op jit(solution)/shard_map/ppermute | solution.py:75
  31.5 10.9 %collective-permute-start.3 = (f32[32,128]{1,0:T(8,128)S(1)}, f32[32,128]{1,0:T(8,128)S(1)}, u32[]{:S(2)}, u32[]{:S(2)}) collective-permute-start(f32[32,128]{1,0:T(8,128)S(1)} %pad_maximum_fusion), channel_id=1, source_target_pairs={{1,2},{2,1},{3,4},{4,3},{5,6},{6,5},{9,10},{10,9},{11,12},{12,11},... | collective-permute-start | bytes 49160 | tf_op jit(solution)/shard_map/ppermute | solution.py:95
  36.7 2.2 %copy-start = (s32[1,64,512]{2,1,0:T(8,128)S(1)}, s32[1,64,512]{2,1,0:T(8,128)}, u32[]{:S(2)}) copy-start(s32[1,64,512]{2,1,0:T(8,128)} %param.5) | copy-start | bytes 393220
  36.7 5.7 %collective-permute-start.2 = (f32[24,128]{1,0:T(8,128)S(1)}, f32[24,128]{1,0:T(8,128)S(1)}, u32[]{:S(2)}, u32[]{:S(2)}) collective-permute-start(f32[24,128]{1,0:T(8,128)S(1)} %broadcast_select_fusion.3), channel_id=1, source_target_pairs={{0,1},{1,0},{2,3},{3,2},{4,5},{5,4},{6,7},{7,6},{8,9},{9,8},{10,11... | collective-permute-start | bytes 36872 | tf_op jit(solution)/shard_map/ppermute | solution.py:96

commit v5 on v4

--- a/solution.py
+++ b/solution.py
@@ -52,7 +52,7 @@
         return lax.dynamic_index_in_dim(value, index, 0, keepdims=False)
 
     total = share(chip)
-    for step in range(1, chips):
+    for step in (3, 2, 1):
         route = [(i, (i // 2 ^ step) * 2 + i % 2) for i in range(slabs)]
         total = total + lax.ppermute(share(chip ^ step), "slab", route)
     return total

time: 44.6 us -> 44.2 us (level)
  starting transfers between devices: 29.5 us -> 28.7 us
  waiting for transfers between devices: 7.11 us -> 7.57 us
    ppermute x3, starting transfers between devices: 10.4 us -> 9.83 us  [sum_by_swaps(): total = total + lax.ppermute(share(chip ^ step), 'slab', route)]
where the time goes in v5:
time: 44.2 us; the launch traced here: 43.8 us
  starting transfers between devices  28.7 us (65%)
  waiting for transfers between devices  7.57 us (17%)
  Pallas kernels  6.08 us (14%)
  between operations  0.94 us (2%)
    ppermute x3, starting transfers between devices, sum_by_swaps(): total = total + lax.ppermute(share(chip ^ step), 'slab', route)  9.83 us
    ppermute x1, starting transfers between devices, neighbour_columns(): far = lax.ppermute(long, 'tile', far)[:-8]  5.18 us
    all_to_all x1, starting transfers between devices, local(): lax.all_to_all(depth_layers.reshape(slabs, rows, width), 'slab', split_ax...  4.48 us
    ppermute x1, waiting for transfers between devices, neighbour_rows(): far = lax.ppermute(long, ('slab', 'tile'), across)  3.71 us
    ppermute x1, starting transfers between devices, neighbour_rows(): far = lax.ppermute(long, ('slab', 'tile'), across)  2.82 us
    ppermute x1, starting transfers between devices, pair_sum(): lax.ppermute(pick(1), 'slab', [(i, i ^ 1) for i in range(bands)])  2.41 us
    pallas_call x1, Pallas kernels, local(): pl.pallas_call(functools.partial(inner_kernel, rows, grid), compiler_para...  2.24 us
    pallas_call x2, Pallas kernels, pick(): pl.pallas_call(functools.partial(pick_kernel, flip), compiler_params=PARA...  2.11 us
  transfers between devices with their start and end apart: 9, of which 5 were waited for; matrix products, arithmetic and copies ran while one was open for 1% of the time, Pallas kernels for 10%

profile of v5, /device:TPU:288, one launch (start us, length us, event | category | flops | bytes accessed | tf_op | source)
XLA Modules:
  0.0 43.8 jit_solution(11103581434518991101)
XLA Ops:
  0.6 4.5 %all-to-all-start = ((f32[8,64,512]{2,1,0:T(8,128)}), f32[8,64,512]{2,1,0:T(8,128)S(1)}, u32[]{:S(2)}, u32[]{:S(2)}) async-start(f32[8,64,512]{2,1,0:T(8,128)} %bitcast.21), calls=%async_computation | async-start | bytes 2097152 | tf_op jit(solution)/shard_map/all_to_all | solution.py:276
  5.1 1.0 %shard_map.51 = f32[4,64,512]{2,1,0:T(8,128)S(1)} custom-call(f32[4,2,64,512]{3,2,1,0:T(8,128)} %bitcast.19), custom_call_target="tpu_custom_call" | custom-call | tf_op jit(solution)/shard_map/pallas_call | solution.py:33
  6.2 2.4 %collective-permute-start.4 = (f32[4,64,512]{2,1,0:T(8,128)S(1)}, f32[4,64,512]{2,1,0:T(8,128)S(1)}, u32[]{:S(2)}, u32[]{:S(2)}) collective-permute-start(f32[4,64,512]{2,1,0:T(8,128)S(1)} %shard_map.51), channel_id=1, source_target_pairs={{0,64},{64,0},{128,192},{192,128},{256,320},{320,256},{384,448},{4... | collective-permute-start | bytes 1572872 | tf_op jit(solution)/shard_map/ppermute | solution.py:43
  8.6 1.1 %shard_map.50 = f32[4,64,512]{2,1,0:T(8,128)S(1)} custom-call(f32[4,2,64,512]{3,2,1,0:T(8,128)} %bitcast.20), custom_call_target="tpu_custom_call" | custom-call | tf_op jit(solution)/shard_map/pallas_call | solution.py:33
  9.8 0.3 collective-permute-done.4
  10.1 0.1 add.39
  10.2 5.0 %collective-permute-start.5 = (f32[64,512]{1,0:T(8,128)S(1)}, f32[64,512]{1,0:T(8,128)S(1)}, u32[]{:S(2)}, u32[]{:S(2)}) collective-permute-start(f32[64,512]{1,0:T(8,128)S(1)} %get-tuple-element.13), channel_id=1, source_target_pairs={{0,384},{64,448},{128,256},{192,320},{256,128},{320,192},{384,0},{... | collective-permute-start | bytes 393224 | tf_op jit(solution)/shard_map/ppermute | solution.py:57
  15.3 2.8 %collective-permute-start.6 = (f32[64,512]{1,0:T(8,128)S(1)}, f32[64,512]{1,0:T(8,128)S(1)}, u32[]{:S(2)}, u32[]{:S(2)}) collective-permute-start(f32[64,512]{1,0:T(8,128)S(1)} %get-tuple-element.15), channel_id=1, source_target_pairs={{0,256},{64,320},{128,384},{192,448},{256,0},{320,64},{384,128},{4... | collective-permute-start | bytes 393224 | tf_op jit(solution)/shard_map/ppermute | solution.py:57
  18.0 2.1 %collective-permute-start.7 = (f32[64,512]{1,0:T(8,128)S(1)}, f32[64,512]{1,0:T(8,128)S(1)}, u32[]{:S(2)}, u32[]{:S(2)}) collective-permute-start(f32[64,512]{1,0:T(8,128)S(1)} %get-tuple-element.14), channel_id=1, source_target_pairs={{0,128},{64,192},{128,0},{192,64},{256,384},{320,448},{384,256},{4... | collective-permute-start | bytes 393224 | tf_op jit(solution)/shard_map/ppermute | solution.py:57
  20.1 1.1 %all-to-all-done = f32[8,64,512]{2,1,0:T(8,128)S(1)} async-done(((f32[8,64,512]{2,1,0:T(8,128)}), f32[8,64,512]{2,1,0:T(8,128)S(1)}, u32[]{:S(2)}, u32[]{:S(2)}) %all-to-all-start) | async-done | bytes 1048608 | tf_op jit(solution)/shard_map/all_to_all | solution.py:276
  21.2 0.1 reduce_min.9.band_ref
  21.3 2.8 %collective-permute-start.1 = (f32[24,512]{1,0:T(8,128)S(1)}, f32[24,512]{1,0:T(8,128)S(1)}, u32[]{:S(2)}, u32[]{:S(2)}) collective-permute-start(f32[24,512]{1,0:T(8,128)S(1)} %slice_select_fusion), channel_id=1, source_target_pairs={{64,128},{128,64},{192,256},{256,192},{320,384},{384,320},{448,8},... | collective-permute-start | bytes 147464 | tf_op jit(solution)/shard_map/ppermute | solution.py:73
  24.1 1.9 %collective-permute-start = (f32[16,512]{1,0:T(8,128)S(1)}, f32[16,512]{1,0:T(8,128)S(1)}, u32[]{:S(2)}, u32[]{:S(2)}) collective-permute-start(f32[16,512]{1,0:T(8,128)S(1)} %slice_select_fusion.2), channel_id=1, source_target_pairs={{0,64},{64,0},{128,192},{192,128},{256,320},{320,256},{384,448},{4... | collective-permute-start | bytes 98312 | tf_op jit(solution)/shard_map/ppermute | solution.py:75
  26.1 0.1 fusion.10
  26.2 1.1 %collective-permute-done = f32[16,512]{1,0:T(8,128)S(1)} collective-permute-done((f32[16,512]{1,0:T(8,128)S(1)}, f32[16,512]{1,0:T(8,128)S(1)}, u32[]{:S(2)}, u32[]{:S(2)}) %collective-permute-start) | collective-permute-done | bytes 32800 | tf_op jit(solution)/shard_map/ppermute | solution.py:75
  27.2 3.7 %collective-permute-done.1 = f32[24,512]{1,0:T(8,128)S(1)} collective-permute-done((f32[24,512]{1,0:T(8,128)S(1)}, f32[24,512]{1,0:T(8,128)S(1)}, u32[]{:S(2)}, u32[]{:S(2)}) %collective-permute-start.1) | collective-permute-done | bytes 49184 | tf_op jit(solution)/shard_map/ppermute | solution.py:73
  31.0 0.1 broadcast_select_fusion.2
  31.1 5.2 %collective-permute-start.3 = (f32[32,128]{1,0:T(8,128)S(1)}, f32[32,128]{1,0:T(8,128)S(1)}, u32[]{:S(2)}, u32[]{:S(2)}) collective-permute-start(f32[32,128]{1,0:T(8,128)S(1)} %pad_maximum_fusion), channel_id=1, source_target_pairs={{1,2},{2,1},{3,4},{4,3},{5,6},{6,5},{9,10},{10,9},{11,12},{12,11},... | collective-permute-start | bytes 49160 | tf_op jit(solution)/shard_map/ppermute | solution.py:95
  36.3 0.0 copy-start
  36.3 2.1 %collective-permute-start.2 = (f32[24,128]{1,0:T(8,128)S(1)}, f32[24,128]{1,0:T(8,128)S(1)}, u32[]{:S(2)}, u32[]{:S(2)}) collective-permute-start(f32[24,128]{1,0:T(8,128)S(1)} %broadcast_select_fusion.3), channel_id=1, source_target_pairs={{0,1},{1,0},{2,3},{3,2},{4,5},{5,4},{6,7},{7,6},{8,9},{9,8},{10,11... | collective-permute-start | bytes 36872 | tf_op jit(solution)/shard_map/ppermute | solution.py:96
  38.4 0.0 collective-permute-done.5
  38.4 0.0 collective-permute-done.6
  38.4 0.0 collective-permute-done.7
  38.4 0.0 copy-done
  38.5 2.2 %shard_map.52 = (f32[64,512]{1,0:T(8,128)S(1)}, f32[64,512]{1,0:T(8,128)S(1)}) custom-call(f32[16,512]{1,0:T(8,128)S(1)} %get-tuple-element.23.above_ref, f32[64,512]{1,0:T(8,128)S(1)} %reduce_min.9.band_ref, f32[16,512]{1,0:T(8,128)S(1)} %get-tuple-element.22.below_ref, f32[64,512]{1,0:T(8,128)S(1)} %fusion.1.thick_ref, s32[64,512]{1,0:T(8,128)S(1)} %bitcast.17), custom_call_target="tpu_custom_call" | custom-call | tf_op jit(solution)/shard_map/pallas_call | solution.py:298
  40.7 1.3 %collective-permute-done.2 = f32[24,128]{1,0:T(8,128)S(1)} collective-permute-done((f32[24,128]{1,0:T(8,128)S(1)}, f32[24,128]{1,0:T(8,128)S(1)}, u32[]{:S(2)}, u32[]{:S(2)}) %collective-permute-start.2) | collective-permute-done | bytes 12320 | tf_op jit(solution)/shard_map/ppermute | solution.py:96
  42.0 0.0 collective-permute-done.3
  42.0 1.7 %shard_map.53 = (f32[64,512]{1,0:T(8,128)}, f32[64,512]{1,0:T(8,128)}) custom-call(f32[16,512]{1,0:T(8,128)S(1)} %get-tuple-element.23.above_ref, f32[64,512]{1,0:T(8,128)S(1)} %reduce_min.9.band_ref, f32[16,512]{1,0:T(8,128)S(1)} %get-tuple-element.22.below_ref, f32[24,128]{1,0:T(8,128)S(1)} %get-tuple-element.29.left_ref, ...), custom_call_target="tpu_custom_call" | custom-call | tf_op jit(solution)/shard_map/pallas_call | solution.py:307
  (11 shorter events, 0.1 us)
Async XLA Ops:
  0.6 20.6 %all-to-all-start = ((f32[8,64,512]{2,1,0:T(8,128)}), f32[8,64,512]{2,1,0:T(8,128)S(1)}, u32[]{:S(2)}, u32[]{:S(2)}) async-start(f32[8,64,512]{2,1,0:T(8,128)} %bitcast.21), calls=%async_computation | async-start | bytes 2097152 | tf_op jit(solution)/shard_map/all_to_all | solution.py:276
  6.2 3.9 %collective-permute-start.4 = (f32[4,64,512]{2,1,0:T(8,128)S(1)}, f32[4,64,512]{2,1,0:T(8,128)S(1)}, u32[]{:S(2)}, u32[]{:S(2)}) collective-permute-start(f32[4,64,512]{2,1,0:T(8,128)S(1)} %shard_map.51), channel_id=1, source_target_pairs={{0,64},{64,0},{128,192},{192,128},{256,320},{320,256},{384,448},{4... | collective-permute-start | bytes 1572872 | tf_op jit(solution)/shard_map/ppermute | solution.py:43
  10.2 28.1 %collective-permute-start.5 = (f32[64,512]{1,0:T(8,128)S(1)}, f32[64,512]{1,0:T(8,128)S(1)}, u32[]{:S(2)}, u32[]{:S(2)}) collective-permute-start(f32[64,512]{1,0:T(8,128)S(1)} %get-tuple-element.13), channel_id=1, source_target_pairs={{0,384},{64,448},{128,256},{192,320},{256,128},{320,192},{384,0},{... | collective-permute-start | bytes 393224 | tf_op jit(solution)/shard_map/ppermute | solution.py:57
  15.3 23.1 %collective-permute-start.6 = (f32[64,512]{1,0:T(8,128)S(1)}, f32[64,512]{1,0:T(8,128)S(1)}, u32[]{:S(2)}, u32[]{:S(2)}) collective-permute-start(f32[64,512]{1,0:T(8,128)S(1)} %get-tuple-element.15), channel_id=1, source_target_pairs={{0,256},{64,320},{128,384},{192,448},{256,0},{320,64},{384,128},{4... | collective-permute-start | bytes 393224 | tf_op jit(solution)/shard_map/ppermute | solution.py:57
  18.0 20.4 %collective-permute-start.7 = (f32[64,512]{1,0:T(8,128)S(1)}, f32[64,512]{1,0:T(8,128)S(1)}, u32[]{:S(2)}, u32[]{:S(2)}) collective-permute-start(f32[64,512]{1,0:T(8,128)S(1)} %get-tuple-element.14), channel_id=1, source_target_pairs={{0,128},{64,192},{128,0},{192,64},{256,384},{320,448},{384,256},{4... | collective-permute-start | bytes 393224 | tf_op jit(solution)/shard_map/ppermute | solution.py:57
  21.3 9.6 %collective-permute-start.1 = (f32[24,512]{1,0:T(8,128)S(1)}, f32[24,512]{1,0:T(8,128)S(1)}, u32[]{:S(2)}, u32[]{:S(2)}) collective-permute-start(f32[24,512]{1,0:T(8,128)S(1)} %slice_select_fusion), channel_id=1, source_target_pairs={{64,128},{128,64},{192,256},{256,192},{320,384},{384,320},{448,8},... | collective-permute-start | bytes 147464 | tf_op jit(solution)/shard_map/ppermute | solution.py:73
  24.1 3.1 %collective-permute-start = (f32[16,512]{1,0:T(8,128)S(1)}, f32[16,512]{1,0:T(8,128)S(1)}, u32[]{:S(2)}, u32[]{:S(2)}) collective-permute-start(f32[16,512]{1,0:T(8,128)S(1)} %slice_select_fusion.2), channel_id=1, source_target_pairs={{0,64},{64,0},{128,192},{192,128},{256,320},{320,256},{384,448},{4... | collective-permute-start | bytes 98312 | tf_op jit(solution)/shard_map/ppermute | solution.py:75
  31.1 10.9 %collective-permute-start.3 = (f32[32,128]{1,0:T(8,128)S(1)}, f32[32,128]{1,0:T(8,128)S(1)}, u32[]{:S(2)}, u32[]{:S(2)}) collective-permute-start(f32[32,128]{1,0:T(8,128)S(1)} %pad_maximum_fusion), channel_id=1, source_target_pairs={{1,2},{2,1},{3,4},{4,3},{5,6},{6,5},{9,10},{10,9},{11,12},{12,11},... | collective-permute-start | bytes 49160 | tf_op jit(solution)/shard_map/ppermute | solution.py:95
  36.3 2.2 %copy-start = (s32[1,64,512]{2,1,0:T(8,128)S(1)}, s32[1,64,512]{2,1,0:T(8,128)}, u32[]{:S(2)}) copy-start(s32[1,64,512]{2,1,0:T(8,128)} %param.5) | copy-start | bytes 393220
  36.3 5.7 %collective-permute-start.2 = (f32[24,128]{1,0:T(8,128)S(1)}, f32[24,128]{1,0:T(8,128)S(1)}, u32[]{:S(2)}, u32[]{:S(2)}) collective-permute-start(f32[24,128]{1,0:T(8,128)S(1)} %broadcast_select_fusion.3), channel_id=1, source_target_pairs={{0,1},{1,0},{2,3},{3,2},{4,5},{5,4},{6,7},{7,6},{8,9},{9,8},{10,11... | collective-permute-start | bytes 36872 | tf_op jit(solution)/shard_map/ppermute | solution.py:96

commit v6 on v5

--- a/solution.py
+++ b/solution.py
@@ -69,9 +69,9 @@
                 across += [(upper, lower), (lower, upper)]
     odd = core == 1
     head, tail = band[:PAD], band[-PAD:]
-    long = jnp.where(odd, band[-PAD - 8 :], band[: PAD + 8])
-    far = lax.ppermute(long, ("slab", "tile"), across)
-    far = jnp.where(odd, far[:PAD], far[8:])
+    long = jnp.where(odd, tail, head)
+    long = jnp.concatenate([long, long[:, :LANES]], axis=1)
+    far = lax.ppermute(long, ("slab", "tile"), across)[:, :-LANES]
     near = lax.ppermute(jnp.where(odd, head, tail), "slab", [(i, i ^ 1) for i in range(slabs)])
     return far, near
 
@@ -170,8 +170,47 @@
         each(8, total // 8 - 2, groups[1], move)
         return carry
 
-    lax.fori_loop(0, SWEEPS, sweep, 0)
-    each(0, rows // 8, groups[2], lambda r: finish(r, *slopes(top + r)))
+    if pieces > 1:
+        lax.fori_loop(0, SWEEPS, sweep, 0)
+        each(0, rows // 8, groups[2], lambda r: finish(r, *slopes(top + r)))
+        return
+
+    strips = list(range(8, total - 8, 8))
+
+    def steps(values, above, below):
+        up = {r: pltpu.roll(values[r], 7, 0) for r in values}
+        down = {r: pltpu.roll(values[r], 1, 0) for r in values}
+        out = {}
+        for r in strips:
+            under = jnp.where(last_row, up.get(r + 8, up[r]), up[r])
+            over = jnp.where(first_row, down.get(r - 8, down[r]), down[r])
+            if r == bottom - 8:
+                under = jnp.where(last_row & bottom_edge, below(values[r]), under)
+            if r == top:
+                over = jnp.where(first_row & top_edge, above(values[r]), over)
+            out[r] = under - over
+        return out
+
+    def sweep_block(i, carry):
+        values = dict(zip(range(0, total, 8), carry))
+        wide_y = steps(values, lambda v: v, lambda v: v)
+        upright, moved = {}, {}
+        for r in strips:
+            (wide_x,) = across([values[r]], values[r], values[r])
+            inverse = lax.rsqrt(1.0 + 0.25 * (wide_x * wide_x + wide_y[r] * wide_y[r]))
+            upright[r] = wide_y[r] * inverse
+            moved[r] = values[r] + (0.25 * FLOW_STEP) * across([wide_x * inverse], zero, zero)[0]
+        rise = steps(upright, lambda v: zero, lambda v: zero)
+        for r in strips:
+            values[r] = moved[r] + (0.25 * FLOW_STEP) * rise[r]
+        return tuple(values[r] for r in range(0, total, 8))
+
+    start = tuple(surface[0, r : r + 8, :] for r in range(0, total, 8))
+    values = dict(zip(range(0, total, 8), lax.fori_loop(0, SWEEPS, sweep_block, start)))
+    wide_y = steps(values, lambda v: v, lambda v: v)
+    for r in range(0, rows, 8):
+        here = values[top + r]
+        finish(r, [here], across([here], here, here), [wide_y[top + r]])
 
 
 def shaded(wide_x, wide_y, layers, cover):

time: 44.2 us -> 44 us (level)
  the two profiles are of different devices: /device:TPU:288 before, /device:TPU:416 now
where the time goes in v6:
time: 44 us; the launch traced here: 43.6 us
  starting transfers between devices  30.7 us (70%)
  Pallas kernels  6.05 us (14%)
  waiting for transfers between devices  5.37 us (12%)
  between operations  0.95 us (2%)
    ppermute x3, starting transfers between devices, sum_by_swaps(): total = total + lax.ppermute(share(chip ^ step), 'slab', route)  9.83 us
    ppermute x1, starting transfers between devices, neighbour_columns(): far = lax.ppermute(long, 'tile', far)[:-8]  5.11 us
    ppermute x1, starting transfers between devices, neighbour_rows(): far = lax.ppermute(long, ('slab', 'tile'), across)[:, :-LANES]  4.93 us
    all_to_all x1, starting transfers between devices, local(): lax.all_to_all(depth_layers.reshape(slabs, rows, width), 'slab', split_ax...  4.48 us
    ppermute x1, starting transfers between devices, pair_sum(): lax.ppermute(pick(1), 'slab', [(i, i ^ 1) for i in range(bands)])  2.41 us
    pallas_call x1, Pallas kernels, local(): pl.pallas_call(functools.partial(inner_kernel, rows, grid), compiler_para...  2.24 us
    pallas_call x2, Pallas kernels, pick(): pl.pallas_call(functools.partial(pick_kernel, flip), compiler_params=PARA...  2.11 us
    ppermute x1, starting transfers between devices, neighbour_columns(): near = lax.ppermute(jnp.where(odd, first, last), 'tile', near)  2.05 us
  transfers between devices with their start and end apart: 9, of which 5 were waited for; matrix products, arithmetic and copies ran while one was open for 1% of the time, Pallas kernels for 10%

profile of v6, /device:TPU:416, one launch (start us, length us, event | category | flops | bytes accessed | tf_op | source)
XLA Modules:
  0.0 43.6 jit_solution(1386273167903722327)
XLA Ops:
  0.6 4.5 %all-to-all-start = ((f32[8,64,512]{2,1,0:T(8,128)}), f32[8,64,512]{2,1,0:T(8,128)S(1)}, u32[]{:S(2)}, u32[]{:S(2)}) async-start(f32[8,64,512]{2,1,0:T(8,128)} %bitcast.21), calls=%async_computation | async-start | bytes 2097152 | tf_op jit(solution)/shard_map/all_to_all | solution.py:315
  5.1 1.0 %shard_map.51 = f32[4,64,512]{2,1,0:T(8,128)S(1)} custom-call(f32[4,2,64,512]{3,2,1,0:T(8,128)} %bitcast.19), custom_call_target="tpu_custom_call" | custom-call | tf_op jit(solution)/shard_map/pallas_call | solution.py:33
  6.2 2.4 %collective-permute-start.4 = (f32[4,64,512]{2,1,0:T(8,128)S(1)}, f32[4,64,512]{2,1,0:T(8,128)S(1)}, u32[]{:S(2)}, u32[]{:S(2)}) collective-permute-start(f32[4,64,512]{2,1,0:T(8,128)S(1)} %shard_map.51), channel_id=1, source_target_pairs={{0,64},{64,0},{128,192},{192,128},{256,320},{320,256},{384,448},{4... | collective-permute-start | bytes 1572872 | tf_op jit(solution)/shard_map/ppermute | solution.py:43
  8.6 1.1 %shard_map.50 = f32[4,64,512]{2,1,0:T(8,128)S(1)} custom-call(f32[4,2,64,512]{3,2,1,0:T(8,128)} %bitcast.20), custom_call_target="tpu_custom_call" | custom-call | tf_op jit(solution)/shard_map/pallas_call | solution.py:33
  9.8 0.3 collective-permute-done.4
  10.1 0.1 add.39
  10.2 5.0 %collective-permute-start.5 = (f32[64,512]{1,0:T(8,128)S(1)}, f32[64,512]{1,0:T(8,128)S(1)}, u32[]{:S(2)}, u32[]{:S(2)}) collective-permute-start(f32[64,512]{1,0:T(8,128)S(1)} %get-tuple-element.13), channel_id=1, source_target_pairs={{0,384},{64,448},{128,256},{192,320},{256,128},{320,192},{384,0},{... | collective-permute-start | bytes 393224 | tf_op jit(solution)/shard_map/ppermute | solution.py:57
  15.3 2.8 %collective-permute-start.6 = (f32[64,512]{1,0:T(8,128)S(1)}, f32[64,512]{1,0:T(8,128)S(1)}, u32[]{:S(2)}, u32[]{:S(2)}) collective-permute-start(f32[64,512]{1,0:T(8,128)S(1)} %get-tuple-element.15), channel_id=1, source_target_pairs={{0,256},{64,320},{128,384},{192,448},{256,0},{320,64},{384,128},{4... | collective-permute-start | bytes 393224 | tf_op jit(solution)/shard_map/ppermute | solution.py:57
  18.0 2.1 %collective-permute-start.7 = (f32[64,512]{1,0:T(8,128)S(1)}, f32[64,512]{1,0:T(8,128)S(1)}, u32[]{:S(2)}, u32[]{:S(2)}) collective-permute-start(f32[64,512]{1,0:T(8,128)S(1)} %get-tuple-element.14), channel_id=1, source_target_pairs={{0,128},{64,192},{128,0},{192,64},{256,384},{320,448},{384,256},{4... | collective-permute-start | bytes 393224 | tf_op jit(solution)/shard_map/ppermute | solution.py:57
  20.1 1.1 %all-to-all-done = f32[8,64,512]{2,1,0:T(8,128)S(1)} async-done(((f32[8,64,512]{2,1,0:T(8,128)}), f32[8,64,512]{2,1,0:T(8,128)S(1)}, u32[]{:S(2)}, u32[]{:S(2)}) %all-to-all-start) | async-done | bytes 1048608 | tf_op jit(solution)/shard_map/all_to_all | solution.py:315
  21.2 0.1 reduce_min.9.band_ref
  21.3 4.9 %collective-permute-start.1 = (f32[16,640]{1,0:T(8,128)S(1)}, f32[16,640]{1,0:T(8,128)S(1)}, u32[]{:S(2)}, u32[]{:S(2)}) collective-permute-start(f32[16,640]{1,0:T(8,128)S(1)} %pad_maximum_fusion), channel_id=1, source_target_pairs={{64,128},{128,64},{192,256},{256,192},{320,384},{384,320},{448,8},... | collective-permute-start | bytes 122888 | tf_op jit(solution)/shard_map/ppermute | solution.py:74
  26.3 1.9 %collective-permute-start = (f32[16,512]{1,0:T(8,128)S(1)}, f32[16,512]{1,0:T(8,128)S(1)}, u32[]{:S(2)}, u32[]{:S(2)}) collective-permute-start(f32[16,512]{1,0:T(8,128)S(1)} %get-tuple-element.23), channel_id=1, source_target_pairs={{0,64},{64,0},{128,192},{192,128},{256,320},{320,256},{384,448},{4... | collective-permute-start | bytes 98312 | tf_op jit(solution)/shard_map/ppermute | solution.py:75
  28.2 0.1 fusion.10
  28.3 1.1 %collective-permute-done = f32[16,512]{1,0:T(8,128)S(1)} collective-permute-done((f32[16,512]{1,0:T(8,128)S(1)}, f32[16,512]{1,0:T(8,128)S(1)}, u32[]{:S(2)}, u32[]{:S(2)}) %collective-permute-start) | collective-permute-done | bytes 32800 | tf_op jit(solution)/shard_map/ppermute | solution.py:75
  29.4 1.5 %collective-permute-done.1 = f32[16,640]{1,0:T(8,128)S(1)} collective-permute-done((f32[16,640]{1,0:T(8,128)S(1)}, f32[16,640]{1,0:T(8,128)S(1)}, u32[]{:S(2)}, u32[]{:S(2)}) %collective-permute-start.1) | collective-permute-done | bytes 40992 | tf_op jit(solution)/shard_map/ppermute | solution.py:74
  30.9 0.1 broadcast_select_fusion
  31.0 5.1 %collective-permute-start.3 = (f32[32,128]{1,0:T(8,128)S(1)}, f32[32,128]{1,0:T(8,128)S(1)}, u32[]{:S(2)}, u32[]{:S(2)}) collective-permute-start(f32[32,128]{1,0:T(8,128)S(1)} %pad_maximum_fusion.1), channel_id=1, source_target_pairs={{1,2},{2,1},{3,4},{4,3},{5,6},{6,5},{9,10},{10,9},{11,12},{12,11},... | collective-permute-start | bytes 49160 | tf_op jit(solution)/shard_map/ppermute | solution.py:95
  36.1 0.0 copy-start
  36.1 2.1 %collective-permute-start.2 = (f32[24,128]{1,0:T(8,128)S(1)}, f32[24,128]{1,0:T(8,128)S(1)}, u32[]{:S(2)}, u32[]{:S(2)}) collective-permute-start(f32[24,128]{1,0:T(8,128)S(1)} %broadcast_select_fusion.1), channel_id=1, source_target_pairs={{0,1},{1,0},{2,3},{3,2},{4,5},{5,4},{6,7},{7,6},{8,9},{9,8},{10,11... | collective-permute-start | bytes 36872 | tf_op jit(solution)/shard_map/ppermute | solution.py:96
  38.2 0.0 collective-permute-done.5
  38.2 0.0 collective-permute-done.6
  38.2 0.0 collective-permute-done.7
  38.3 0.0 copy-done
  38.3 2.2 %shard_map.52 = (f32[64,512]{1,0:T(8,128)S(1)}, f32[64,512]{1,0:T(8,128)S(1)}) custom-call(f32[16,512]{1,0:T(8,128)S(1)} %get-tuple-element.25.above_ref, f32[64,512]{1,0:T(8,128)S(1)} %reduce_min.9.band_ref, f32[16,512]{1,0:T(8,128)S(1)} %get-tuple-element.24.below_ref, f32[64,512]{1,0:T(8,128)S(1)} %fusion.1.thick_ref, s32[64,512]{1,0:T(8,128)S(1)} %bitcast.17), custom_call_target="tpu_custom_call" | custom-call | tf_op jit(solution)/shard_map/pallas_call | solution.py:337
  40.5 1.3 %collective-permute-done.2 = f32[24,128]{1,0:T(8,128)S(1)} collective-permute-done((f32[24,128]{1,0:T(8,128)S(1)}, f32[24,128]{1,0:T(8,128)S(1)}, u32[]{:S(2)}, u32[]{:S(2)}) %collective-permute-start.2) | collective-permute-done | bytes 12320 | tf_op jit(solution)/shard_map/ppermute | solution.py:96
  41.9 0.0 collective-permute-done.3
  41.9 1.7 %shard_map.53 = (f32[64,512]{1,0:T(8,128)}, f32[64,512]{1,0:T(8,128)}) custom-call(f32[16,512]{1,0:T(8,128)S(1)} %get-tuple-element.25.above_ref, f32[64,512]{1,0:T(8,128)S(1)} %reduce_min.9.band_ref, f32[16,512]{1,0:T(8,128)S(1)} %get-tuple-element.24.below_ref, f32[24,128]{1,0:T(8,128)S(1)} %get-tuple-element.31.left_ref, ...), custom_call_target="tpu_custom_call" | custom-call | tf_op jit(solution)/shard_map/pallas_call | solution.py:346
  (12 shorter events, 0.1 us)
Async XLA Ops:
  0.6 20.6 %all-to-all-start = ((f32[8,64,512]{2,1,0:T(8,128)}), f32[8,64,512]{2,1,0:T(8,128)S(1)}, u32[]{:S(2)}, u32[]{:S(2)}) async-start(f32[8,64,512]{2,1,0:T(8,128)} %bitcast.21), calls=%async_computation | async-start | bytes 2097152 | tf_op jit(solution)/shard_map/all_to_all | solution.py:315
  6.2 3.9 %collective-permute-start.4 = (f32[4,64,512]{2,1,0:T(8,128)S(1)}, f32[4,64,512]{2,1,0:T(8,128)S(1)}, u32[]{:S(2)}, u32[]{:S(2)}) collective-permute-start(f32[4,64,512]{2,1,0:T(8,128)S(1)} %shard_map.51), channel_id=1, source_target_pairs={{0,64},{64,0},{128,192},{192,128},{256,320},{320,256},{384,448},{4... | collective-permute-start | bytes 1572872 | tf_op jit(solution)/shard_map/ppermute | solution.py:43
  10.2 28.0 %collective-permute-start.5 = (f32[64,512]{1,0:T(8,128)S(1)}, f32[64,512]{1,0:T(8,128)S(1)}, u32[]{:S(2)}, u32[]{:S(2)}) collective-permute-start(f32[64,512]{1,0:T(8,128)S(1)} %get-tuple-element.13), channel_id=1, source_target_pairs={{0,384},{64,448},{128,256},{192,320},{256,128},{320,192},{384,0},{... | collective-permute-start | bytes 393224 | tf_op jit(solution)/shard_map/ppermute | solution.py:57
  15.3 23.0 %collective-permute-start.6 = (f32[64,512]{1,0:T(8,128)S(1)}, f32[64,512]{1,0:T(8,128)S(1)}, u32[]{:S(2)}, u32[]{:S(2)}) collective-permute-start(f32[64,512]{1,0:T(8,128)S(1)} %get-tuple-element.15), channel_id=1, source_target_pairs={{0,256},{64,320},{128,384},{192,448},{256,0},{320,64},{384,128},{4... | collective-permute-start | bytes 393224 | tf_op jit(solution)/shard_map/ppermute | solution.py:57
  18.0 20.2 %collective-permute-start.7 = (f32[64,512]{1,0:T(8,128)S(1)}, f32[64,512]{1,0:T(8,128)S(1)}, u32[]{:S(2)}, u32[]{:S(2)}) collective-permute-start(f32[64,512]{1,0:T(8,128)S(1)} %get-tuple-element.14), channel_id=1, source_target_pairs={{0,128},{64,192},{128,0},{192,64},{256,384},{320,448},{384,256},{4... | collective-permute-start | bytes 393224 | tf_op jit(solution)/shard_map/ppermute | solution.py:57
  21.3 9.5 %collective-permute-start.1 = (f32[16,640]{1,0:T(8,128)S(1)}, f32[16,640]{1,0:T(8,128)S(1)}, u32[]{:S(2)}, u32[]{:S(2)}) collective-permute-start(f32[16,640]{1,0:T(8,128)S(1)} %pad_maximum_fusion), channel_id=1, source_target_pairs={{64,128},{128,64},{192,256},{256,192},{320,384},{384,320},{448,8},... | collective-permute-start | bytes 122888 | tf_op jit(solution)/shard_map/ppermute | solution.py:74
  26.3 3.1 %collective-permute-start = (f32[16,512]{1,0:T(8,128)S(1)}, f32[16,512]{1,0:T(8,128)S(1)}, u32[]{:S(2)}, u32[]{:S(2)}) collective-permute-start(f32[16,512]{1,0:T(8,128)S(1)} %get-tuple-element.23), channel_id=1, source_target_pairs={{0,64},{64,0},{128,192},{192,128},{256,320},{320,256},{384,448},{4... | collective-permute-start | bytes 98312 | tf_op jit(solution)/shard_map/ppermute | solution.py:75
  31.0 10.9 %collective-permute-start.3 = (f32[32,128]{1,0:T(8,128)S(1)}, f32[32,128]{1,0:T(8,128)S(1)}, u32[]{:S(2)}, u32[]{:S(2)}) collective-permute-start(f32[32,128]{1,0:T(8,128)S(1)} %pad_maximum_fusion.1), channel_id=1, source_target_pairs={{1,2},{2,1},{3,4},{4,3},{5,6},{6,5},{9,10},{10,9},{11,12},{12,11},... | collective-permute-start | bytes 49160 | tf_op jit(solution)/shard_map/ppermute | solution.py:95
  36.1 2.2 %copy-start = (s32[1,64,512]{2,1,0:T(8,128)S(1)}, s32[1,64,512]{2,1,0:T(8,128)}, u32[]{:S(2)}) copy-start(s32[1,64,512]{2,1,0:T(8,128)} %param.5) | copy-start | bytes 393220
  36.1 5.7 %collective-permute-start.2 = (f32[24,128]{1,0:T(8,128)S(1)}, f32[24,128]{1,0:T(8,128)S(1)}, u32[]{:S(2)}, u32[]{:S(2)}) collective-permute-start(f32[24,128]{1,0:T(8,128)S(1)} %broadcast_select_fusion.1), channel_id=1, source_target_pairs={{0,1},{1,0},{2,3},{3,2},{4,5},{5,4},{6,7},{7,6},{8,9},{9,8},{10,11... | collective-permute-start | bytes 36872 | tf_op jit(solution)/shard_map/ppermute | solution.py:96

commit v7 on v6

--- a/solution.py
+++ b/solution.py
@@ -258,6 +258,8 @@
     inner_shade_ref,
     smooth_ref,
     shade_ref,
+    ends,
+    sems,
     *scratch,
 ):
     surface = scratch[0]
@@ -283,9 +285,14 @@
         at_right = jnp.where(lane < quarter, pltpu.roll(own(r, blocks - 1), quarter, 1), right)
         at_left = jnp.where(lane < 3 * quarter, left, pltpu.roll(own(r, 0), 3 * quarter, 1))
         surface[0, r : r + 8, :] = jnp.where(low, at_right, at_left)
+    inner_refs, out_refs = (inner_smooth_ref, inner_shade_ref), (smooth_ref, shade_ref)
     middle = pl.ds(LANES, (blocks - 2) * LANES)
-    smooth_ref[:, middle] = inner_smooth_ref[:, middle]
-    shade_ref[:, middle] = inner_shade_ref[:, middle]
+    copies = [
+        pltpu.make_async_copy(a.at[:, middle], b.at[:, middle], sems.at[2, k])
+        for k, (a, b) in enumerate(zip(inner_refs, out_refs))
+    ]
+    for copy in copies:
+        copy.start()
     outer = (
         (0, quarter, lane < quarter // 2),
         (blocks - 1, 3 * quarter, lane >= LANES - quarter // 2),
@@ -293,14 +300,22 @@
 
     def finish(r, here, wide_x, wide_y):
         span = pl.ds(r, 8)
-        for block, shift, new in outer:
+        for end, (block, shift, new) in enumerate(outer):
             cols = pl.ds(block * LANES, LANES)
             smooth, x, y = (pltpu.roll(a[0], shift, 1) for a in (here, wide_x, wide_y))
             shade = shaded(x, y, [thick_ref[span, cols]], cover_ref[span, cols])
-            smooth_ref[span, cols] = jnp.where(new, smooth, inner_smooth_ref[span, cols])
-            shade_ref[span, cols] = jnp.where(new, shade, inner_shade_ref[span, cols])
+            ends[0, end, span, :] = jnp.where(new, smooth, inner_smooth_ref[span, cols])
+            ends[1, end, span, :] = jnp.where(new, shade, inner_shade_ref[span, cols])
 
     flow(rows, grid, 1, (0, quarter - 1), (0, 3 * quarter), (10, 10, 8), *scratch, finish)
+    for k, ref in enumerate(out_refs):
+        for end, (block, _, _) in enumerate(outer):
+            cols = pl.ds(block * LANES, LANES)
+            copy = pltpu.make_async_copy(ends.at[k, end], ref.at[:, cols], sems.at[end, k])
+            copy.start()
+            copies.append(copy)
+    for copy in copies:
+        copy.wait()
 
 
 def local(depth_layers, thickness_layers, coverage):
@@ -348,8 +363,12 @@
         compiler_params=PARAMS,
         out_shape=(out, out),
         in_specs=[vmem] * 9,
-        out_specs=(vmem, vmem),
-        scratch_shapes=[pltpu.VMEM((1, total, LANES), jnp.float32)] * 3,
+        out_specs=(pl.BlockSpec(memory_space=pltpu.HBM),) * 2,
+        scratch_shapes=[
+            pltpu.VMEM((2, 2, rows, LANES), jnp.float32),
+            pltpu.SemaphoreType.DMA((3, 2)),
+            *[pltpu.VMEM((1, total, LANES), jnp.float32)] * 3,
+        ],
     )(
         above,
         band,

time: 44 us -> 44 us (level)
  the two profiles are of different devices: /device:TPU:416 before, /device:TPU:288 now
where the time goes in v7:
time: 44 us; the launch traced here: 43.6 us
  starting transfers between devices  28.6 us (65%)
  waiting for transfers between devices  7.47 us (17%)
  Pallas kernels  6.06 us (14%)
  between operations  0.95 us (2%)
    ppermute x3, starting transfers between devices, sum_by_swaps(): total = total + lax.ppermute(share(chip ^ step), 'slab', route)  9.83 us
    ppermute x1, starting transfers between devices, neighbour_columns(): far = lax.ppermute(long, 'tile', far)[:-8]  5.11 us
    all_to_all x1, starting transfers between devices, local(): lax.all_to_all(depth_layers.reshape(slabs, rows, width), 'slab', split_ax...  4.48 us
    ppermute x1, waiting for transfers between devices, neighbour_rows(): far = lax.ppermute(long, ('slab', 'tile'), across)[:, :-LANES]  3.61 us
    ppermute x1, starting transfers between devices, neighbour_rows(): far = lax.ppermute(long, ('slab', 'tile'), across)[:, :-LANES]  2.82 us
    ppermute x1, starting transfers between devices, pair_sum(): lax.ppermute(pick(1), 'slab', [(i, i ^ 1) for i in range(bands)])  2.41 us
    pallas_call x1, Pallas kernels, local(): pl.pallas_call(functools.partial(inner_kernel, rows, grid), compiler_para...  2.24 us
    pallas_call x2, Pallas kernels, pick(): pl.pallas_call(functools.partial(pick_kernel, flip), compiler_params=PARA...  2.11 us
  transfers between devices with their start and end apart: 9, of which 5 were waited for; matrix products, arithmetic and copies ran while one was open for 1% of the time, Pallas kernels for 10%

profile of v7, /device:TPU:288, one launch (start us, length us, event | category | flops | bytes accessed | tf_op | source)
XLA Modules:
  0.0 43.6 jit_solution(933807201283999320)
XLA Ops:
  0.6 4.5 %all-to-all-start = ((f32[8,64,512]{2,1,0:T(8,128)}), f32[8,64,512]{2,1,0:T(8,128)S(1)}, u32[]{:S(2)}, u32[]{:S(2)}) async-start(f32[8,64,512]{2,1,0:T(8,128)} %bitcast.21), calls=%async_computation | async-start | bytes 2097152 | tf_op jit(solution)/shard_map/all_to_all | solution.py:330
  5.1 1.0 %shard_map.51 = f32[4,64,512]{2,1,0:T(8,128)S(1)} custom-call(f32[4,2,64,512]{3,2,1,0:T(8,128)} %bitcast.19), custom_call_target="tpu_custom_call" | custom-call | tf_op jit(solution)/shard_map/pallas_call | solution.py:33
  6.2 2.4 %collective-permute-start.4 = (f32[4,64,512]{2,1,0:T(8,128)S(1)}, f32[4,64,512]{2,1,0:T(8,128)S(1)}, u32[]{:S(2)}, u32[]{:S(2)}) collective-permute-start(f32[4,64,512]{2,1,0:T(8,128)S(1)} %shard_map.51), channel_id=1, source_target_pairs={{0,64},{64,0},{128,192},{192,128},{256,320},{320,256},{384,448},{4... | collective-permute-start | bytes 1572872 | tf_op jit(solution)/shard_map/ppermute | solution.py:43
  8.6 1.1 %shard_map.50 = f32[4,64,512]{2,1,0:T(8,128)S(1)} custom-call(f32[4,2,64,512]{3,2,1,0:T(8,128)} %bitcast.20), custom_call_target="tpu_custom_call" | custom-call | tf_op jit(solution)/shard_map/pallas_call | solution.py:33
  9.8 0.3 collective-permute-done.4
  10.1 0.1 add.39
  10.2 5.0 %collective-permute-start.5 = (f32[64,512]{1,0:T(8,128)S(1)}, f32[64,512]{1,0:T(8,128)S(1)}, u32[]{:S(2)}, u32[]{:S(2)}) collective-permute-start(f32[64,512]{1,0:T(8,128)S(1)} %get-tuple-element.13), channel_id=1, source_target_pairs={{0,384},{64,448},{128,256},{192,320},{256,128},{320,192},{384,0},{... | collective-permute-start | bytes 393224 | tf_op jit(solution)/shard_map/ppermute | solution.py:57
  15.3 2.8 %collective-permute-start.6 = (f32[64,512]{1,0:T(8,128)S(1)}, f32[64,512]{1,0:T(8,128)S(1)}, u32[]{:S(2)}, u32[]{:S(2)}) collective-permute-start(f32[64,512]{1,0:T(8,128)S(1)} %get-tuple-element.15), channel_id=1, source_target_pairs={{0,256},{64,320},{128,384},{192,448},{256,0},{320,64},{384,128},{4... | collective-permute-start | bytes 393224 | tf_op jit(solution)/shard_map/ppermute | solution.py:57
  18.0 2.1 %collective-permute-start.7 = (f32[64,512]{1,0:T(8,128)S(1)}, f32[64,512]{1,0:T(8,128)S(1)}, u32[]{:S(2)}, u32[]{:S(2)}) collective-permute-start(f32[64,512]{1,0:T(8,128)S(1)} %get-tuple-element.14), channel_id=1, source_target_pairs={{0,128},{64,192},{128,0},{192,64},{256,384},{320,448},{384,256},{4... | collective-permute-start | bytes 393224 | tf_op jit(solution)/shard_map/ppermute | solution.py:57
  20.1 1.1 %all-to-all-done = f32[8,64,512]{2,1,0:T(8,128)S(1)} async-done(((f32[8,64,512]{2,1,0:T(8,128)}), f32[8,64,512]{2,1,0:T(8,128)S(1)}, u32[]{:S(2)}, u32[]{:S(2)}) %all-to-all-start) | async-done | bytes 1048608 | tf_op jit(solution)/shard_map/all_to_all | solution.py:330
  21.2 0.1 reduce_min.9.band_ref
  21.3 2.8 %collective-permute-start.1 = (f32[16,640]{1,0:T(8,128)S(1)}, f32[16,640]{1,0:T(8,128)S(1)}, u32[]{:S(2)}, u32[]{:S(2)}) collective-permute-start(f32[16,640]{1,0:T(8,128)S(1)} %pad_maximum_fusion), channel_id=1, source_target_pairs={{64,128},{128,64},{192,256},{256,192},{320,384},{384,320},{448,8},... | collective-permute-start | bytes 122888 | tf_op jit(solution)/shard_map/ppermute | solution.py:74
  24.1 1.9 %collective-permute-start = (f32[16,512]{1,0:T(8,128)S(1)}, f32[16,512]{1,0:T(8,128)S(1)}, u32[]{:S(2)}, u32[]{:S(2)}) collective-permute-start(f32[16,512]{1,0:T(8,128)S(1)} %get-tuple-element.23), channel_id=1, source_target_pairs={{0,64},{64,0},{128,192},{192,128},{256,320},{320,256},{384,448},{4... | collective-permute-start | bytes 98312 | tf_op jit(solution)/shard_map/ppermute | solution.py:75
  26.1 0.1 fusion.10
  26.2 1.1 %collective-permute-done = f32[16,512]{1,0:T(8,128)S(1)} collective-permute-done((f32[16,512]{1,0:T(8,128)S(1)}, f32[16,512]{1,0:T(8,128)S(1)}, u32[]{:S(2)}, u32[]{:S(2)}) %collective-permute-start) | collective-permute-done | bytes 32800 | tf_op jit(solution)/shard_map/ppermute | solution.py:75
  27.2 3.6 %collective-permute-done.1 = f32[16,640]{1,0:T(8,128)S(1)} collective-permute-done((f32[16,640]{1,0:T(8,128)S(1)}, f32[16,640]{1,0:T(8,128)S(1)}, u32[]{:S(2)}, u32[]{:S(2)}) %collective-permute-start.1) | collective-permute-done | bytes 40992 | tf_op jit(solution)/shard_map/ppermute | solution.py:74
  30.9 0.1 broadcast_select_fusion
  31.0 5.1 %collective-permute-start.3 = (f32[32,128]{1,0:T(8,128)S(1)}, f32[32,128]{1,0:T(8,128)S(1)}, u32[]{:S(2)}, u32[]{:S(2)}) collective-permute-start(f32[32,128]{1,0:T(8,128)S(1)} %pad_maximum_fusion.1), channel_id=1, source_target_pairs={{1,2},{2,1},{3,4},{4,3},{5,6},{6,5},{9,10},{10,9},{11,12},{12,11},... | collective-permute-start | bytes 49160 | tf_op jit(solution)/shard_map/ppermute | solution.py:95
  36.1 0.0 copy-start
  36.1 2.1 %collective-permute-start.2 = (f32[24,128]{1,0:T(8,128)S(1)}, f32[24,128]{1,0:T(8,128)S(1)}, u32[]{:S(2)}, u32[]{:S(2)}) collective-permute-start(f32[24,128]{1,0:T(8,128)S(1)} %broadcast_select_fusion.1), channel_id=1, source_target_pairs={{0,1},{1,0},{2,3},{3,2},{4,5},{5,4},{6,7},{7,6},{8,9},{9,8},{10,11... | collective-permute-start | bytes 36872 | tf_op jit(solution)/shard_map/ppermute | solution.py:96
  38.2 0.0 collective-permute-done.5
  38.2 0.0 collective-permute-done.6
  38.2 0.0 collective-permute-done.7
  38.3 0.0 copy-done
  38.3 2.2 %shard_map.52 = (f32[64,512]{1,0:T(8,128)S(1)}, f32[64,512]{1,0:T(8,128)S(1)}) custom-call(f32[16,512]{1,0:T(8,128)S(1)} %get-tuple-element.25.above_ref, f32[64,512]{1,0:T(8,128)S(1)} %reduce_min.9.band_ref, f32[16,512]{1,0:T(8,128)S(1)} %get-tuple-element.24.below_ref, f32[64,512]{1,0:T(8,128)S(1)} %fusion.1.thick_ref, s32[64,512]{1,0:T(8,128)S(1)} %bitcast.17), custom_call_target="tpu_custom_call" | custom-call | tf_op jit(solution)/shard_map/pallas_call | solution.py:352
  40.5 1.3 %collective-permute-done.2 = f32[24,128]{1,0:T(8,128)S(1)} collective-permute-done((f32[24,128]{1,0:T(8,128)S(1)}, f32[24,128]{1,0:T(8,128)S(1)}, u32[]{:S(2)}, u32[]{:S(2)}) %collective-permute-start.2) | collective-permute-done | bytes 12320 | tf_op jit(solution)/shard_map/ppermute | solution.py:96
  41.9 0.0 collective-permute-done.3
  41.9 1.7 %shard_map.53 = (f32[64,512]{1,0:T(8,128)}, f32[64,512]{1,0:T(8,128)}) custom-call(f32[16,512]{1,0:T(8,128)S(1)} %get-tuple-element.25.above_ref, f32[64,512]{1,0:T(8,128)S(1)} %reduce_min.9.band_ref, f32[16,512]{1,0:T(8,128)S(1)} %get-tuple-element.24.below_ref, f32[24,128]{1,0:T(8,128)S(1)} %get-tuple-element.31.left_ref, ...), custom_call_target="tpu_custom_call" | custom-call | tf_op jit(solution)/shard_map/pallas_call | solution.py:361
  (12 shorter events, 0.1 us)
Async XLA Ops:
  0.6 20.6 %all-to-all-start = ((f32[8,64,512]{2,1,0:T(8,128)}), f32[8,64,512]{2,1,0:T(8,128)S(1)}, u32[]{:S(2)}, u32[]{:S(2)}) async-start(f32[8,64,512]{2,1,0:T(8,128)} %bitcast.21), calls=%async_computation | async-start | bytes 2097152 | tf_op jit(solution)/shard_map/all_to_all | solution.py:330
  6.2 3.9 %collective-permute-start.4 = (f32[4,64,512]{2,1,0:T(8,128)S(1)}, f32[4,64,512]{2,1,0:T(8,128)S(1)}, u32[]{:S(2)}, u32[]{:S(2)}) collective-permute-start(f32[4,64,512]{2,1,0:T(8,128)S(1)} %shard_map.51), channel_id=1, source_target_pairs={{0,64},{64,0},{128,192},{192,128},{256,320},{320,256},{384,448},{4... | collective-permute-start | bytes 1572872 | tf_op jit(solution)/shard_map/ppermute | solution.py:43
  10.2 28.0 %collective-permute-start.5 = (f32[64,512]{1,0:T(8,128)S(1)}, f32[64,512]{1,0:T(8,128)S(1)}, u32[]{:S(2)}, u32[]{:S(2)}) collective-permute-start(f32[64,512]{1,0:T(8,128)S(1)} %get-tuple-element.13), channel_id=1, source_target_pairs={{0,384},{64,448},{128,256},{192,320},{256,128},{320,192},{384,0},{... | collective-permute-start | bytes 393224 | tf_op jit(solution)/shard_map/ppermute | solution.py:57
  15.3 23.0 %collective-permute-start.6 = (f32[64,512]{1,0:T(8,128)S(1)}, f32[64,512]{1,0:T(8,128)S(1)}, u32[]{:S(2)}, u32[]{:S(2)}) collective-permute-start(f32[64,512]{1,0:T(8,128)S(1)} %get-tuple-element.15), channel_id=1, source_target_pairs={{0,256},{64,320},{128,384},{192,448},{256,0},{320,64},{384,128},{4... | collective-permute-start | bytes 393224 | tf_op jit(solution)/shard_map/ppermute | solution.py:57
  18.0 20.2 %collective-permute-start.7 = (f32[64,512]{1,0:T(8,128)S(1)}, f32[64,512]{1,0:T(8,128)S(1)}, u32[]{:S(2)}, u32[]{:S(2)}) collective-permute-start(f32[64,512]{1,0:T(8,128)S(1)} %get-tuple-element.14), channel_id=1, source_target_pairs={{0,128},{64,192},{128,0},{192,64},{256,384},{320,448},{384,256},{4... | collective-permute-start | bytes 393224 | tf_op jit(solution)/shard_map/ppermute | solution.py:57
  21.3 9.5 %collective-permute-start.1 = (f32[16,640]{1,0:T(8,128)S(1)}, f32[16,640]{1,0:T(8,128)S(1)}, u32[]{:S(2)}, u32[]{:S(2)}) collective-permute-start(f32[16,640]{1,0:T(8,128)S(1)} %pad_maximum_fusion), channel_id=1, source_target_pairs={{64,128},{128,64},{192,256},{256,192},{320,384},{384,320},{448,8},... | collective-permute-start | bytes 122888 | tf_op jit(solution)/shard_map/ppermute | solution.py:74
  24.1 3.1 %collective-permute-start = (f32[16,512]{1,0:T(8,128)S(1)}, f32[16,512]{1,0:T(8,128)S(1)}, u32[]{:S(2)}, u32[]{:S(2)}) collective-permute-start(f32[16,512]{1,0:T(8,128)S(1)} %get-tuple-element.23), channel_id=1, source_target_pairs={{0,64},{64,0},{128,192},{192,128},{256,320},{320,256},{384,448},{4... | collective-permute-start | bytes 98312 | tf_op jit(solution)/shard_map/ppermute | solution.py:75
  31.0 10.9 %collective-permute-start.3 = (f32[32,128]{1,0:T(8,128)S(1)}, f32[32,128]{1,0:T(8,128)S(1)}, u32[]{:S(2)}, u32[]{:S(2)}) collective-permute-start(f32[32,128]{1,0:T(8,128)S(1)} %pad_maximum_fusion.1), channel_id=1, source_target_pairs={{1,2},{2,1},{3,4},{4,3},{5,6},{6,5},{9,10},{10,9},{11,12},{12,11},... | collective-permute-start | bytes 49160 | tf_op jit(solution)/shard_map/ppermute | solution.py:95
  36.1 2.2 %copy-start = (s32[1,64,512]{2,1,0:T(8,128)S(1)}, s32[1,64,512]{2,1,0:T(8,128)}, u32[]{:S(2)}) copy-start(s32[1,64,512]{2,1,0:T(8,128)} %param.5) | copy-start | bytes 393220
  36.1 5.7 %collective-permute-start.2 = (f32[24,128]{1,0:T(8,128)S(1)}, f32[24,128]{1,0:T(8,128)S(1)}, u32[]{:S(2)}, u32[]{:S(2)}) collective-permute-start(f32[24,128]{1,0:T(8,128)S(1)} %broadcast_select_fusion.1), channel_id=1, source_target_pairs={{0,1},{1,0},{2,3},{3,2},{4,5},{5,4},{6,7},{7,6},{8,9},{9,8},{10,11... | collective-permute-start | bytes 36872 | tf_op jit(solution)/shard_map/ppermute | solution.py:96
